TPU v7x, 32 devices: a whole 2x2x4 slice. The times are simulated.
32 devices in a mesh: dp: 16 (over z, y, x), band: 2 (over core).
Axes of the slice: x: 2, y: 2, z: 4, core: 2. Of those that a mesh axis runs over, the one named last changes fastest.
Arguments:
- pixels: bfloat16 [32, 254, 896], P('dp', None, 'band'), may hold values from -6 to 6
- time_loc: float32 [32, 8], P(('dp', 'band')), may hold values from -1 to 1
- band_mask: int32 [32, 14], P('dp', 'band'), may hold values from 0 to 1, as said below
- wavelengths: int32 [32, 14], P('dp', 'band'), may hold values from 0 to 15
- visible: int32 [32, 254], P(('dp', 'band')), may hold values from 0 to 1023, as said below
- band_table: bfloat16 [768, 16, 64], P('dp'), may hold values from -1.5 to 1.5
- cls_token: bfloat16 [768], P('dp'), may hold values from -4 to 4
- loc_weight: bfloat16 [768, 8], P('dp'), may hold values from -2 to 2
- enc_attn_gain: bfloat16 [768], P('dp'), may hold values from 0.5 to 1.5
- enc_attn_shift: bfloat16 [768], P('dp'), may hold values from -1 to 1
- enc_qkv: bfloat16 [768, 2304], P('dp'), may hold values from -0.21875 to 0.21875
- enc_out: bfloat16 [768, 768], P('dp'), may hold values from -0.875 to 0.875
- enc_mlp_gain: bfloat16 [768], P('dp'), may hold values from 0.5 to 1.5
- enc_mlp_shift: bfloat16 [768], P('dp'), may hold values from -1 to 1
- enc_up: bfloat16 [768, 3072], P('dp'), may hold values from -0.21875 to 0.21875
- enc_down: bfloat16 [3072, 768], P('dp'), may hold values from -0.109375 to 0.109375
- projection: bfloat16 [768, 512], P('dp'), may hold values from -0.21875 to 0.21875
- mask_token: bfloat16 [512], P('dp'), may hold values from -4 to 4
- dec_attn_gain: bfloat16 [512], P('dp'), may hold values from 0.5 to 1.5
- dec_attn_shift: bfloat16 [512], P('dp'), may hold values from -1 to 1
- dec_qkv: bfloat16 [512, 1536], P('dp'), may hold values from -0.25 to 0.25
- dec_out: bfloat16 [512, 512], P('dp'), may hold values from -1.5 to 1.5
- dec_mlp_gain: bfloat16 [512], P('dp'), may hold values from 0.5 to 1.5
- dec_mlp_shift: bfloat16 [512], P('dp'), may hold values from -1 to 1
- dec_up: bfloat16 [512, 2048], P('dp'), may hold values from -0.25 to 0.25
- dec_down: bfloat16 [2048, 512], P('dp'), may hold values from -0.125 to 0.125
- cotangent: bfloat16 [32, 1024, 512], P(('dp', 'band')), may hold values from -6 to 6
Outputs:
- decoded: bfloat16 [32, 1024, 512], P(('dp', 'band'))
- grad_pixels: float32 [32, 254, 896], P('dp', None, 'band')
- grad_time_loc: float32 [32, 8], P(('dp', 'band'))
- grad_band_table: float32 [768, 16, 64], P('dp')
- grad_cls_token: float32 [768], P('dp')
- grad_loc_weight: float32 [768, 8], P('dp')
- grad_enc_attn_gain: float32 [768], P('dp')
- grad_enc_attn_shift: float32 [768], P('dp')
- grad_enc_qkv: float32 [768, 2304], P('dp')
- grad_enc_out: float32 [768, 768], P('dp')
- grad_enc_mlp_gain: float32 [768], P('dp')
- grad_enc_mlp_shift: float32 [768], P('dp')
- grad_enc_up: float32 [768, 3072], P('dp')
- grad_enc_down: float32 [3072, 768], P('dp')
- grad_projection: float32 [768, 512], P('dp')
- grad_mask_token: float32 [512], P('dp')
- grad_dec_attn_gain: float32 [512], P('dp')
- grad_dec_attn_shift: float32 [512], P('dp')
- grad_dec_qkv: float32 [512, 1536], P('dp')
- grad_dec_out: float32 [512, 512], P('dp')
- grad_dec_mlp_gain: float32 [512], P('dp')
- grad_dec_mlp_shift: float32 [512], P('dp')
- grad_dec_up: float32 [512, 2048], P('dp')
- grad_dec_down: float32 [2048, 512], P('dp')
Inputs may be any that keep to these rules, and one draw needn't show every extreme that they name: `band_mask`: band slot 0 of every chip holds a real band. `visible`: the 254 indices of a chip are distinct.
All inputs are finite; a program needn't handle non-finite values.
Results may differ from a plain program's by a relative error of at most 0.03.
Values may be sent and summed in bfloat16 or wider, within the bound.
No kernel may reach another device: no remote copies, remote signals or barrier semaphores. Data moves between devices by JAX's collectives and lax.ppermute only.
A program may use at most 320 MiB of HBM per device.

v0:
```python
import math

import jax
import jax.numpy as jnp
from jax import lax
from jax.sharding import PartitionSpec as P

HEADS_ENC = 12
HEADS_DEC = 16


EPSILON = 1e-05


def gelu_tanh(upper):
    return jax.nn.gelu(upper, approximate=True)


def sincos(place_index, model_width):
    half_width = model_width // 2
    frequency = jnp.exp(-math.log(10000.0) * jnp.arange(half_width, dtype=jnp.float32) / half_width)
    angles = place_index[..., None] * frequency
    return jnp.concatenate([jnp.sin(angles), jnp.cos(angles)], -1)


def project(acts_in, weight_in):
    return jnp.einsum("cld,df->clf", acts_in, weight_in, preferred_element_type=jnp.float32)


def project_back(grads_in, weight_in):
    return jnp.einsum("clf,df->cld", grads_in, weight_in, preferred_element_type=jnp.float32)


def weight_grad(acts_in, grads_in):
    return jnp.einsum("cld,clf->df", acts_in, grads_in, preferred_element_type=jnp.float32)


def norm_forward(rows_in, gain_row, shift_row):
    centred = rows_in - jnp.mean(rows_in, -1, keepdims=True)
    inverse = lax.rsqrt(jnp.mean(centred * centred, -1, keepdims=True) + EPSILON)
    unit_rows = centred * inverse
    return (unit_rows * gain_row + shift_row, unit_rows, inverse)


def norm_backward(grad_normed, unit_rows, inverse, gain_row):
    grad_unit = grad_normed * gain_row
    grad_input = inverse * (
        grad_unit
        - jnp.mean(grad_unit, -1, keepdims=True)
        - unit_rows * jnp.mean(grad_unit * unit_rows, -1, keepdims=True)
    )
    return (grad_input, jnp.sum(grad_normed * unit_rows, (0, 1)), jnp.sum(grad_normed, (0, 1)))


def attend_forward(queries, key_rows, value_rows, score_scale):
    chip_count, length, head_count, head_size = queries.shape
    block_rows = min(length, 512)
    block_count = length // block_rows

    def one_block(start):
        query_block = lax.dynamic_slice_in_dim(queries, start, block_rows, 1)
        scores = (
            jnp.einsum("cqhe,ckhe->chqk", query_block, key_rows, preferred_element_type=jnp.float32)
            * score_scale
        )
        top_score = jnp.max(scores, -1, keepdims=True)
        weights = jnp.exp(scores - top_score)
        totals = jnp.sum(weights, -1, keepdims=True)
        probability = (weights / totals).astype(jnp.bfloat16)
        mixed_out = jnp.einsum(
            "chqk,ckhe->cqhe", probability, value_rows, preferred_element_type=jnp.float32
        )
        return (mixed_out.astype(jnp.bfloat16), (top_score + jnp.log(totals))[..., 0])

    starts = jnp.arange(block_count, dtype=jnp.int32) * block_rows
    outputs, log_sums = lax.map(one_block, starts)
    outputs = jnp.moveaxis(outputs, 0, 1).reshape(chip_count, length, head_count, head_size)
    log_sums = jnp.transpose(log_sums, (1, 2, 0, 3)).reshape(chip_count, head_count, length)
    return (outputs, log_sums)


def attend_backward(queries, key_rows, value_rows, log_sums, grad_out, score_scale):
    chip_count, length, head_count, head_size = queries.shape
    block_rows = min(length, 512)
    block_count = length // block_rows

    def one_block(start):
        query_block = lax.dynamic_slice_in_dim(queries, start, block_rows, 1)
        grad_block = lax.dynamic_slice_in_dim(grad_out, start, block_rows, 1)
        sums_block = lax.dynamic_slice_in_dim(log_sums, start, block_rows, 2)
        scores = (
            jnp.einsum("cqhe,ckhe->chqk", query_block, key_rows, preferred_element_type=jnp.float32)
            * score_scale
        )
        probability = jnp.exp(scores - sums_block[..., None])
        grad_probs = jnp.einsum(
            "cqhe,ckhe->chqk", grad_block, value_rows, preferred_element_type=jnp.float32
        )
        grad_scores = (
            probability * (grad_probs - jnp.sum(grad_probs * probability, -1, keepdims=True))
        ).astype(jnp.bfloat16)
        grad_query = (
            jnp.einsum("chqk,ckhe->cqhe", grad_scores, key_rows, preferred_element_type=jnp.float32)
            * score_scale
        )
        grad_key = (
            jnp.einsum(
                "chqk,cqhe->ckhe", grad_scores, query_block, preferred_element_type=jnp.float32
            )
            * score_scale
        )
        grad_value = jnp.einsum(
            "chqk,cqhe->ckhe",
            probability.astype(jnp.bfloat16),
            grad_block,
            preferred_element_type=jnp.float32,
        )
        return (grad_query, grad_key, grad_value)

    starts = jnp.arange(block_count, dtype=jnp.int32) * block_rows
    grad_queries, grad_keys, grad_values = lax.map(one_block, starts)
    grad_queries = jnp.moveaxis(grad_queries, 0, 1).reshape(
        chip_count, length, head_count, head_size
    )
    return (grad_queries, jnp.sum(grad_keys, 0), jnp.sum(grad_values, 0))


def block_forward(rows_in, weights, head_count):
    gain_one, shift_one, w_qkv, w_out, gain_two, shift_two, w_up, w_down = weights
    chip_count, length, model_width = rows_in.shape
    head_size = model_width // head_count
    normed, unit_one, inverse_one = norm_forward(
        rows_in, gain_one.astype(jnp.float32), shift_one.astype(jnp.float32)
    )
    normed_one = normed.astype(jnp.bfloat16)
    mixed_rows = project(normed_one, w_qkv).astype(jnp.bfloat16)
    queries = mixed_rows[..., :model_width].reshape(chip_count, length, head_count, head_size)
    key_rows = mixed_rows[..., model_width : 2 * model_width].reshape(
        chip_count, length, head_count, head_size
    )
    value_rows = mixed_rows[..., 2 * model_width :].reshape(
        chip_count, length, head_count, head_size
    )
    attn_heads, log_sums = attend_forward(queries, key_rows, value_rows, head_size ** (-0.5))
    attn_rows = attn_heads.reshape(chip_count, length, model_width)
    middle = rows_in + project(attn_rows, w_out)
    normed, unit_two, inverse_two = norm_forward(
        middle, gain_two.astype(jnp.float32), shift_two.astype(jnp.float32)
    )
    normed_two = normed.astype(jnp.bfloat16)
    upper = project(normed_two, w_up)
    active = gelu_tanh(upper).astype(jnp.bfloat16)
    rows_out = middle + project(active, w_down)
    saved = (
        unit_one,
        inverse_one,
        normed_one,
        queries,
        key_rows,
        value_rows,
        log_sums,
        attn_rows,
        unit_two,
        inverse_two,
        normed_two,
        upper,
        active,
    )
    return (rows_out, saved)


def block_backward(grad_out, weights, saved, head_count):
    gain_one, shift_one, w_qkv, w_out, gain_two, shift_two, w_up, w_down = weights
    (
        unit_one,
        inverse_one,
        normed_one,
        queries,
        key_rows,
        value_rows,
        log_sums,
        attn_rows,
        unit_two,
        inverse_two,
        normed_two,
        upper,
        active,
    ) = saved
    chip_count, length, model_width = grad_out.shape
    head_size = model_width // head_count
    grad_branch = grad_out.astype(jnp.bfloat16)
    grad_down = weight_grad(active, grad_branch)
    grad_active = project_back(grad_branch, w_down)
    gelu_pull = jax.vjp(gelu_tanh, upper)[1]
    grad_upper = gelu_pull(grad_active)[0].astype(jnp.bfloat16)
    grad_up = weight_grad(normed_two, grad_upper)
    grad_normed = project_back(grad_upper, w_up)
    grad_middle, grad_gain_two, grad_shift_two = norm_backward(
        grad_normed, unit_two, inverse_two, gain_two.astype(jnp.float32)
    )
    grad_middle = grad_out + grad_middle
    grad_attn_branch = grad_middle.astype(jnp.bfloat16)
    grad_wout = weight_grad(attn_rows, grad_attn_branch)
    grad_attn = project_back(grad_attn_branch, w_out).astype(jnp.bfloat16)
    grad_attn = grad_attn.reshape(chip_count, length, head_count, head_size)
    grad_query, grad_key, grad_value = attend_backward(
        queries, key_rows, value_rows, log_sums, grad_attn, head_size ** (-0.5)
    )
    grad_mixed = jnp.concatenate(
        [
            grad_query.reshape(chip_count, length, model_width),
            grad_key.reshape(chip_count, length, model_width),
            grad_value.reshape(chip_count, length, model_width),
        ],
        -1,
    ).astype(jnp.bfloat16)
    grad_qkv = weight_grad(normed_one, grad_mixed)
    grad_normed_one = project_back(grad_mixed, w_qkv)
    grad_input, grad_gain_one, grad_shift_one = norm_backward(
        grad_normed_one, unit_one, inverse_one, gain_one.astype(jnp.float32)
    )
    return (
        grad_middle + grad_input,
        (
            grad_gain_one,
            grad_shift_one,
            grad_qkv,
            grad_wout,
            grad_gain_two,
            grad_shift_two,
            grad_up,
            grad_down,
        ),
    )


def per_device(
    pixels,
    time_loc,
    band_mask,
    wavelengths,
    visible,
    band_table,
    cls_token,
    loc_weight,
    enc_attn_gain,
    enc_attn_shift,
    enc_qkv,
    enc_out,
    enc_mlp_gain,
    enc_mlp_shift,
    enc_up,
    enc_down,
    projection,
    mask_token,
    dec_attn_gain,
    dec_attn_shift,
    dec_qkv,
    dec_out,
    dec_mlp_gain,
    dec_mlp_shift,
    dec_up,
    dec_down,
    cotangent,
):
    enc_full = (
        lax.all_gather(band_table, "dp", axis=0, tiled=True),
        lax.all_gather(cls_token, "dp", axis=0, tiled=True),
        lax.all_gather(loc_weight, "dp", axis=0, tiled=True),
        lax.all_gather(enc_attn_gain, "dp", axis=0, tiled=True),
        lax.all_gather(enc_attn_shift, "dp", axis=0, tiled=True),
        lax.all_gather(enc_qkv, "dp", axis=0, tiled=True),
        lax.all_gather(enc_out, "dp", axis=0, tiled=True),
        lax.all_gather(enc_mlp_gain, "dp", axis=0, tiled=True),
        lax.all_gather(enc_mlp_shift, "dp", axis=0, tiled=True),
        lax.all_gather(enc_up, "dp", axis=0, tiled=True),
        lax.all_gather(enc_down, "dp", axis=0, tiled=True),
    )
    dec_full = (
        lax.all_gather(projection, "dp", axis=0, tiled=True),
        lax.all_gather(mask_token, "dp", axis=0, tiled=True),
        lax.all_gather(dec_attn_gain, "dp", axis=0, tiled=True),
        lax.all_gather(dec_attn_shift, "dp", axis=0, tiled=True),
        lax.all_gather(dec_qkv, "dp", axis=0, tiled=True),
        lax.all_gather(dec_out, "dp", axis=0, tiled=True),
        lax.all_gather(dec_mlp_gain, "dp", axis=0, tiled=True),
        lax.all_gather(dec_mlp_shift, "dp", axis=0, tiled=True),
        lax.all_gather(dec_up, "dp", axis=0, tiled=True),
        lax.all_gather(dec_down, "dp", axis=0, tiled=True),
    )
    table_full = enc_full[0]
    model_width = table_full.shape[0]
    pair_chips, visible_count, slot_width = pixels.shape
    chip_count = visible.shape[0]
    live_slots = band_mask.reshape(-1).astype(jnp.bfloat16)
    chosen = jnp.take(table_full, wavelengths.reshape(-1), axis=1) * live_slots[None, :, None]
    chosen = chosen.reshape(model_width, pair_chips, slot_width)
    partial_value = jnp.einsum("cvk,dck->cvd", pixels, chosen, preferred_element_type=jnp.float32)
    live_counts = jnp.sum(band_mask, 1).astype(jnp.float32)
    raw_sum, band_count = (
        lax.psum_scatter(
            partial_value.astype(jnp.bfloat16), "band", scatter_dimension=0, tiled=True
        ).astype(jnp.float32),
        lax.psum_scatter(
            live_counts.astype(jnp.bfloat16), "band", scatter_dimension=0, tiled=True
        ).astype(jnp.float32),
    )
    patch_rows = raw_sum / band_count[:, None, None] + sincos(
        visible.astype(jnp.float32), model_width
    )
    loc_float = enc_full[2].astype(jnp.float32)
    loc_token = jnp.dot(time_loc, loc_float.T, precision=lax.Precision.HIGHEST)
    cls_rows = jnp.broadcast_to(enc_full[1].astype(jnp.float32), (chip_count, model_width))
    tokens = jnp.concatenate([cls_rows[:, None, :], loc_token[:, None, :], patch_rows], 1)
    encoded, enc_saved = block_forward(tokens, enc_full[3:], HEADS_ENC)
    latent_in = encoded[:, 2:, :].astype(jnp.bfloat16)
    latent = project(latent_in, dec_full[0]).astype(jnp.bfloat16)
    dec_width = latent.shape[2]
    positions = jnp.arange(cotangent.shape[1], dtype=jnp.int32)
    matches = positions[None, :, None] == visible[:, None, :]
    seen_count = jnp.sum(matches.astype(jnp.float32), 2, keepdims=True)
    inserted = jnp.einsum(
        "cpv,cvd->cpd", matches.astype(jnp.bfloat16), latent, preferred_element_type=jnp.float32
    )
    inserted = (
        inserted
        + (1.0 - seen_count) * dec_full[1].astype(jnp.float32)
        + sincos(positions.astype(jnp.float32), dec_width)
    )
    decoded, dec_saved = block_forward(inserted, dec_full[2:], HEADS_DEC)
    grad_inserted, dec_grads = block_backward(
        cotangent.astype(jnp.float32), dec_full[2:], dec_saved, HEADS_DEC
    )
    grad_mask = jnp.sum(grad_inserted * (1.0 - seen_count), (0, 1))
    grad_latent = jax.vmap(lambda rows_all, picks_row: jnp.take(rows_all, picks_row, axis=0))(
        grad_inserted, visible
    )
    grad_latent = grad_latent.astype(jnp.bfloat16)
    grad_proj = weight_grad(latent_in, grad_latent)
    grad_rows = project_back(grad_latent, dec_full[0])
    dec_joint = (
        lax.psum_scatter(grad_proj, ("dp", "band"), scatter_dimension=0, tiled=True),
        lax.psum_scatter(grad_mask, ("dp", "band"), scatter_dimension=0, tiled=True),
        lax.psum_scatter(dec_grads[0], ("dp", "band"), scatter_dimension=0, tiled=True),
        lax.psum_scatter(dec_grads[1], ("dp", "band"), scatter_dimension=0, tiled=True),
        lax.psum_scatter(dec_grads[2], ("dp", "band"), scatter_dimension=0, tiled=True),
        lax.psum_scatter(dec_grads[3], ("dp", "band"), scatter_dimension=0, tiled=True),
        lax.psum_scatter(dec_grads[4], ("dp", "band"), scatter_dimension=0, tiled=True),
        lax.psum_scatter(dec_grads[5], ("dp", "band"), scatter_dimension=0, tiled=True),
        lax.psum_scatter(dec_grads[6], ("dp", "band"), scatter_dimension=0, tiled=True),
        lax.psum_scatter(dec_grads[7], ("dp", "band"), scatter_dimension=0, tiled=True),
    )
    dec_sums = (
        lax.all_gather(dec_joint[0].astype(jnp.bfloat16), "band", axis=0, tiled=True).astype(
            jnp.float32
        ),
        lax.all_gather(dec_joint[1].astype(jnp.bfloat16), "band", axis=0, tiled=True).astype(
            jnp.float32
        ),
        lax.all_gather(dec_joint[2].astype(jnp.bfloat16), "band", axis=0, tiled=True).astype(
            jnp.float32
        ),
        lax.all_gather(dec_joint[3].astype(jnp.bfloat16), "band", axis=0, tiled=True).astype(
            jnp.float32
        ),
        lax.all_gather(dec_joint[4].astype(jnp.bfloat16), "band", axis=0, tiled=True).astype(
            jnp.float32
        ),
        lax.all_gather(dec_joint[5].astype(jnp.bfloat16), "band", axis=0, tiled=True).astype(
            jnp.float32
        ),
        lax.all_gather(dec_joint[6].astype(jnp.bfloat16), "band", axis=0, tiled=True).astype(
            jnp.float32
        ),
        lax.all_gather(dec_joint[7].astype(jnp.bfloat16), "band", axis=0, tiled=True).astype(
            jnp.float32
        ),
        lax.all_gather(dec_joint[8].astype(jnp.bfloat16), "band", axis=0, tiled=True).astype(
            jnp.float32
        ),
        lax.all_gather(dec_joint[9].astype(jnp.bfloat16), "band", axis=0, tiled=True).astype(
            jnp.float32
        ),
    )
    grad_encoded = jnp.concatenate(
        [jnp.zeros((chip_count, 2, model_width), jnp.float32), grad_rows], 1
    )
    grad_tokens, enc_grads = block_backward(grad_encoded, enc_full[3:], enc_saved, HEADS_ENC)
    grad_cls = jnp.sum(grad_tokens[:, 0], 0)
    grad_loc_rows = grad_tokens[:, 1]
    grad_loc = jnp.dot(grad_loc_rows.T, time_loc, precision=lax.Precision.HIGHEST)
    grad_time = jnp.dot(grad_loc_rows, loc_float, precision=lax.Precision.HIGHEST)
    grad_raw = (grad_tokens[:, 2:] / band_count[:, None, None]).astype(jnp.bfloat16)
    grad_pair = lax.all_gather(grad_raw, "band", axis=0, tiled=True)
    grad_pixels = jnp.einsum("cvd,dck->cvk", grad_pair, chosen, preferred_element_type=jnp.float32)
    per_slot = jnp.einsum("cvk,cvd->dck", pixels, grad_pair, preferred_element_type=jnp.float32)
    wave_count, pixel_size = (table_full.shape[1], table_full.shape[2])
    per_slot = per_slot.reshape(model_width, -1, pixel_size)
    select = (
        wavelengths.reshape(-1)[:, None] == jnp.arange(wave_count, dtype=jnp.int32)[None, :]
    ).astype(jnp.float32)
    select = select * band_mask.reshape(-1)[:, None].astype(jnp.float32)
    grad_table = jnp.einsum("dsp,sw->dwp", per_slot, select, precision=lax.Precision.HIGHEST)
    enc_joint = (
        lax.psum_scatter(grad_table, ("dp", "band"), scatter_dimension=0, tiled=True),
        lax.psum_scatter(grad_cls, ("dp", "band"), scatter_dimension=0, tiled=True),
        lax.psum_scatter(grad_loc, ("dp", "band"), scatter_dimension=0, tiled=True),
        lax.psum_scatter(enc_grads[0], ("dp", "band"), scatter_dimension=0, tiled=True),
        lax.psum_scatter(enc_grads[1], ("dp", "band"), scatter_dimension=0, tiled=True),
        lax.psum_scatter(enc_grads[2], ("dp", "band"), scatter_dimension=0, tiled=True),
        lax.psum_scatter(enc_grads[3], ("dp", "band"), scatter_dimension=0, tiled=True),
        lax.psum_scatter(enc_grads[4], ("dp", "band"), scatter_dimension=0, tiled=True),
        lax.psum_scatter(enc_grads[5], ("dp", "band"), scatter_dimension=0, tiled=True),
        lax.psum_scatter(enc_grads[6], ("dp", "band"), scatter_dimension=0, tiled=True),
        lax.psum_scatter(enc_grads[7], ("dp", "band"), scatter_dimension=0, tiled=True),
    )
    enc_sums = (
        lax.all_gather(enc_joint[0].astype(jnp.bfloat16), "band", axis=0, tiled=True).astype(
            jnp.float32
        ),
        lax.all_gather(enc_joint[1].astype(jnp.bfloat16), "band", axis=0, tiled=True).astype(
            jnp.float32
        ),
        lax.all_gather(enc_joint[2].astype(jnp.bfloat16), "band", axis=0, tiled=True).astype(
            jnp.float32
        ),
        lax.all_gather(enc_joint[3].astype(jnp.bfloat16), "band", axis=0, tiled=True).astype(
            jnp.float32
        ),
        lax.all_gather(enc_joint[4].astype(jnp.bfloat16), "band", axis=0, tiled=True).astype(
            jnp.float32
        ),
        lax.all_gather(enc_joint[5].astype(jnp.bfloat16), "band", axis=0, tiled=True).astype(
            jnp.float32
        ),
        lax.all_gather(enc_joint[6].astype(jnp.bfloat16), "band", axis=0, tiled=True).astype(
            jnp.float32
        ),
        lax.all_gather(enc_joint[7].astype(jnp.bfloat16), "band", axis=0, tiled=True).astype(
            jnp.float32
        ),
        lax.all_gather(enc_joint[8].astype(jnp.bfloat16), "band", axis=0, tiled=True).astype(
            jnp.float32
        ),
        lax.all_gather(enc_joint[9].astype(jnp.bfloat16), "band", axis=0, tiled=True).astype(
            jnp.float32
        ),
        lax.all_gather(enc_joint[10].astype(jnp.bfloat16), "band", axis=0, tiled=True).astype(
            jnp.float32
        ),
    )
    return (
        decoded.astype(jnp.bfloat16),
        grad_pixels,
        grad_time,
        enc_sums[0],
        enc_sums[1],
        enc_sums[2],
        enc_sums[3],
        enc_sums[4],
        enc_sums[5],
        enc_sums[6],
        enc_sums[7],
        enc_sums[8],
        enc_sums[9],
        enc_sums[10],
        dec_sums[0],
        dec_sums[1],
        dec_sums[2],
        dec_sums[3],
        dec_sums[4],
        dec_sums[5],
        dec_sums[6],
        dec_sums[7],
        dec_sums[8],
        dec_sums[9],
    )


def solution(mesh):
    in_specs = (
        P("dp", None, "band"),
        P(("dp", "band"), None),
        P("dp", "band"),
        P("dp", "band"),
        P(("dp", "band"), None),
        P("dp", None, None),
        P("dp"),
        P("dp", None),
        P("dp"),
        P("dp"),
        P("dp", None),
        P("dp", None),
        P("dp"),
        P("dp"),
        P("dp", None),
        P("dp", None),
        P("dp", None),
        P("dp"),
        P("dp"),
        P("dp"),
        P("dp", None),
        P("dp", None),
        P("dp"),
        P("dp"),
        P("dp", None),
        P("dp", None),
        P(("dp", "band"), None, None),
    )
    out_specs = (
        P(("dp", "band"), None, None),
        P("dp", None, "band"),
        P(("dp", "band"), None),
        P("dp", None, None),
        P("dp"),
        P("dp", None),
        P("dp"),
        P("dp"),
        P("dp", None),
        P("dp", None),
        P("dp"),
        P("dp"),
        P("dp", None),
        P("dp", None),
        P("dp", None),
        P("dp"),
        P("dp"),
        P("dp"),
        P("dp", None),
        P("dp", None),
        P("dp"),
        P("dp"),
        P("dp", None),
        P("dp", None),
    )
    return jax.shard_map(
        per_device, mesh=mesh, in_specs=in_specs, out_specs=out_specs, check_vma=False
    )
```

profile of v0, /device:TPU:1, one launch (start us, length us, event | category | flops | bytes accessed | tf_op | source)
XLA Modules:
  0.0 1958.8 jit_solution(6175773187536282408)
XLA Ops:
  11.3 68.7 %all-gather.11.cloned.1.call-done = bf16[768,16,64]{2,1,0:T(8,128)(2,1)} async-done(((bf16[48,16,64]{2,1,0:T(8,128)(2,1)}), bf16[768,16,64]{2,1,0:T(8,128)(2,1)}) %all-gather.11.cloned.1.call-update) | async-done | bytes 1572880 | tf_op jit(solution)/shard_map/all_gather | solution.py:267
  92.1 32.2 %all-gather = bf16[16,48,8]{1,2,0:T(8,128)(2,1)S(1)} all-gather(bf16[1,48,8]{1,2,0:T(8,128)(2,1)S(1)} %bitcast.347), channel_id=1, replica_groups=mesh['dp'=16,'band'=2] {'dp'}, dimensions={0}, use_global_device_ids=true | all-gather | bytes 13056 | tf_op jit(solution)/shard_map/all_gather | solution.py:269
  129.3 58.6 %all-reduce.34 = (bf16[768]{0:T(1024)(128)(2,1)S(1)}, bf16[512]{0:T(512)(128)(2,1)S(1)}, bf16[768]{0:T(1024)(128)(2,1)S(1)}, bf16[768]{0:T(1024)(128)(2,1)S(1)},...) all-reduce(bf16[768]{0:T(1024)(128)(2,1)S(1)} %dynamic-update-slice, ...), channel_id=1, replica_groups=mesh['dp'=16,'band'=2] {'dp'}, use_global_device_ids=true, to_apply=%add.1 | all-reduce | flops 6400 | bytes 25600
  189.5 24.2 %all-reduce.21 = bf16[2]{0:T(256)(128)(2,1)S(1)} all-reduce(bf16[2]{0:T(256)(128)(2,1)S(1)} %convert_convert_fusion), channel_id=3, replica_groups=mesh['dp'=16,'band'=2] {'band'}, use_global_device_ids=true, to_apply=%region_2.3.clone | all-reduce | flops 2 | bytes 8
  218.2 35.1 %all_gather.145 = bf16[512,512]{1,0:T(8,128)(2,1)} all-gather(bf16[32,512]{1,0:T(8,128)(2,1)S(1)} %copy-done.90), channel_id=1, replica_groups=mesh['dp'=16,'band'=2] {'dp'}, dimensions={0}, use_global_device_ids=true | all-gather | bytes 557056 | tf_op jit(solution)/shard_map/all_gather | solution.py:285
  253.2 41.4 %all_gather.140 = bf16[768,512]{1,0:T(8,128)(2,1)} all-gather(bf16[48,512]{1,0:T(8,128)(2,1)S(1)} %copy-done.81), channel_id=1, replica_groups=mesh['dp'=16,'band'=2] {'dp'}, dimensions={0}, use_global_device_ids=true | all-gather | bytes 835584 | tf_op jit(solution)/shard_map/all_gather | solution.py:280
  325.3 77.3 %all-gather.19.cloned.1.call-done = bf16[3072,768]{1,0:T(8,128)(2,1)} async-done(((bf16[192,768]{1,0:T(8,128)(2,1)}), bf16[3072,768]{1,0:T(8,128)(2,1)}) %all-gather.19.cloned.1.call-update) | async-done | bytes 4718608 | tf_op jit(solution)/shard_map/all_gather | solution.py:277
  412.2 49.9 %all-gather.21.cloned.1.call-done = bf16[512,1536]{1,0:T(8,128)(2,1)} async-done(((bf16[32,1536]{1,0:T(8,128)(2,1)}), bf16[512,1536]{1,0:T(8,128)(2,1)}) %all-gather.21.cloned.1.call-update) | async-done | bytes 1572880 | tf_op jit(solution)/shard_map/all_gather | solution.py:284
  473.0 88.8 %while.4 = (s32[]{:T(128)}, bf16[2,1,512,16,32]{2,4,3,1,0:T(8,128)(2,1)}, f32[2,1,16,512]{3,2,1,0:T(8,128)S(1)}, s32[2]{0:T(128)S(1)}, bf16[1,1024,16,32]{1,3,2,...) while((s32[]{:T(128)}, ...), condition=%wide.region_15.16_spmd, body=%wide.region_12.15_spmd.sunk | while | flops 1149493248 | bytes 116654328 | solution.py:76
  475.6 13.3 multiply_reduce_fusion.23
  488.9 14.5 fusion.217
  503.4 13.1 fusion.218
  520.0 13.3 multiply_reduce_fusion.23
  533.3 14.5 fusion.217
  547.8 13.0 fusion.218
  575.2 12.8 all-gather.25.cloned.1.call-done
  617.1 193.5 %while.5 = (s32[]{:T(128)}, bf16[2,1,512,16,32]{2,4,3,1,0:T(8,128)(2,1)}, f32[2,1,1024,16,32]{2,4,3,1,0:T(8,128)}, f32[2,1,1024,16,32]{2,4,3,1,0:T(8,128)}, s32[...) while((s32[]{:T(128)}, ...), condition=%wide.region_22.23_spmd, body=%wide.region_20.22_spmd.sunk | while | flops 2785796096 | bytes 371425600 | solution.py:121
  620.0 13.3 fusion.227
  646.0 24.7 %multiply_reduce_fusion.24 = (f32[16,512]{1,0:T(8,128)S(1)}, f32[16,512,1024]{2,1,0:T(8,128)}) fusion(f32[16,512,1024]{2,1,0:T(8,128)} %fusion.227, f32[16,512]{1,0:T(8,128)S(1)} %dynamic-slice_bitcast_fusion.2, bf16[1,1024,16,32]{1,3,2,0:T(8,128)(2,1)S(1)} %copy-done.5, bf16[1,1024,16,32]{1,3,2,0:T(8,128)(2,1)S(1)} %copy-done.8, s32[]{:T(128)S(6)} %select_n.95), kind=kOutput, calls=%fused_computation.19.clone.1 | convolution fusion | flops 570417152 | bytes 68747264 | tf_op jit(solution)/shard_map/while/body/eval_jaxpr/cqhe,ckhe->chqk/dot_general | solution.py:96
  670.6 28.0 %multiply_convert_fusion.9 = bf16[16,512,1024]{2,1,0:T(8,128)(2,1)} fusion(f32[16,512,1024]{2,1,0:T(8,128)} %get-tuple-element.537, f32[16,512,1024]{2,1,0:T(8,128)} %fusion.227, f32[16,512]{1,0:T(8,128)S(1)} %get-tuple-element.538, f32[16,512]{1,0:T(8,128)S(1)} %dynamic-slice_bitcast_fusion.2), kind=kLoop, calls=%fused_computation.18.clone.1 | loop fusion | flops 41943040 | bytes 83951616 | tf_op jit(solution)/shard_map/while/body/eval_jaxpr/convert_element_type | solution.py:101
  716.5 13.3 fusion.227
  742.5 24.7 %multiply_reduce_fusion.24 = (f32[16,512]{1,0:T(8,128)S(1)}, f32[16,512,1024]{2,1,0:T(8,128)}) fusion(f32[16,512,1024]{2,1,0:T(8,128)} %fusion.227, f32[16,512]{1,0:T(8,128)S(1)} %dynamic-slice_bitcast_fusion.2, bf16[1,1024,16,32]{1,3,2,0:T(8,128)(2,1)S(1)} %copy-done.5, bf16[1,1024,16,32]{1,3,2,0:T(8,128)(2,1)S(1)} %copy-done.8, s32[]{:T(128)S(6)} %select_n.95), kind=kOutput, calls=%fused_computation.19.clone.1 | convolution fusion | flops 570417152 | bytes 68747264 | tf_op jit(solution)/shard_map/while/body/eval_jaxpr/cqhe,ckhe->chqk/dot_general | solution.py:96
  767.2 27.9 %multiply_convert_fusion.9 = bf16[16,512,1024]{2,1,0:T(8,128)(2,1)} fusion(f32[16,512,1024]{2,1,0:T(8,128)} %get-tuple-element.537, f32[16,512,1024]{2,1,0:T(8,128)} %fusion.227, f32[16,512]{1,0:T(8,128)S(1)} %get-tuple-element.538, f32[16,512]{1,0:T(8,128)S(1)} %dynamic-slice_bitcast_fusion.2), kind=kLoop, calls=%fused_computation.18.clone.1 | loop fusion | flops 41943040 | bytes 83951616 | tf_op jit(solution)/shard_map/while/body/eval_jaxpr/convert_element_type | solution.py:101
  952.0 40.2 %all-reduce.33 = (bf16[768,8]{0,1:T(8,128)(2,1)S(1)}, bf16[768]{0:T(1024)(128)(2,1)S(1)}, bf16[768]{0:T(1024)(128)(2,1)S(1)}, bf16[768]{0:T(1024)(128)(2,1)S(1)}...) all-reduce(f32[768,8]{0,1:T(8,128)S(1)} %broadcast_multiply_fusion,, ...), channel_id=6, replica_groups=mesh['dp'=16,'band'=2] {'dp','band'}, use_global_device_ids=true, to_apply=%region_34.35.clone | all-reduce | flops 12544 | bytes 75264
  1015.4 19.6 %reduce-scatter.19.cloned.1.call-done = f32[24,768]{1,0:T(8,128)} async-done(((f32[768,768]{1,0:T(8,128)}), f32[24,768]{1,0:T(8,128)}) %reduce-scatter.19.cloned.1.call-update) | async-done | bytes 73744 | tf_op jit(solution)/shard_map/reduce_scatter | solution.py:411
  1040.3 101.4 %reduce-scatter.27.cloned.1.call-done = f32[16,1536]{1,0:T(8,128)} async-done(((f32[512,1536]{1,0:T(8,128)}), f32[16,1536]{1,0:T(8,128)}) %reduce-scatter.27.cloned.1.call-update) | async-done | bytes 98320 | tf_op jit(solution)/shard_map/reduce_scatter | solution.py:346
  1147.3 114.7 %reduce-scatter.15.cloned.1.call-done = f32[24,16,64]{2,1,0:T(8,128)} async-done(((f32[768,16,64]{2,1,0:T(8,128)}), f32[24,16,64]{2,1,0:T(8,128)}) %reduce-scatter.15.cloned.1.call-update) | async-done | bytes 98320 | tf_op jit(solution)/shard_map/reduce_scatter | solution.py:405
  1267.5 132.9 %reduce-scatter.33.cloned.1.call-done = f32[64,512]{1,0:T(8,128)} async-done(((f32[2048,512]{1,0:T(8,128)}), f32[64,512]{1,0:T(8,128)}) %reduce-scatter.33.cloned.1.call-update) | async-done | bytes 131088 | tf_op jit(solution)/shard_map/reduce_scatter | solution.py:351
  1409.7 129.8 %reduce-scatter.31.cloned.1.call-done = f32[16,2048]{1,0:T(8,128)} async-done(((f32[512,2048]{1,0:T(8,128)}), f32[16,2048]{1,0:T(8,128)}) %reduce-scatter.31.cloned.1.call-update) | async-done | bytes 131088 | tf_op jit(solution)/shard_map/reduce_scatter | solution.py:350
  1548.8 115.1 %reduce-scatter.17.cloned.1.call-done = f32[24,2304]{1,0:T(8,128)} async-done(((f32[768,2304]{1,0:T(8,128)}), f32[24,2304]{1,0:T(8,128)}) %reduce-scatter.17.cloned.1.call-update) | async-done | bytes 221200 | tf_op jit(solution)/shard_map/reduce_scatter | solution.py:410
  1669.6 135.7 %reduce-scatter.23.cloned.1.call-done = f32[96,768]{1,0:T(8,128)} async-done(((f32[3072,768]{1,0:T(8,128)}), f32[96,768]{1,0:T(8,128)}) %reduce-scatter.23.cloned.1.call-update) | async-done | bytes 294928 | tf_op jit(solution)/shard_map/reduce_scatter | solution.py:415
  1811.4 134.4 %reduce-scatter.21.cloned.1.call-done = f32[24,3072]{1,0:T(8,128)} async-done(((f32[768,3072]{1,0:T(8,128)}), f32[24,3072]{1,0:T(8,128)}) %reduce-scatter.21.cloned.1.call-update) | async-done | bytes 294928 | tf_op jit(solution)/shard_map/reduce_scatter | solution.py:414
  (585 shorter events, 392.9 us)
Async XLA Ops:
  7.2 72.8 %all-gather.11.cloned.1.call-start = ((), (), s32[]{:S(2)}) async-start(), calls=%async_computation.11 | async-start | bytes 3342336 | tf_op jit(solution)/shard_map/all_gather | solution.py:267
  7.9 296.4 %reduce-scatter.13.cloned.1.call-start = ((), (), s32[]{:S(2)}) async-start(), calls=%async_computation.12 | async-start | bytes 1179648 | tf_op jit(solution)/shard_map/reduce_scatter | solution.py:301
  86.7 127.0 %copy-start.107 = (u32[32]{0:T(128)S(1)}, u32[32]{0:T(128)}, u32[]{:S(2)}) copy-start(u32[32]{0:T(128)} %constant.248) | copy-start | bytes 388
  86.7 131.4 %copy-start.90 = (bf16[32,512]{1,0:T(8,128)(2,1)S(1)}, bf16[32,512]{1,0:T(8,128)(2,1)}, u32[]{:S(2)}) copy-start(bf16[32,512]{1,0:T(8,128)(2,1)} %param.52) | copy-start | bytes 98308
  86.7 166.5 %copy-start.81 = (bf16[48,512]{1,0:T(8,128)(2,1)S(1)}, bf16[48,512]{1,0:T(8,128)(2,1)}, u32[]{:S(2)}) copy-start(bf16[48,512]{1,0:T(8,128)(2,1)} %param.47) | copy-start | bytes 147460
  86.7 219.8 %all-gather.13.cloned.1.call-start = ((), (), s32[]{:S(2)}) async-start(), calls=%async_computation.13 | async-start | bytes 3760128 | tf_op jit(solution)/shard_map/all_gather | solution.py:272
  87.5 228.9 %all-gather.15.cloned.1.call-start = ((), (), s32[]{:S(2)}) async-start(), calls=%async_computation.14 | async-start | bytes 1253376 | tf_op jit(solution)/shard_map/all_gather | solution.py:273
  88.0 231.7 %all-gather.17.cloned.1.call-start = ((), (), s32[]{:S(2)}) async-start(), calls=%async_computation.15 | async-start | bytes 5013504 | tf_op jit(solution)/shard_map/all_gather | solution.py:276
  88.6 314.0 %all-gather.19.cloned.1.call-start = ((), (), s32[]{:S(2)}) async-start(), calls=%async_computation.16 | async-start | bytes 5013504 | tf_op jit(solution)/shard_map/all_gather | solution.py:277
  89.2 372.9 %all-gather.21.cloned.1.call-start = ((), (), s32[]{:S(2)}) async-start(), calls=%async_computation.17 | async-start | bytes 1671168 | tf_op jit(solution)/shard_map/all_gather | solution.py:284
  90.0 477.1 %all-gather.23.cloned.1.call-start = ((), (), s32[]{:S(2)}) async-start(), calls=%async_computation.18 | async-start | bytes 2228224 | tf_op jit(solution)/shard_map/all_gather | solution.py:288
  90.7 497.2 %all-gather.25.cloned.1.call-start = ((), (), s32[]{:S(2)}) async-start(), calls=%async_computation.19 | async-start | bytes 2228224 | tf_op jit(solution)/shard_map/all_gather | solution.py:289
  91.4 917.5 %reduce-scatter.29.cloned.1.call-start = ((), (), s32[]{:S(2)}) async-start(), calls=%async_computation.27 | async-start | bytes 1081344 | tf_op jit(solution)/shard_map/reduce_scatter | solution.py:347
  124.4 179.9 %copy-start.82 = (bf16[768,8]{0,1:T(8,128)(2,1)}, bf16[768,8]{0,1:T(8,128)(2,1)S(1)}, u32[]{:S(2)}) copy-start(bf16[768,8]{0,1:T(8,128)(2,1)S(1)} %reshape.1313) | copy-start | bytes 36868
  124.7 191.6 %copy-start.22 = (f32[1,768]{0,1:T(8,128)}, f32[1,768]{0,1:T(8,128)S(1)}, u32[]{:S(2)}) copy-start(f32[1,768]{0,1:T(8,128)S(1)} %concatenate.80) | copy-start | bytes 9220
  188.1 128.3 %copy-start.24 = (f32[1,768]{0,1:T(8,128)}, f32[1,768]{0,1:T(8,128)S(1)}, u32[]{:S(2)}) copy-start(f32[1,768]{0,1:T(8,128)S(1)} %concatenate.79) | copy-start | bytes 9220
  188.3 273.8 %copy-start.93 = (f32[512]{0:T(512)}, f32[512]{0:T(512)S(1)}, u32[]{:S(2)}) copy-start(f32[512]{0:T(512)S(1)} %convert_element_type.413) | copy-start | bytes 6148
  188.9 273.2 %copy-start.110 = (f32[512]{0:T(512)}, f32[512]{0:T(512)S(1)}, u32[]{:S(2)}) copy-start(f32[512]{0:T(512)S(1)} %convert_element_type.414) | copy-start | bytes 6148
  216.8 89.8 %copy-start.65 = (f32[768]{0:T(1024)}, f32[768]{0:T(1024)S(1)}, u32[]{:S(2)}) copy-start(f32[768]{0:T(1024)S(1)} %convert_element_type.396) | copy-start | bytes 9220
  216.8 103.0 %copy-start.60 = (f32[768]{0:T(1024)}, f32[768]{0:T(1024)S(1)}, u32[]{:S(2)}) copy-start(f32[768]{0:T(1024)S(1)} %convert_element_type.405) | copy-start | bytes 9220
  216.8 89.8 %copy-start.69 = (f32[768]{0:T(1024)}, f32[768]{0:T(1024)S(1)}, u32[]{:S(2)}) copy-start(f32[768]{0:T(1024)S(1)} %convert_element_type.397) | copy-start | bytes 9220
  216.8 102.9 %copy-start.63 = (f32[768]{0:T(1024)}, f32[768]{0:T(1024)S(1)}, u32[]{:S(2)}) copy-start(f32[768]{0:T(1024)S(1)} %convert_element_type.406) | copy-start | bytes 9220
  218.2 190.9 %copy-start.97 = (f32[1024]{0:T(1024)}, f32[1024]{0:T(1024)S(1)}, u32[]{:S(2)}) copy-start(f32[1024]{0:T(1024)S(1)} %broadcast_subtract_fusion) | copy-start | bytes 12292
  617.1 395.1 %reduce-scatter.25.cloned.1.call-start = ((), (), s32[]{:S(2)}) async-start(), calls=%async_computation.25 | async-start | bytes 1622016 | tf_op jit(solution)/shard_map/reduce_scatter | solution.py:342
  836.5 198.5 %reduce-scatter.19.cloned.1.call-start = ((), (), s32[]{:S(2)}) async-start(), calls=%async_computation.22 | async-start | bytes 2433024 | tf_op jit(solution)/shard_map/reduce_scatter | solution.py:411
  854.8 287.0 %reduce-scatter.27.cloned.1.call-start = ((), (), s32[]{:S(2)}) async-start(), calls=%async_computation.26 | async-start | bytes 3244032 | tf_op jit(solution)/shard_map/reduce_scatter | solution.py:346
  863.2 398.7 %reduce-scatter.15.cloned.1.call-start = ((), (), s32[]{:S(2)}) async-start(), calls=%async_computation.20 | async-start | bytes 6488064 | tf_op jit(solution)/shard_map/reduce_scatter | solution.py:405
  898.5 502.0 %reduce-scatter.33.cloned.1.call-start = ((), (), s32[]{:S(2)}) async-start(), calls=%async_computation.29 | async-start | bytes 4325376 | tf_op jit(solution)/shard_map/reduce_scatter | solution.py:351
  908.2 631.3 %reduce-scatter.31.cloned.1.call-start = ((), (), s32[]{:S(2)}) async-start(), calls=%async_computation.28 | async-start | bytes 4325376 | tf_op jit(solution)/shard_map/reduce_scatter | solution.py:350
  916.2 747.7 %reduce-scatter.17.cloned.1.call-start = ((), (), s32[]{:S(2)}) async-start(), calls=%async_computation.21 | async-start | bytes 7299072 | tf_op jit(solution)/shard_map/reduce_scatter | solution.py:410
  923.0 882.3 %reduce-scatter.23.cloned.1.call-start = ((), (), s32[]{:S(2)}) async-start(), calls=%async_computation.24 | async-start | bytes 9732096 | tf_op jit(solution)/shard_map/reduce_scatter | solution.py:415
  931.8 1014.1 %reduce-scatter.21.cloned.1.call-start = ((), (), s32[]{:S(2)}) async-start(), calls=%async_computation.23 | async-start | bytes 9732096 | tf_op jit(solution)/shard_map/reduce_scatter | solution.py:414
  (127 other events, 1903.5 us)
Sparse Core Ops, SparseCore 0:
  10.8 69.1 all-gather.10
  86.8 8.1 reduce-scatter.12
  98.3 71.6 all-gather.12
  173.0 55.3 all-gather.14
  231.4 88.2 all-gather.16
  322.8 79.8 all-gather.18
  405.8 56.3 all-gather.20
  465.3 59.9 all-gather.22
  528.4 59.4 all-gather.24
  617.2 129.0 reduce-scatter.28
  836.6 94.6 reduce-scatter.24
  936.5 98.5 reduce-scatter.18
  1041.4 100.3 reduce-scatter.26
  1148.2 113.7 reduce-scatter.14
  1264.1 136.3 reduce-scatter.32
  1402.6 136.9 reduce-scatter.30
  1545.1 118.7 reduce-scatter.16
  1670.7 134.5 reduce-scatter.22
  1811.1 134.6 reduce-scatter.20
where the time goes:
time: 1970 us; the launch traced here: 1960 us
  waiting for transfers between devices  1100 us (56%)
  matrix products  326 us (17%)
  blocking collectives  282 us (14%)
  other arithmetic  147 us (7%)
  local copies, waits for them, and re-layouts  75 us (4%)
    reduce_scatter x1, waiting for transfers between devices, per_device(): lax.psum_scatter(enc_grads[7], ('dp', 'band'), scatter_dimension=0, tiled...  136 us
    reduce_scatter x1, waiting for transfers between devices, per_device(): lax.psum_scatter(enc_grads[6], ('dp', 'band'), scatter_dimension=0, tiled...  134 us
    reduce_scatter x1, waiting for transfers between devices, per_device(): lax.psum_scatter(dec_grads[7], ('dp', 'band'), scatter_dimension=0, tiled...  133 us
    reduce_scatter x1, waiting for transfers between devices, per_device(): lax.psum_scatter(dec_grads[6], ('dp', 'band'), scatter_dimension=0, tiled...  130 us
    unnamed x4, blocking collectives  126 us
    reduce_scatter x1, waiting for transfers between devices, per_device(): lax.psum_scatter(enc_grads[2], ('dp', 'band'), scatter_dimension=0, tiled...  115 us
    reduce_scatter x1, waiting for transfers between devices, per_device(): lax.psum_scatter(grad_table, ('dp', 'band'), scatter_dimension=0, tiled=T...  115 us
    reduce_scatter x1, waiting for transfers between devices, per_device(): lax.psum_scatter(dec_grads[2], ('dp', 'band'), scatter_dimension=0, tiled...  101 us
  transfers between devices with their start and end apart: 19, of which 13 were waited for; matrix products, arithmetic and copies ran while one was open for 25% of the time, Pallas kernels for 0%

commit v1 on v0

v1 whole, which is shorter than its diff:
```python
import functools
import math

import jax
import jax.numpy as jnp
from jax import lax
from jax.experimental import pallas as pl
from jax.experimental.pallas import tpu as pltpu
from jax.sharding import PartitionSpec as P

HEADS_ENC = 12
HEADS_DEC = 16
EPSILON = 1e-05
F32 = jnp.float32
BF16 = jnp.bfloat16
BOTH = ("dp", "band")


def dot(a, b, ca, cb):
    return lax.dot_general(a, b, (((ca,), (cb,)), ((), ())), preferred_element_type=F32)


def sincos(place_index, model_width):
    half_width = model_width // 2
    frequency = jnp.exp(-math.log(10000.0) * jnp.arange(half_width, dtype=F32) / half_width)
    angles = place_index[..., None] * frequency
    return jnp.concatenate([jnp.sin(angles), jnp.cos(angles)], -1)


def attend_forward_kernel(q_ref, k_ref, v_ref, out_ref, lse_ref, *, head_size, scale):
    log_scale = scale * math.log2(math.e)
    for first in range(0, q_ref.shape[0], head_size):
        rows = slice(first, first + head_size)
        scores = dot(k_ref[rows], q_ref[rows], 0, 0)
        top = jnp.max(scores, axis=0, keepdims=True) * log_scale
        weights = jnp.exp2(scores * log_scale - top)
        total = jnp.sum(weights, axis=0, keepdims=True)
        mixed = dot(v_ref[rows], weights.astype(BF16), 1, 0)
        out_ref[rows] = (mixed / total).astype(BF16)
        lse_ref[first // head_size] = top + jnp.log2(total)


def attend_forward(mixed_rows, head_count, heads_a_step):
    triple, length = mixed_rows.shape
    width = triple // 3
    head_size = width // head_count
    steps = head_count // heads_a_step
    slab = heads_a_step * head_size
    part = lambda which: pl.BlockSpec((slab, length), lambda h: (which * steps + h, 0))
    return pl.pallas_call(
        functools.partial(attend_forward_kernel, head_size=head_size, scale=head_size**-0.5),
        grid=(steps,),
        in_specs=[part(0), part(1), part(2)],
        out_specs=[part(0), pl.BlockSpec((heads_a_step, 1, length), lambda h: (h, 0, 0))],
        out_shape=[
            jax.ShapeDtypeStruct((width, length), BF16),
            jax.ShapeDtypeStruct((head_count, 1, length), F32),
        ],
        compiler_params=pltpu.CompilerParams(vmem_limit_bytes=40 << 20),
    )(mixed_rows, mixed_rows, mixed_rows)


def attend_backward_kernel(
    q_ref, k_ref, v_ref, out_ref, grad_ref, lse_ref, grad_mixed_ref, *, head_size, scale
):
    log_scale = scale * math.log2(math.e)
    for first in range(0, q_ref.shape[0], head_size):
        rows = slice(first, first + head_size)
        q, k, v, grad = q_ref[rows], k_ref[rows], v_ref[rows], grad_ref[rows]
        delta = jnp.sum(grad.astype(F32) * out_ref[rows].astype(F32), axis=0, keepdims=True)
        probs = jnp.exp2(dot(k, q, 0, 0) * log_scale - lse_ref[first // head_size])
        grad_probs = dot(v, grad, 0, 0)
        grad_scores = (probs * (grad_probs - delta)).astype(BF16)
        grad_mixed_ref[0, rows] = (dot(k, grad_scores, 1, 0) * scale).astype(BF16)
        grad_mixed_ref[1, rows] = (dot(q, grad_scores, 1, 1) * scale).astype(BF16)
        grad_mixed_ref[2, rows] = dot(grad, probs.astype(BF16), 1, 1).astype(BF16)


def attend_backward(mixed_rows, out_rows, grad_rows, lse, head_count, heads_a_step):
    triple, length = mixed_rows.shape
    width = triple // 3
    head_size = width // head_count
    steps = head_count // heads_a_step
    slab = heads_a_step * head_size
    part = lambda which: pl.BlockSpec((slab, length), lambda h: (which * steps + h, 0))
    grads = pl.pallas_call(
        functools.partial(attend_backward_kernel, head_size=head_size, scale=head_size**-0.5),
        grid=(steps,),
        in_specs=[
            part(0),
            part(1),
            part(2),
            part(0),
            part(0),
            pl.BlockSpec((heads_a_step, 1, length), lambda h: (h, 0, 0)),
        ],
        out_specs=pl.BlockSpec((3, slab, length), lambda h: (0, h, 0)),
        out_shape=jax.ShapeDtypeStruct((3, width, length), BF16),
        compiler_params=pltpu.CompilerParams(vmem_limit_bytes=40 << 20),
    )(mixed_rows, mixed_rows, mixed_rows, out_rows, grad_rows, lse)
    return grads.reshape(triple, length)


def norm_forward(rows_in, gain_row, shift_row):
    centred = rows_in - jnp.mean(rows_in, -1, keepdims=True)
    inverse = lax.rsqrt(jnp.mean(centred * centred, -1, keepdims=True) + EPSILON)
    unit_rows = centred * inverse
    return (unit_rows * gain_row + shift_row).astype(BF16), unit_rows, inverse


def norm_backward(grad_normed, unit_rows, inverse, gain_row):
    grad_unit = grad_normed * gain_row
    grad_input = inverse * (
        grad_unit
        - jnp.mean(grad_unit, -1, keepdims=True)
        - unit_rows * jnp.mean(grad_unit * unit_rows, -1, keepdims=True)
    )
    return grad_input, jnp.sum(grad_normed * unit_rows, 0), jnp.sum(grad_normed, 0)


def gelu_tanh(upper):
    return jax.nn.gelu(upper, approximate=True)


def block_forward(rows_in, weights, head_count, heads_a_step):
    gain_one, shift_one, w_qkv, w_out, gain_two, shift_two, w_up, w_down = weights
    normed_one, unit_one, inverse_one = norm_forward(rows_in, gain_one, shift_one)
    mixed_rows = dot(w_qkv, normed_one, 0, 1).astype(BF16)
    attn_rows, lse = attend_forward(mixed_rows, head_count, heads_a_step)
    middle = rows_in + dot(attn_rows, w_out, 0, 0)
    normed_two, unit_two, inverse_two = norm_forward(middle, gain_two, shift_two)
    upper = dot(normed_two, w_up, 1, 0)
    active = gelu_tanh(upper).astype(BF16)
    rows_out = middle + dot(active, w_down, 1, 0)
    saved = (
        unit_one, inverse_one, normed_one, mixed_rows, lse, attn_rows,
        unit_two, inverse_two, normed_two, upper, active,
    )
    return rows_out, saved


def block_backward(grad_out, weights, saved, head_count, heads_a_step):
    gain_one, shift_one, w_qkv, w_out, gain_two, shift_two, w_up, w_down = weights
    (
        unit_one, inverse_one, normed_one, mixed_rows, lse, attn_rows,
        unit_two, inverse_two, normed_two, upper, active,
    ) = saved
    grad_branch = grad_out.astype(BF16)
    grad_down = dot(active, grad_branch, 0, 0).astype(BF16)
    grad_active = dot(grad_branch, w_down, 1, 1)
    grad_upper = jax.vjp(gelu_tanh, upper)[1](grad_active)[0].astype(BF16)
    grad_up = dot(normed_two, grad_upper, 0, 0).astype(BF16)
    grad_normed = dot(grad_upper, w_up, 1, 1)
    grad_middle, grad_gain_two, grad_shift_two = norm_backward(
        grad_normed, unit_two, inverse_two, gain_two
    )
    grad_middle = grad_out + grad_middle
    grad_attn_branch = grad_middle.astype(BF16)
    grad_wout = dot(attn_rows, grad_attn_branch, 1, 0).astype(BF16)
    grad_attn = dot(w_out, grad_attn_branch, 1, 1).astype(BF16)
    grad_mixed = attend_backward(mixed_rows, attn_rows, grad_attn, lse, head_count, heads_a_step)
    grad_qkv = dot(normed_one, grad_mixed, 0, 1).astype(BF16)
    grad_normed_one = dot(grad_mixed, w_qkv, 0, 1)
    grad_input, grad_gain_one, grad_shift_one = norm_backward(
        grad_normed_one, unit_one, inverse_one, gain_one
    )
    vectors = (grad_gain_one, grad_shift_one, grad_gain_two, grad_shift_two)
    return grad_middle + grad_input, vectors, (grad_qkv, grad_wout, grad_up, grad_down)


def swap(array):
    return lax.ppermute(array, "band", [(0, 1), (1, 0)])


def join_pair(mine, axis):
    first = lax.axis_index("band") == 0
    other = swap(mine)
    return jnp.concatenate([jnp.where(first, mine, other), jnp.where(first, other, mine)], axis)


def groups_of(shards):
    rows = 0
    for shard in shards:
        rows = math.gcd(rows, shard.shape[0] // 2)
    return rows


def pack_rows(array, rows):
    lead, (length, width) = array.shape[:-2], array.shape[-2:]
    array = array.reshape(*lead, length // rows, rows, width)
    return jnp.swapaxes(array, -3, -2).reshape(*lead, rows, length // rows * width)


def unpack_rows(array, width):
    lead, (rows, total) = array.shape[:-2], array.shape[-2:]
    array = array.reshape(*lead, rows, total // width, width)
    return jnp.swapaxes(array, -3, -2).reshape(*lead, rows * (total // width), width)


def gather_all(shards):
    rows = groups_of(shards)
    side = lax.axis_index("band")
    halves = [
        lax.dynamic_slice_in_dim(s, side * (s.shape[0] // 2), s.shape[0] // 2, 0) for s in shards
    ]
    packed = jnp.concatenate([pack_rows(h, rows) for h in halves], 1)
    whole = lax.all_gather(packed, BOTH, axis=0, tiled=False)
    out, at = [], 0
    for half in halves:
        span = half.size // rows
        piece = unpack_rows(whole[:, :, at : at + span], half.shape[1])
        out.append(piece.reshape(-1, half.shape[1]))
        at += span
    return out


def scatter_sums(grads, device_count):
    split = [g.reshape(device_count, -1, g.shape[1]) for g in grads]
    rows = 0
    for s in split:
        rows = math.gcd(rows, s.shape[1])
    packed = jnp.concatenate([pack_rows(s, rows) for s in split], 2)
    summed = lax.psum_scatter(packed, BOTH, scatter_dimension=0, tiled=False)
    both = join_pair(summed[None], 0)
    out, at = [], 0
    for s in split:
        span = s.shape[1] * s.shape[2] // rows
        piece = unpack_rows(both[:, :, at : at + span], s.shape[2])
        out.append(piece.reshape(-1, s.shape[2]).astype(F32))
        at += span
    return out


LANES = 128


def columns(vectors):
    stacked = jnp.concatenate([v if v.ndim == 2 else v[:, None] for v in vectors], 1)
    return jnp.pad(stacked, ((0, 0), (0, LANES - stacked.shape[1])))


def per_device(
    pixels, time_loc, band_mask, wavelengths, visible, band_table, cls_token, loc_weight,
    enc_attn_gain, enc_attn_shift, enc_qkv, enc_out, enc_mlp_gain, enc_mlp_shift, enc_up, enc_down,
    projection, mask_token, dec_attn_gain, dec_attn_shift, dec_qkv, dec_out, dec_mlp_gain,
    dec_mlp_shift, dec_up, dec_down, cotangent, *, device_count,
):
    side = lax.axis_index("band")
    table_rows = band_table.shape[0]
    wave_count, pixel_size = band_table.shape[1:]
    (
        table, enc_vectors, w_enc_qkv, w_enc_out, w_enc_up, w_enc_down, w_proj,
        dec_vectors, w_dec_qkv, w_dec_out, w_dec_up, w_dec_down,
    ) = gather_all([
        band_table.reshape(table_rows, -1),
        columns([cls_token, enc_attn_gain, enc_attn_shift, enc_mlp_gain, enc_mlp_shift, loc_weight]),
        enc_qkv, enc_out, enc_up, enc_down, projection,
        columns([mask_token, dec_attn_gain, dec_attn_shift, dec_mlp_gain, dec_mlp_shift]),
        dec_qkv, dec_out, dec_up, dec_down,
    ])
    enc_vec = enc_vectors.T.astype(F32)
    dec_vec = dec_vectors.T.astype(F32)
    loc_rows = enc_vec[5 : 5 + loc_weight.shape[1]]
    enc_weights = (
        enc_vec[1], enc_vec[2], w_enc_qkv, w_enc_out, enc_vec[3], enc_vec[4], w_enc_up, w_enc_down
    )
    dec_weights = (
        dec_vec[1], dec_vec[2], w_dec_qkv, w_dec_out, dec_vec[3], dec_vec[4], w_dec_up, w_dec_down
    )

    def own_chip(array):
        mine = lax.dynamic_index_in_dim(array, side, 0, keepdims=False)
        theirs = lax.dynamic_index_in_dim(array, 1 - side, 0, keepdims=False)
        return jnp.concatenate([mine, swap(theirs)], -1)

    chip_pixels = own_chip(pixels)
    chip_mask = own_chip(band_mask)
    chip_waves = own_chip(wavelengths)
    picks = visible[0]
    slot_wave = (chip_waves[:, None] == jnp.arange(wave_count, dtype=jnp.int32)) & (
        chip_mask[:, None] > 0
    )
    same_pixel = jnp.arange(pixel_size)[:, None] == jnp.arange(pixel_size)
    spread = (slot_wave[:, None, :, None] & same_pixel[None, :, None, :]).astype(BF16)
    spread = spread.reshape(chip_pixels.shape[1], wave_count * pixel_size)
    wave_pixels = dot(chip_pixels, spread, 1, 0).astype(BF16)
    band_count = jnp.sum(chip_mask).astype(F32)

    width = table.shape[0]
    patch_rows = dot(wave_pixels, table, 1, 1) / band_count + sincos(picks.astype(F32), width)
    loc_token = jnp.dot(time_loc, loc_rows, precision=lax.Precision.HIGHEST)
    tokens = jnp.concatenate([enc_vec[0:1], loc_token, patch_rows], 0)
    encoded, enc_saved = block_forward(tokens, enc_weights, HEADS_ENC, HEADS_ENC)
    latent_in = encoded[2:].astype(BF16)
    latent = dot(latent_in, w_proj, 1, 0).astype(BF16)

    positions = jnp.arange(cotangent.shape[1], dtype=jnp.int32)
    matches = positions[:, None] == picks[None, :]
    hidden = 1.0 - jnp.sum(matches.astype(F32), 1, keepdims=True)
    matches = matches.astype(BF16)
    inserted = (
        dot(matches, latent, 1, 0)
        + hidden * dec_vec[0]
        + sincos(positions.astype(F32), latent.shape[1])
    )
    decoded, dec_saved = block_forward(inserted, dec_weights, HEADS_DEC, 1)
    grad_inserted, dec_vec_grads, dec_grads = block_backward(
        cotangent[0].astype(F32), dec_weights, dec_saved, HEADS_DEC, 1
    )
    grad_mask = jnp.sum(grad_inserted * hidden, 0)
    grad_latent = dot(matches, grad_inserted.astype(BF16), 0, 0).astype(BF16)
    grad_proj = dot(latent_in, grad_latent, 0, 0).astype(BF16)
    grad_rows = dot(grad_latent, w_proj, 1, 1)
    dec_sums = scatter_sums(
        [grad_proj, columns((grad_mask,) + dec_vec_grads).astype(BF16), *dec_grads], device_count
    )

    grad_encoded = jnp.concatenate([jnp.zeros((2, width), F32), grad_rows], 0)
    grad_tokens, enc_vec_grads, enc_grads = block_backward(
        grad_encoded, enc_weights, enc_saved, HEADS_ENC, HEADS_ENC
    )
    grad_loc_row = grad_tokens[1:2]
    grad_loc = jnp.dot(grad_loc_row.T, time_loc, precision=lax.Precision.HIGHEST)
    grad_time = jnp.dot(grad_loc_row, loc_rows.T, precision=lax.Precision.HIGHEST)
    grad_raw = (grad_tokens[2:] / band_count).astype(BF16)
    grad_table = dot(grad_raw, wave_pixels, 0, 0).astype(BF16)
    grad_waves = dot(grad_raw, table, 1, 0).astype(BF16)
    grad_chip = dot(grad_waves, spread, 1, 1).astype(BF16)
    here = grad_chip.shape[1] // 2
    mine, theirs = grad_chip[:, :here], swap(grad_chip[:, here:])
    grad_pixels = jnp.where(
        side == 0, jnp.stack([mine, theirs]), jnp.stack([theirs, mine])
    ).astype(F32)
    enc_sums = scatter_sums(
        [
            grad_table,
            columns((grad_tokens[0],) + enc_vec_grads + (grad_loc,)).astype(BF16),
            *enc_grads,
        ],
        device_count,
    )
    s_table, s_enc_vec, s_enc_qkv, s_enc_out, s_enc_up, s_enc_down = enc_sums
    s_proj, s_dec_vec, s_dec_qkv, s_dec_out, s_dec_up, s_dec_down = dec_sums
    return (
        decoded.astype(BF16)[None],
        grad_pixels,
        grad_time,
        s_table.reshape(band_table.shape),
        s_enc_vec[:, 0],
        s_enc_vec[:, 5 : 5 + loc_weight.shape[1]],
        s_enc_vec[:, 1],
        s_enc_vec[:, 2],
        s_enc_qkv,
        s_enc_out,
        s_enc_vec[:, 3],
        s_enc_vec[:, 4],
        s_enc_up,
        s_enc_down,
        s_proj,
        s_dec_vec[:, 0],
        s_dec_vec[:, 1],
        s_dec_vec[:, 2],
        s_dec_qkv,
        s_dec_out,
        s_dec_vec[:, 3],
        s_dec_vec[:, 4],
        s_dec_up,
        s_dec_down,
    )


def solution(mesh):
    dp, chip, both, matrix = P("dp"), P("dp", "band"), P(BOTH, None), P("dp", None)
    block = (dp, dp, matrix, matrix, dp, dp, matrix, matrix)
    in_specs = (
        P("dp", None, "band"), both, chip, chip, both,
        P("dp", None, None), dp, matrix, *block, matrix, dp, *block, P(BOTH, None, None),
    )
    out_specs = (
        P(BOTH, None, None), P("dp", None, "band"), both,
        P("dp", None, None), dp, matrix, *block, matrix, dp, *block,
    )
    return jax.shard_map(
        functools.partial(per_device, device_count=mesh.size),
        mesh=mesh, in_specs=in_specs, out_specs=out_specs, check_vma=False,
    )
```

time: 1970 us -> 700 us (0.36)
  waiting for transfers between devices: 1100 us -> 383 us
  blocking collectives: 282 us -> 0 us
  matrix products: 326 us -> 83.5 us
  other arithmetic: 147 us -> 32.5 us
  Pallas kernels: 0 us -> 80.2 us
    reduce_scatter x11 -> x1, waiting for transfers between devices: 884 us -> 84.6 us  [scatter_sums(): summed = lax.psum_scatter(packed, BOTH, scatter_dimension=0, tiled=False)]
    dot_general x53 -> x34, matrix products: 326 us -> 83.5 us  [the longest x32 82 us: dot(): lax.dot_general(a, b, (((ca,), (cb,)), ((), ())), preferred_element_type=...]
    unnamed x19 -> x4, waiting for transfers between devices: 5.19 us -> 173 us
    all_gather x15 -> x0, blocking collectives: 157 us -> none  [the longest x1 41.4 us: per_device(): lax.all_gather(projection, 'dp', axis=0, tiled=True)]
    unnamed x4 -> x0, blocking collectives: 126 us -> none
    all_gather x8 -> x1, waiting for transfers between devices: 210 us -> 126 us  [gather_all(): whole = lax.all_gather(packed, BOTH, axis=0, tiled=False)]
    pallas_call x0 -> x4, Pallas kernels: none -> 80.2 us  [the longest x2 49.1 us: attend_backward(): pl.pallas_call(functools.partial(attend_backward_kernel, head_size=head_s...]
    convert_element_type x46 -> x17, other arithmetic: 81.1 us -> 8.04 us  [the longest x12 5.88 us: scatter_sums(): out.append(piece.reshape(-1, s.shape[2]).astype(F32))]
  transfers between devices with their start and end apart: 19 -> 9, of which waited for: 13 -> 3; matrix products, arithmetic and copies ran while one was open for 25% -> 11% of each run, Pallas kernels for 0% -> 1%
where the time goes in v1:
time: 700 us; the launch traced here: 694 us
  waiting for transfers between devices  383 us (55%)
  local copies, waits for them, and re-layouts  88.1 us (13%)
  matrix products  83.5 us (12%)
  Pallas kernels  80.2 us (11%)
  other arithmetic  32.5 us (5%)
  between operations  17.1 us (2%)
  starting transfers between devices  9.56 us (1%)
    unnamed x4, waiting for transfers between devices  173 us
    all_gather x1, waiting for transfers between devices, gather_all(): whole = lax.all_gather(packed, BOTH, axis=0, tiled=False)  126 us
    reduce_scatter x1, waiting for transfers between devices, scatter_sums(): summed = lax.psum_scatter(packed, BOTH, scatter_dimension=0, tiled=False)  84.6 us
    dot_general x32, matrix products, dot(): lax.dot_general(a, b, (((ca,), (cb,)), ((), ())), preferred_element_type=...  82 us
    pallas_call x2, Pallas kernels, attend_backward(): pl.pallas_call(functools.partial(attend_backward_kernel, head_size=head_s...  49.1 us
    pallas_call x2, Pallas kernels, attend_forward(): pl.pallas_call(functools.partial(attend_forward_kernel, head_size=head_si...  31.1 us
    unnamed x251, local copies, waits for them, and re-layouts  27 us
    slice x8, local copies, waits for them, and re-layouts, gather_all(): piece = unpack_rows(whole[:, :, at:at + span], half.shape[1])  26.5 us
  transfers between devices with their start and end apart: 9, of which 3 were waited for; matrix products, arithmetic and copies ran while one was open for 11% of the time, Pallas kernels for 1%

profile of v1, /device:TPU:1, one launch (start us, length us, event | category | flops | bytes accessed | tf_op | source)
XLA Modules:
  0.0 694.5 jit_solution(10328575088887155424)
XLA Ops:
  25.3 4.8 multiply_sine_fusion
  33.3 4.5 and.35
  37.8 2.8 convolution_convert_fusion.12
  40.6 125.7 %all-gather.3.cloned.1.call-done = bf16[256,45184]{1,0:T(8,128)(2,1)} async-done(((bf16[8,45184]{1,0:T(8,128)(2,1)}), bf16[256,45184]{1,0:T(8,128)(2,1)}) %all-gather.3.cloned.1.call-update) | async-done | bytes 23134224 | tf_op jit(solution)/shard_map/all_gather | solution.py:207
  172.9 4.1 fusion.66
  177.0 4.0 slice.214
  181.1 4.8 fusion.65
  185.8 7.9 %fusion.67 = (bf16[32,8,9216]{2,1,0:T(8,128)(2,1)}, bf16[32,8,9216]{2,1,0:T(8,128)(2,1)}) fusion(bf16[32,8,45184]{2,1,0:T(8,128)(2,1)} %bitcast.337), kind=kLoop, calls=%fused_computation.247 | loop fusion | bytes 18874368 | tf_op jit(solution)/shard_map/slice | solution.py:211
  199.7 3.4 shard_map.442
  209.3 2.5 fusion.69
  213.3 4.0 convolution_convert_fusion.4.q_ref.k_ref.v_ref
  217.3 27.8 %shard_map.443 = (bf16[512,1024]{1,0:T(8,128)(2,1)S(1)}, f32[16,1,1024]{2,1,0:T(1,128)S(1)}) custom-call(bf16[1536,1024]{1,0:T(8,128)(2,1)S(1)} %convolution_convert_fusion.4.q_ref.k_ref.v_ref, bf16[1536,1024]{1,0:T(8,128)(2,1)S(1)} %convolution_convert_fusion.4.q_ref.k_ref.v_ref, bf16[1536,1024]{1,0:T(8,128)(2,1)S(1)} %convolution_convert_fusion.4.q_ref.k_ref.v_ref), custom_call_target="tpu_custom_call" | custom-call | tf_op jit(solution)/shard_map/pallas_call | solution.py:50
  247.6 2.6 fusion.64
  250.3 4.4 convolution_convert_fusion.5
  254.6 7.6 %fusion.6 = bf16[1024,2048]{1,0:T(8,128)(2,1)S(1)} fusion(f32[1024,2048]{1,0:T(8,128)S(1)} %fusion.64, bf16[2048,512]{1,0:T(8,128)(2,1)S(1)} %bitcast.366, bf16[1,1024,512]{2,1,0:T(8,128)(2,1)S(1)} %copy-done.44), kind=kOutput, calls=%fused_computation.8 | convolution fusion | flops 2189426688 | bytes 15728640 | tf_op jit(solution)/shard_map/dot_general | solution.py:20
  262.2 4.3 fusion.72
  266.5 3.8 convolution_convert_fusion.6
  270.3 2.9 copy.139
  273.3 3.1 multiply_reduce_fusion
  281.1 45.5 %shard_map.444 = bf16[3,512,1024]{2,1,0:T(8,128)(2,1)S(1)} custom-call(bf16[1536,1024]{1,0:T(8,128)(2,1)S(1)} %convolution_convert_fusion.4.q_ref.k_ref.v_ref, bf16[1536,1024]{1,0:T(8,128)(2,1)S(1)} %convolution_convert_fusion.4.q_ref.k_ref.v_ref, bf16[1536,1024]{1,0:T(8,128)(2,1)S(1)} %convolution_convert_fusion.4.q_ref.k_ref.v_ref, ...), custom_call_target="tpu_custom_call" | custom-call | tf_op jit(solution)/shard_map/pallas_call | solution.py:86
  326.7 3.2 fusion.71
  329.9 3.2 convolution_convert_fusion.7
  333.2 3.2 copy.140
  352.1 7.0 %fusion.16 = bf16[256,3072]{1,0:T(8,128)(2,1)S(1)} fusion(f32[256,3072]{1,0:T(8,128)} %copy-done.104, bf16[3072,768]{1,0:T(8,128)(2,1)} %bitcast.352, f32[254,768]{1,0:T(8,128)S(1)} %fusion.73), kind=kOutput, calls=%fused_computation.29 | convolution fusion | flops 1223688192 | bytes 10217472 | tf_op jit(solution)/shard_map/dot_general | solution.py:20
  362.7 3.6 shard_map.445
  369.9 4.4 convolution_convert_fusion
  387.6 2.6 constant_dynamic-update-slice_fusion.12
  391.4 3.7 convolution_convert_fusion.15
  397.3 7.7 %fusion.17 = bf16[1,1024,512]{1,2,0:T(8,128)(2,1)S(1)} fusion(f32[1024,512]{0,1:T(8,128)S(1)} %copy-done.10, bf16[2048,512]{1,0:T(8,128)(2,1)} %bitcast.365, f32[1024,2048]{1,0:T(8,128)} %copy-done.103), kind=kOutput, calls=%fused_computation.58 | convolution fusion | flops 2167406592 | bytes 13631488 | tf_op jit(solution)/shard_map/dot_general | solution.py:20
  405.0 84.6 %reduce-scatter.5.cloned.1.call-done = bf16[1,8,14080]{2,1,0:T(8,128)(2,1)} async-done(((bf16[32,8,14080]{2,1,0:T(8,128)(2,1)}), bf16[1,8,14080]{2,1,0:T(8,128)(2,1)}) %reduce-scatter.5.cloned.1.call-update) | async-done | bytes 225296 | tf_op jit(solution)/shard_map/reduce_scatter | solution.py:223
  489.6 6.1 collective-permute-start.5
  503.0 172.9 %reduce-scatter.7.cloned.1.call-done = bf16[1,24,10368]{2,1,0:T(8,128)(2,1)} async-done(((bf16[32,24,10368]{2,1,0:T(8,128)(2,1)}), bf16[1,24,10368]{2,1,0:T(8,128)(2,1)}) %reduce-scatter.7.cloned.1.call-update) | async-done | bytes 497680
  (406 shorter events, 104.6 us)
Async XLA Ops:
  7.2 8.7 %copy-start = (bf16[48,3072]{1,0:T(8,128)(2,1)S(1)}, bf16[48,3072]{1,0:T(8,128)(2,1)}, u32[]{:S(2)}) copy-start(bf16[48,3072]{1,0:T(8,128)(2,1)} %param.41) | copy-start | bytes 884740
  7.2 11.6 %copy-start.98 = (s32[2,7]{1,0:T(2,128)S(1)}, s32[2,7]{1,0:T(2,128)}, u32[]{:S(2)}) copy-start(s32[2,7]{1,0:T(2,128)} %param.29) | copy-start | bytes 172
  7.2 12.3 %copy-start.99 = (s32[2,7]{1,0:T(2,128)S(1)}, s32[2,7]{1,0:T(2,128)}, u32[]{:S(2)}) copy-start(s32[2,7]{1,0:T(2,128)} %param.30) | copy-start | bytes 172
  7.2 12.8 %copy-start.51 = (bf16[2,254,448]{1,2,0:T(8,128)(2,1)S(1)}, bf16[2,254,448]{1,2,0:T(8,128)(2,1)}, u32[]{:S(2)}) copy-start(bf16[2,254,448]{1,2,0:T(8,128)(2,1)} %param.27) | copy-start | bytes 1365508
  7.2 13.6 %copy-start.92 = (s32[1,254]{1,0:T(1,128)S(1)}, s32[1,254]{1,0:T(1,128)}, u32[]{:S(2)}) copy-start(s32[1,254]{1,0:T(1,128)} %param.31) | copy-start | bytes 3052
  7.3 13.6 %copy-start.43 = (bf16[1,1024,512]{2,1,0:T(8,128)(2,1)S(1)}, bf16[1,1024,512]{2,1,0:T(8,128)(2,1)}, u32[]{:S(2)}) copy-start(bf16[1,1024,512]{2,1,0:T(8,128)(2,1)} %param.53) | copy-start | bytes 3145732
  7.3 159.0 %all-gather.3.cloned.1.call-start = ((), (), s32[]{:S(2)}) async-start(), calls=%async_computation.3 | async-start | bytes 23857152 | tf_op jit(solution)/shard_map/all_gather | solution.py:207
  18.8 470.8 %reduce-scatter.5.cloned.1.call-start = ((), (), s32[]{:S(2)}) async-start(), calls=%async_computation.2 | async-start | bytes 7434240 | tf_op jit(solution)/shard_map/reduce_scatter | solution.py:223
  19.5 10.6 %collective-permute-start.2 = (s32[7]{0:T(128)S(1)}, s32[7]{0:T(128)S(1)}, u32[]{:S(2)}, u32[]{:S(2)}) collective-permute-start(s32[7]{0:T(128)S(1)} %get-tuple-element.211), channel_id=1, source_target_pairs={{0,1},{1,0},{2,3},{3,2},{4,5},{5,4},{6,7},{7,6},{8,9},{9,8},{10,11... | collective-permute-start | bytes 92 | tf_op jit(solution)/shard_map/ppermute | solution.py:172
  19.5 12.5 %collective-permute-start.1 = (s32[7]{0:T(128)S(1)}, s32[7]{0:T(128)S(1)}, u32[]{:S(2)}, u32[]{:S(2)}) collective-permute-start(s32[7]{0:T(128)S(1)} %get-tuple-element.214), channel_id=1, source_target_pairs={{0,1},{1,0},{2,3},{3,2},{4,5},{5,4},{6,7},{7,6},{8,9},{9,8},{10,11... | collective-permute-start | bytes 92 | tf_op jit(solution)/shard_map/ppermute | solution.py:172
  20.8 17.0 %collective-permute-start = (bf16[254,448]{0,1:T(8,128)(2,1)}, bf16[254,448]{0,1:T(8,128)(2,1)}, u32[]{:S(2)}, u32[]{:S(2)}) collective-permute-start(bf16[254,448]{0,1:T(8,128)(2,1)} %get-tuple-element.200), channel_id=1, source_target_pairs={{0,1},{1,0},{2,3},{3,2},{4,5},{5,4},{6,7},{7,6},{8,9},{9,8},{10,11... | collective-permute-start | bytes 682760 | tf_op jit(solution)/shard_map/ppermute | solution.py:172
  37.8 130.4 %copy-start.45 = (pred[896,1024]{1,0:T(32,128)(4,1)}, pred[896,1024]{1,0:T(32,128)(4,1)S(1)}, u32[]{:S(2)}) copy-start(pred[896,1024]{1,0:T(32,128)(4,1)S(1)} %and.35) | copy-start | bytes 2752516
  171.3 38.0 %copy-start.30 = (bf16[32,8,1536]{2,1,0:T(8,128)(2,1)}, bf16[32,8,1536]{2,1,0:T(8,128)(2,1)S(1)}, u32[]{:S(2)}) copy-start(bf16[32,8,1536]{2,1,0:T(8,128)(2,1)S(1)} %slice.224) | copy-start | bytes 2359300
  172.9 30.2 %copy-start.26 = (bf16[32,8,2304]{2,1,0:T(8,128)(2,1)}, bf16[32,8,2304]{2,1,0:T(8,128)(2,1)S(1)}, u32[]{:S(2)}) copy-start(bf16[32,8,2304]{2,1,0:T(8,128)(2,1)S(1)} %slice.217) | copy-start | bytes 3538948
  185.8 9.5 %copy-start.101 = (f32[1,8]{1,0:T(1,128)S(1)}, f32[1,8]{1,0:T(1,128)}, u32[]{:S(2)}) copy-start(f32[1,8]{1,0:T(1,128)} %param.28) | copy-start | bytes 100
  195.3 7.8 %copy-start.60 = (f32[1,768]{1,0:T(1,128)}, f32[1,768]{1,0:T(1,128)S(1)}, u32[]{:S(2)}) copy-start(f32[1,768]{1,0:T(1,128)S(1)} %get-tuple-element.205) | copy-start | bytes 9220
  195.3 8.7 %copy-start.56 = (f32[768]{0:T(1024)}, f32[768]{0:T(1024)S(1)}, u32[]{:S(2)}) copy-start(f32[768]{0:T(1024)S(1)} %get-tuple-element.167) | copy-start | bytes 9220
  195.5 7.7 %copy-start.67 = (f32[1,768]{1,0:T(1,128)}, f32[1,768]{1,0:T(1,128)S(1)}, u32[]{:S(2)}) copy-start(f32[1,768]{1,0:T(1,128)S(1)} %fusion.41) | copy-start | bytes 9220
  217.3 27.8 %copy-start.12 = (f32[1024,512]{0,1:T(8,128)S(1)}, f32[1024,512]{0,1:T(8,128)}, u32[]{:S(2)}) copy-start(f32[1024,512]{0,1:T(8,128)} %copy-done.11) | copy-start | bytes 6291460
  217.3 27.8 %copy-start.24 = (bf16[32,8,1024]{2,1,0:T(8,128)(2,1)S(1)}, bf16[32,8,1024]{2,1,0:T(8,128)(2,1)}, u32[]{:S(2)}) copy-start(bf16[32,8,1024]{2,1,0:T(8,128)(2,1)} %slice.230) | copy-start | bytes 1572868
  245.9 20.6 %copy-start.8 = (f32[1024,512]{0,1:T(8,128)}, f32[1024,512]{0,1:T(8,128)S(1)}, u32[]{:S(2)}) copy-start(f32[1024,512]{0,1:T(8,128)S(1)} %get-tuple-element.220) | copy-start | bytes 6291460
  245.9 20.5 %copy-start.65 = (f32[1024]{0:T(1024)}, f32[1024]{0:T(1024)S(1)}, u32[]{:S(2)}) copy-start(f32[1024]{0:T(1024)S(1)} %broadcast_multiply_fusion.4) | copy-start | bytes 12292
  246.3 20.2 %copy-start.72 = (f32[1024]{0:T(1024)}, f32[1024]{0:T(1024)S(1)}, u32[]{:S(2)}) copy-start(f32[1024]{0:T(1024)S(1)} %add_rsqrt_fusion) | copy-start | bytes 12292
  281.1 45.5 %copy-start.39 = (bf16[32,8,3072]{2,1,0:T(8,128)(2,1)S(1)}, bf16[32,8,3072]{2,1,0:T(8,128)(2,1)}, u32[]{:S(2)}) copy-start(bf16[32,8,3072]{2,1,0:T(8,128)(2,1)} %get-tuple-element.189) | copy-start | bytes 4718596
  350.5 8.6 %slice-start.2 = ((s8[4718592]{0:T(1024)(128)(4,1)}), s8[524288]{0:T(1024)(128)(4,1)S(1)}, s32[]{:S(2)}) async-start(s8[4718592]{0:T(1024)(128)(4,1)} %bitcast.349), calls=%async_computation.7 | async-start | bytes 1048576
  350.5 325.3 %reduce-scatter.7.cloned.1.call-start = ((), (), s32[]{:S(2)}) async-start(), calls=%async_computation.4 | async-start | bytes 16422912
  352.0 9.4 %copy-start.32 = (f32[254,768]{1,0:T(8,128)}, f32[254,768]{1,0:T(8,128)S(1)}, u32[]{:S(2)}) copy-start(f32[254,768]{1,0:T(8,128)S(1)} %fusion.73) | copy-start | bytes 2340868
  352.1 7.1 %copy-start.19 = (f32[256,768]{1,0:T(8,128)S(1)}, f32[256,768]{1,0:T(8,128)}, u32[]{:S(2)}) copy-start(f32[256,768]{1,0:T(8,128)} %copy-done.18) | copy-start | bytes 2359300
  397.0 101.5 %collective-permute-start.3 = (bf16[254,448]{1,0:T(8,128)(2,1)}, bf16[254,448]{1,0:T(8,128)(2,1)}, u32[]{:S(2)}, u32[]{:S(2)}) collective-permute-start(bf16[254,448]{1,0:T(8,128)(2,1)} %get-tuple-element.198), channel_id=1, source_target_pairs={{0,1},{1,0},{2,3},{3,2},{4,5},{5,4},{6,7},{7,6},{8,9},{9,8},{10,11... | collective-permute-start | bytes 682760 | tf_op jit(solution)/shard_map/ppermute | solution.py:172
  489.6 11.3 %copy-start.52 = (bf16[1,8,14080]{2,1,0:T(8,128)(2,1)S(1)}, bf16[1,8,14080]{2,1,0:T(8,128)(2,1)}, u32[]{:S(2)}) copy-start(bf16[1,8,14080]{2,1,0:T(8,128)(2,1)} %reduce-scatter.5.cloned.1.call-done) | copy-start | bytes 675844
  489.6 11.3 %collective-permute-start.5 = (bf16[1,8,14080]{2,1,0:T(8,128)(2,1)}, bf16[1,8,14080]{2,1,0:T(8,128)(2,1)S(1)}, u32[]{:S(2)}, u32[]{:S(2)}) collective-permute-start(bf16[1,8,14080]{2,1,0:T(8,128)(2,1)} %reduce-scatter.5.cloned.1.call-done), channel_id=1, source_target_pairs={{0,1},{1,0},{2,3},{3,2},{4,5},{5,4},{6,7},{7,6},{8,9},{9,8},{10,11... | collective-permute-start | bytes 675848 | tf_op jit(solution)/shard_map/ppermute | solution.py:172
  675.9 4.6 collective-permute-start.4
  (89 other events, 266.9 us)
Sparse Core Ops, SparseCore 0:
  18.9 147.3 all-gather.2
  350.7 138.8 reduce-scatter.4
  496.0 179.7 reduce-scatter.6

commit v2 on v1

--- a/solution.py
+++ b/solution.py
@@ -61,8 +61,9 @@
 
 
 def attend_backward_kernel(
-    q_ref, k_ref, v_ref, out_ref, grad_ref, lse_ref, grad_mixed_ref, *, head_size, scale
+    q_ref, k_ref, v_ref, out_ref, grad_ref, lse_ref, *rest, head_size, scale
 ):
+    grad_mixed_ref = rest[-1]
     log_scale = scale * math.log2(math.e)
     for first in range(0, q_ref.shape[0], head_size):
         rows = slice(first, first + head_size)
@@ -76,14 +77,19 @@
         grad_mixed_ref[2, rows] = dot(grad, probs.astype(BF16), 1, 1).astype(BF16)
 
 
-def attend_backward(mixed_rows, out_rows, grad_rows, lse, head_count, heads_a_step):
+def attend_backward(
+    mixed_rows, out_rows, grad_rows, lse, head_count, heads_a_step, share=(0, 1), before=None
+):
     triple, length = mixed_rows.shape
     width = triple // 3
     head_size = width // head_count
-    steps = head_count // heads_a_step
+    total = head_count // heads_a_step
+    steps = total // share[1]
+    start = share[0] * steps
     slab = heads_a_step * head_size
-    part = lambda which: pl.BlockSpec((slab, length), lambda h: (which * steps + h, 0))
-    grads = pl.pallas_call(
+    part = lambda which: pl.BlockSpec((slab, length), lambda h: (which * total + start + h, 0))
+    extra = [] if before is None else [before]
+    return pl.pallas_call(
         functools.partial(attend_backward_kernel, head_size=head_size, scale=head_size**-0.5),
         grid=(steps,),
         in_specs=[
@@ -92,13 +98,14 @@
             part(2),
             part(0),
             part(0),
-            pl.BlockSpec((heads_a_step, 1, length), lambda h: (h, 0, 0)),
-        ],
-        out_specs=pl.BlockSpec((3, slab, length), lambda h: (0, h, 0)),
+            pl.BlockSpec((heads_a_step, 1, length), lambda h: (start + h, 0, 0)),
+        ]
+        + [pl.BlockSpec(memory_space=pl.ANY) for _ in extra],
+        out_specs=pl.BlockSpec((3, slab, length), lambda h: (0, start + h, 0)),
         out_shape=jax.ShapeDtypeStruct((3, width, length), BF16),
+        input_output_aliases={6: 0} if extra else {},
         compiler_params=pltpu.CompilerParams(vmem_limit_bytes=40 << 20),
-    )(mixed_rows, mixed_rows, mixed_rows, out_rows, grad_rows, lse)
-    return grads.reshape(triple, length)
+    )(mixed_rows, mixed_rows, mixed_rows, out_rows, grad_rows, lse, *extra)
 
 
 def norm_forward(rows_in, gain_row, shift_row):
@@ -139,33 +146,38 @@
     return rows_out, saved
 
 
-def block_backward(grad_out, weights, saved, head_count, heads_a_step):
-    gain_one, shift_one, w_qkv, w_out, gain_two, shift_two, w_up, w_down = weights
-    (
-        unit_one, inverse_one, normed_one, mixed_rows, lse, attn_rows,
-        unit_two, inverse_two, normed_two, upper, active,
-    ) = saved
+def mlp_backward(grad_out, weights, saved):
+    gain_two, w_out, w_up, w_down = weights[4], weights[3], weights[6], weights[7]
+    unit_two, inverse_two, upper = saved[6], saved[7], saved[9]
     grad_branch = grad_out.astype(BF16)
-    grad_down = dot(active, grad_branch, 0, 0).astype(BF16)
     grad_active = dot(grad_branch, w_down, 1, 1)
     grad_upper = jax.vjp(gelu_tanh, upper)[1](grad_active)[0].astype(BF16)
-    grad_up = dot(normed_two, grad_upper, 0, 0).astype(BF16)
-    grad_normed = dot(grad_upper, w_up, 1, 1)
-    grad_middle, grad_gain_two, grad_shift_two = norm_backward(
-        grad_normed, unit_two, inverse_two, gain_two
-    )
-    grad_middle = grad_out + grad_middle
-    grad_attn_branch = grad_middle.astype(BF16)
-    grad_wout = dot(attn_rows, grad_attn_branch, 1, 0).astype(BF16)
-    grad_attn = dot(w_out, grad_attn_branch, 1, 1).astype(BF16)
-    grad_mixed = attend_backward(mixed_rows, attn_rows, grad_attn, lse, head_count, heads_a_step)
-    grad_qkv = dot(normed_one, grad_mixed, 0, 1).astype(BF16)
-    grad_normed_one = dot(grad_mixed, w_qkv, 0, 1)
+
+    def rest(grad_upper):
+        grad_normed = dot(grad_upper, w_up, 1, 1)
+        grad_middle, grad_gain_two, grad_shift_two = norm_backward(
+            grad_normed, unit_two, inverse_two, gain_two
+        )
+        grad_middle = grad_out + grad_middle
+        grad_attn_branch = grad_middle.astype(BF16)
+        grad_attn = dot(w_out, grad_attn_branch, 1, 1).astype(BF16)
+        return grad_middle, grad_attn_branch, grad_attn, (grad_gain_two, grad_shift_two)
+
+    return grad_branch, grad_upper, rest
+
+
+def attn_backward(grad_attn, saved, head_count, heads_a_step, share=(0, 1), before=None):
+    return attend_backward(
+        saved[3], saved[5], grad_attn, saved[4], head_count, heads_a_step, share, before
+    )
+
+
+def input_backward(grad_middle, grad_mixed, weights, saved):
+    grad_normed_one = dot(grad_mixed, weights[2], 0, 1)
     grad_input, grad_gain_one, grad_shift_one = norm_backward(
-        grad_normed_one, unit_one, inverse_one, gain_one
-    )
-    vectors = (grad_gain_one, grad_shift_one, grad_gain_two, grad_shift_two)
-    return grad_middle + grad_input, vectors, (grad_qkv, grad_wout, grad_up, grad_down)
+        grad_normed_one, saved[0], saved[1], weights[0]
+    )
+    return grad_middle + grad_input, (grad_gain_one, grad_shift_one)
 
 
 def swap(array):
@@ -214,29 +226,241 @@
     return out
 
 
-def scatter_sums(grads, device_count):
+def pack_grads(grads, device_count):
     split = [g.reshape(device_count, -1, g.shape[1]) for g in grads]
     rows = 0
     for s in split:
         rows = math.gcd(rows, s.shape[1])
-    packed = jnp.concatenate([pack_rows(s, rows) for s in split], 2)
-    summed = lax.psum_scatter(packed, BOTH, scatter_dimension=0, tiled=False)
+    return jnp.concatenate([pack_rows(s, rows) for s in split], 2)
+
+
+def unpack_sums(summed, shapes):
     both = join_pair(summed[None], 0)
+    rows = both.shape[1]
     out, at = [], 0
-    for s in split:
-        span = s.shape[1] * s.shape[2] // rows
-        piece = unpack_rows(both[:, :, at : at + span], s.shape[2])
-        out.append(piece.reshape(-1, s.shape[2]).astype(F32))
+    for length, width in shapes:
+        span = length // 2 * width // rows
+        piece = unpack_rows(both[:, :, at : at + span], width)
+        out.append(piece.reshape(length, width).astype(F32))
         at += span
     return out
 
 
+def scatter_sums(grads, device_count):
+    packed = pack_grads(grads, device_count)
+    summed = lax.psum_scatter(packed, BOTH, scatter_dimension=0, tiled=False)
+    dp_count = device_count // 2
+    return unpack_sums(summed, [(g.shape[0] // dp_count, g.shape[1]) for g in grads])
+
+
 LANES = 128
-
-
-def columns(vectors):
+TILE = 16
+
+
+def columns(vectors, lanes=LANES):
     stacked = jnp.concatenate([v if v.ndim == 2 else v[:, None] for v in vectors], 1)
-    return jnp.pad(stacked, ((0, 0), (0, LANES - stacked.shape[1])))
+    return jnp.pad(stacked, ((0, 0), (0, lanes - stacked.shape[1])))
+
+
+def hop(flips):
+    return [
+        (dp * 2 + band, (dp ^ flips[band]) * 2 + band) for dp in range(16) for band in range(2)
+    ]
+
+
+FIRST_HOP = hop((2, 1))
+SECOND_HOP = hop((1, 2))
+
+
+def places(shapes):
+    out, at = [], 0
+    for rows, half in shapes:
+        out.append((rows, half, at))
+        at += rows // TILE * half
+    return out, at
+
+
+def lay(dst, src, rows, half, at):
+    for group in range(rows // TILE):
+        dst[:, at + group * half : at + (group + 1) * half] = src[group * TILE : (group + 1) * TILE]
+
+
+def products_of(jobs, spots, refs, which):
+    ins = list(refs)
+    for (left_axis, right_axis), spot in zip(jobs, spots):
+        left = None if left_axis is None else ins.pop(0)
+        right = ins.pop(0)
+        half = spot[1]
+        span = pl.ds(pl.multiple_of(which * half, 128), half)
+        values = right[span] if right_axis == 1 else right[:, span]
+        yield values if left is None else dot(left[...], values, left_axis, right_axis)
+
+
+def send_kernel(scalars, *refs, jobs, spots):
+    out = refs[-1]
+    halves = products_of(jobs, spots, refs[:-1], 1 - scalars[0])
+    for values, (rows, half, at) in zip(halves, spots):
+        values = values.astype(BF16)
+        for block in range(16):
+            lay(out.at[block], values[block * rows : (block + 1) * rows], rows, half, at)
+
+
+def keep_kernel(scalars, *refs, jobs, spots):
+    count = len(spots)
+    arrived, send, keep, landed, sem = refs[-count - 5 : -count]
+    copy = pltpu.make_async_copy(arrived, landed, sem)
+    copy.start()
+    halves = products_of(jobs, spots, refs[: -count - 5], scalars[0])
+    for values, held in zip(halves, refs[-count:]):
+        held[...] = values.astype(F32)
+    copy.wait()
+    for held, (rows, half, at) in zip(refs[-count:], spots):
+        for step in range(16):
+            block = scalars[1 + step]
+            out = (send if step < 8 else keep).at[step % 8]
+            for group in range(rows // TILE):
+                span = slice(at + group * half, at + (group + 1) * half)
+                own = held[pl.ds(pl.multiple_of(block * rows + group * TILE, TILE), TILE)]
+                out[:, span] = (own + landed[block, :, span].astype(F32)).astype(BF16)
+
+
+def split_kernel(table, own_send, own_keep, recv_send, recv_keep, send, keep):
+    send[...] = (own_send[...].astype(F32) + recv_send[...].astype(F32)).astype(BF16)
+    keep[...] = (own_keep[...].astype(F32) + recv_keep[...].astype(F32)).astype(BF16)
+
+
+def unpack_kernel(scalars, mine, theirs, *outs, spots):
+    side = scalars[0]
+    for source, which in ((mine, side), (theirs, 1 - side)):
+        for out, (rows, half, at) in zip(outs, spots):
+            for group in range(rows // TILE):
+                span = slice(at + group * half, at + (group + 1) * half)
+                lanes = pl.ds(pl.multiple_of(which * half, 128), half)
+                out[group * TILE : (group + 1) * TILE, lanes] = source[:, span].astype(F32)
+
+
+def grid_call(kernel, scalars, grid, in_specs, out_specs, out_shape, *args):
+    return pl.pallas_call(
+        kernel,
+        grid_spec=pltpu.PrefetchScalarGridSpec(
+            num_scalar_prefetch=1, grid=grid, in_specs=in_specs, out_specs=out_specs
+        ),
+        out_shape=out_shape,
+        compiler_params=pltpu.CompilerParams(vmem_limit_bytes=40 << 20),
+    )(scalars, *args)
+
+
+def vmem_call(kernel, out_shape, *args, away=0, scratch_shapes=()):
+    whole = pl.BlockSpec(memory_space=pltpu.VMEM)
+    return pl.pallas_call(
+        kernel,
+        in_specs=[pl.BlockSpec(memory_space=pltpu.SMEM)]
+        + [whole] * (len(args) - 1 - away)
+        + [pl.BlockSpec(memory_space=pl.ANY)] * away,
+        out_specs=[whole] * len(out_shape),
+        out_shape=out_shape,
+        scratch_shapes=scratch_shapes,
+        compiler_params=pltpu.CompilerParams(vmem_limit_bytes=56 << 20),
+    )(*args)
+
+
+class Bucket:
+    def __init__(self, products):
+        dp, side = lax.axis_index("dp"), lax.axis_index("band")
+        self.x, self.y, self.z, self.side = dp % 2, dp // 2 % 2, dp // 4, side
+        self.scalars = side[None].astype(jnp.int32)
+        shapes, self.jobs, self.args = [], [], []
+        for left, left_axis, right, right_axis in products:
+            length = right.shape[0] if left is None else left.shape[1 - left_axis]
+            shapes.append((length // 16, right.shape[1 - right_axis] // 2))
+            self.jobs.append((left_axis, right_axis))
+            self.args += [right] if left is None else [left, right]
+        self.spots, self.total = places(shapes)
+        (self.send,) = vmem_call(
+            functools.partial(send_kernel, jobs=self.jobs, spots=self.spots),
+            [self.shaped(16)],
+            self.scalars,
+            *self.args,
+        )
+
+    def shaped(self, count):
+        return jax.ShapeDtypeStruct((count, TILE, self.total), BF16)
+
+    def block(self, index):
+        return pl.BlockSpec((1, TILE, self.total), index)
+
+    def split(self, count, table, goes, stays):
+        goes, stays, out = self.block(goes), self.block(stays), self.block(lambda i, t: (i, 0, 0))
+        self.send, self.keep = grid_call(
+            split_kernel,
+            table.astype(jnp.int32),
+            (count,),
+            [goes, stays, goes, stays],
+            [out] * 2,
+            [self.shaped(count)] * 2,
+            self.keep,
+            self.keep,
+            self.arrived,
+            self.arrived,
+        )
+
+    def pair_hop(self):
+        self.arrived = swap(self.send)
+
+    def first_hop(self, clock):
+        self.arrived, clock = tie(self.arrived, clock)
+        line = jnp.arange(8, dtype=jnp.int32)
+        z, other = line // 2, line % 2
+        near = jnp.where(self.side == 0, self.y, self.x)
+        place = lambda bit: z * 4 + jnp.where(self.side == 0, bit * 2 + other, other * 2 + bit)
+        table = jnp.concatenate([self.side[None], place(1 - near), place(near)])
+        self.send, self.keep = vmem_call(
+            functools.partial(keep_kernel, jobs=self.jobs, spots=self.spots),
+            [self.shaped(8)] * 2,
+            table.astype(jnp.int32),
+            *self.args,
+            self.arrived,
+            away=1,
+            scratch_shapes=[pltpu.VMEM((16, TILE, self.total), BF16), pltpu.SemaphoreType.DMA(())]
+            + [pltpu.VMEM((16 * rows, half), F32) for rows, half, _ in self.spots],
+        )
+        self.arrived = lax.ppermute(self.send, BOTH, FIRST_HOP)
+        return self.send
+
+    def later_hop(self, clock, count, bit, pairs):
+        self.arrived, clock = tie(self.arrived, clock)
+        self.split(
+            count,
+            bit[None],
+            lambda i, t: (2 * i + 1 - t[0], 0, 0),
+            lambda i, t: (2 * i + t[0], 0, 0),
+        )
+        self.arrived = lax.ppermute(self.send, BOTH, pairs)
+        return self.send
+
+    def second_hop(self, clock):
+        far = jnp.where(self.side == 0, self.x, self.y)
+        return self.later_hop(clock, 4, far, SECOND_HOP)
+
+    def third_hop(self, clock):
+        return self.later_hop(clock, 2, self.z % 2, hop((4, 4)))
+
+    def fourth_hop(self, clock):
+        return self.later_hop(clock, 1, self.z // 2, hop((8, 8)))
+
+    def finish(self):
+        mine = (self.keep[0].astype(F32) + self.arrived[0].astype(F32)).astype(BF16)
+        return vmem_call(
+            functools.partial(unpack_kernel, spots=self.spots),
+            [jax.ShapeDtypeStruct((r, 2 * h), F32) for r, h, _ in self.spots],
+            self.scalars,
+            mine,
+            swap(mine),
+        )
+
+
+def tie(first, second):
+    return lax.optimization_barrier((first, second))
 
 
 def per_device(
@@ -283,15 +507,16 @@
     same_pixel = jnp.arange(pixel_size)[:, None] == jnp.arange(pixel_size)
     spread = (slot_wave[:, None, :, None] & same_pixel[None, :, None, :]).astype(BF16)
     spread = spread.reshape(chip_pixels.shape[1], wave_count * pixel_size)
-    wave_pixels = dot(chip_pixels, spread, 1, 0).astype(BF16)
+    wave_pixels = jnp.pad(dot(chip_pixels, spread, 1, 0).astype(BF16), ((2, 0), (0, 0)))
+    picks = jnp.pad(picks, (2, 0), constant_values=-1)
     band_count = jnp.sum(chip_mask).astype(F32)
 
     width = table.shape[0]
     patch_rows = dot(wave_pixels, table, 1, 1) / band_count + sincos(picks.astype(F32), width)
     loc_token = jnp.dot(time_loc, loc_rows, precision=lax.Precision.HIGHEST)
-    tokens = jnp.concatenate([enc_vec[0:1], loc_token, patch_rows], 0)
+    tokens = jnp.concatenate([enc_vec[0:1], loc_token, patch_rows[2:]], 0)
     encoded, enc_saved = block_forward(tokens, enc_weights, HEADS_ENC, HEADS_ENC)
-    latent_in = encoded[2:].astype(BF16)
+    latent_in = encoded.astype(BF16)
     latent = dot(latent_in, w_proj, 1, 0).astype(BF16)
 
     positions = jnp.arange(cotangent.shape[1], dtype=jnp.int32)
@@ -304,43 +529,109 @@
         + sincos(positions.astype(F32), latent.shape[1])
     )
     decoded, dec_saved = block_forward(inserted, dec_weights, HEADS_DEC, 1)
-    grad_inserted, dec_vec_grads, dec_grads = block_backward(
-        cotangent[0].astype(F32), dec_weights, dec_saved, HEADS_DEC, 1
-    )
+    fast = device_count == 32
+    grad_out = cotangent[0].astype(F32)
+    dec_branch, dec_upper, rest = mlp_backward(grad_out, dec_weights, dec_saved)
+    grad_middle, dec_attn_branch, grad_attn, dec_norm_two = rest(dec_upper)
+    dec_products = (
+        (dec_saved[10], 0, dec_branch, 0),
+        (dec_saved[8], 0, dec_upper, 0),
+        (dec_saved[5], 1, dec_attn_branch, 0),
+    )
+    if fast:
+        early = Bucket(dec_products)
+        grad_attn, early.send = tie(grad_attn, early.send)
+        early.pair_hop()
+        dec_mixed = attn_backward(grad_attn, dec_saved, HEADS_DEC, 1, (0, 2))
+        dec_mixed, early.send = tie(dec_mixed, early.first_hop(dec_mixed))
+        dec_mixed = attn_backward(grad_attn, dec_saved, HEADS_DEC, 1, (1, 2), dec_mixed)
+        dec_mixed, early.send = tie(dec_mixed, early.second_hop(dec_mixed))
+    else:
+        dec_mixed = attn_backward(grad_attn, dec_saved, HEADS_DEC, 1)
+    dec_mixed = dec_mixed.reshape(dec_saved[3].shape)
+    grad_inserted, dec_norm_one = input_backward(grad_middle, dec_mixed, dec_weights, dec_saved)
     grad_mask = jnp.sum(grad_inserted * hidden, 0)
+    dec_vec_grads = columns((grad_mask, *dec_norm_one, *dec_norm_two), 2 * LANES).astype(BF16)
     grad_latent = dot(matches, grad_inserted.astype(BF16), 0, 0).astype(BF16)
-    grad_proj = dot(latent_in, grad_latent, 0, 0).astype(BF16)
-    grad_rows = dot(grad_latent, w_proj, 1, 1)
-    dec_sums = scatter_sums(
-        [grad_proj, columns((grad_mask,) + dec_vec_grads).astype(BF16), *dec_grads], device_count
-    )
-
-    grad_encoded = jnp.concatenate([jnp.zeros((2, width), F32), grad_rows], 0)
-    grad_tokens, enc_vec_grads, enc_grads = block_backward(
-        grad_encoded, enc_weights, enc_saved, HEADS_ENC, HEADS_ENC
-    )
+    grad_encoded = dot(grad_latent, w_proj, 1, 1)
+
+    enc_branch, enc_upper, rest = mlp_backward(grad_encoded, enc_weights, enc_saved)
+    first_products = (
+        (enc_saved[10], 0, enc_branch, 0),
+        (enc_saved[8], 0, enc_upper, 0),
+    )
+    if fast:
+        first = Bucket(first_products)
+        enc_upper, first.send = tie(enc_upper, first.send)
+        first.pair_hop()
+    grad_middle, enc_attn_branch, grad_attn, enc_norm_two = rest(enc_upper)
+    enc_mixed = attn_backward(grad_attn, enc_saved, HEADS_ENC, HEADS_ENC)
+    enc_mixed = enc_mixed.reshape(enc_saved[3].shape)
+    second_products = (
+        (enc_saved[5], 1, enc_attn_branch, 0),
+        (enc_saved[2], 0, enc_mixed, 1),
+        (dec_saved[2], 0, dec_mixed, 1),
+        (latent_in, 0, grad_latent, 0),
+        (None, None, dec_vec_grads, 0),
+    )
+    if fast:
+        clock = first.first_hop(enc_mixed)
+        enc_mixed, _ = tie(enc_mixed, early.third_hop(clock))
+        second = Bucket(second_products)
+        second.pair_hop()
+        enc_mixed, _ = tie(enc_mixed, second.send)
+    grad_tokens, enc_norm_one = input_backward(grad_middle, enc_mixed, enc_weights, enc_saved)
     grad_loc_row = grad_tokens[1:2]
     grad_loc = jnp.dot(grad_loc_row.T, time_loc, precision=lax.Precision.HIGHEST)
     grad_time = jnp.dot(grad_loc_row, loc_rows.T, precision=lax.Precision.HIGHEST)
-    grad_raw = (grad_tokens[2:] / band_count).astype(BF16)
-    grad_table = dot(grad_raw, wave_pixels, 0, 0).astype(BF16)
-    grad_waves = dot(grad_raw, table, 1, 0).astype(BF16)
+    enc_vec_grads = columns(
+        (grad_tokens[0], *enc_norm_one, *enc_norm_two, grad_loc), 2 * LANES
+    ).astype(BF16)
+    grad_raw = (grad_tokens / band_count).astype(BF16)
+    third_products = (
+        (grad_raw, 0, wave_pixels, 0),
+        (None, None, enc_vec_grads, 0),
+    )
+    if fast:
+        third = Bucket(third_products)
+        third.pair_hop()
+        grad_raw, _ = tie(grad_raw, third.send)
+    grad_waves = dot(grad_raw[2:], table, 1, 0).astype(BF16)
     grad_chip = dot(grad_waves, spread, 1, 1).astype(BF16)
     here = grad_chip.shape[1] // 2
     mine, theirs = grad_chip[:, :here], swap(grad_chip[:, here:])
     grad_pixels = jnp.where(
         side == 0, jnp.stack([mine, theirs]), jnp.stack([theirs, mine])
     ).astype(F32)
-    enc_sums = scatter_sums(
-        [
-            grad_table,
-            columns((grad_tokens[0],) + enc_vec_grads + (grad_loc,)).astype(BF16),
-            *enc_grads,
-        ],
-        device_count,
-    )
-    s_table, s_enc_vec, s_enc_qkv, s_enc_out, s_enc_up, s_enc_down = enc_sums
-    s_proj, s_dec_vec, s_dec_qkv, s_dec_out, s_dec_up, s_dec_down = dec_sums
+    if fast:
+        clock = second.first_hop(grad_chip)
+        clock = early.fourth_hop(clock)
+        clock = first.second_hop(clock)
+        clock = third.first_hop(clock)
+        early.arrived, clock = tie(early.arrived, clock)
+        s_dec_down, s_dec_up, s_dec_out = early.finish()
+        grad_pixels, s_dec_up = tie(grad_pixels, s_dec_up)
+        clock = first.third_hop(s_dec_up)
+        clock = second.second_hop(clock)
+        clock = third.second_hop(clock)
+        clock = first.fourth_hop(clock)
+        clock = second.third_hop(clock)
+        clock = third.third_hop(clock)
+        clock = second.fourth_hop(clock)
+        clock = third.fourth_hop(clock)
+        s_enc_down, s_enc_up = first.finish()
+        second_sums = second.finish()
+        third_sums = third.finish()
+    else:
+        whole = lambda products: scatter_sums([
+            right if left is None else dot(left, right, i, j).astype(BF16)
+            for left, i, right, j in products
+        ], device_count)
+        s_dec_down, s_dec_up, s_dec_out = whole(dec_products)
+        s_enc_down, s_enc_up = whole(first_products)
+        second_sums, third_sums = whole(second_products), whole(third_products)
+    s_enc_out, s_enc_qkv, s_dec_qkv, s_proj, s_dec_vec = second_sums
+    s_table, s_enc_vec = third_sums
     return (
         decoded.astype(BF16)[None],
         grad_pixels,

time: 700 us -> 549 us (0.78)
  waiting for transfers between devices: 383 us -> 183 us
  Pallas kernels: 80.2 us -> 150 us
  matrix products: 83.5 us -> 58.9 us
  starting transfers between devices: 9.56 us -> 27.3 us
  other arithmetic: 32.5 us -> 22.6 us
    unnamed x4 -> x1, waiting for transfers between devices: 173 us -> 0.02 us
    reduce_scatter x1 -> x0, waiting for transfers between devices: 84.6 us -> none  [scatter_sums(): summed = lax.psum_scatter(packed, BOTH, scatter_dimension=0, tiled=False)]
    pallas_call x0 -> x24, Pallas kernels: none -> 69.9 us  [the longest x12 59.7 us: vmem_call(): pl.pallas_call(kernel, in_specs=[pl.BlockSpec(memory_space=pltpu.SMEM)] +...]
    ppermute x0 -> x16, waiting for transfers between devices: none -> 55.9 us  [the longest x12 43 us: later_hop(): self.arrived = lax.ppermute(self.send, BOTH, pairs)]
    dot_general x32 -> x22, matrix products: 82 us -> 56.6 us  [dot(): lax.dot_general(a, b, (((ca,), (cb,)), ((), ())), preferred_element_type=...]
    ppermute x0 -> x16, starting transfers between devices: none -> 12 us  [the longest x12 8.75 us: later_hop(): self.arrived = lax.ppermute(self.send, BOTH, pairs)]
    ppermute x6 -> x12, starting transfers between devices: 9.44 us -> 15.2 us  [swap(): return lax.ppermute(array, 'band', [(0, 1), (1, 0)])]
    unnamed x251 -> x275, local copies, waits for them, and re-layouts: 27 us -> 27.6 us
  transfers between devices with their start and end apart: 9 -> 29, of which waited for: 3 -> 10; matrix products, arithmetic and copies ran while one was open for 11% -> 9% of each run, Pallas kernels for 1% -> 16%
where the time goes in v2:
time: 549 us; the launch traced here: 543 us
  waiting for transfers between devices  183 us (33%)
  Pallas kernels  150 us (27%)
  local copies, waits for them, and re-layouts  83.4 us (15%)
  matrix products  58.9 us (11%)
  starting transfers between devices  27.3 us (5%)
  other arithmetic  22.6 us (4%)
  between operations  17.4 us (3%)
    all_gather x1, waiting for transfers between devices, gather_all(): whole = lax.all_gather(packed, BOTH, axis=0, tiled=False)  127 us
    pallas_call x12, Pallas kernels, vmem_call(): pl.pallas_call(kernel, in_specs=[pl.BlockSpec(memory_space=pltpu.SMEM)] +...  59.7 us
    dot_general x22, matrix products, dot(): lax.dot_general(a, b, (((ca,), (cb,)), ((), ())), preferred_element_type=...  56.6 us
    pallas_call x3, Pallas kernels, attend_backward(): pl.pallas_call(functools.partial(attend_backward_kernel, head_size=head_s...  49.1 us
    ppermute x12, waiting for transfers between devices, later_hop(): self.arrived = lax.ppermute(self.send, BOTH, pairs)  43 us
    pallas_call x2, Pallas kernels, attend_forward(): pl.pallas_call(functools.partial(attend_forward_kernel, head_size=head_si...  31.1 us
    slice x8, local copies, waits for them, and re-layouts, gather_all(): piece = unpack_rows(whole[:, :, at:at + span], half.shape[1])  27.8 us
    unnamed x275, local copies, waits for them, and re-layouts  27.6 us
  transfers between devices with their start and end apart: 29, of which 10 were waited for; matrix products, arithmetic and copies ran while one was open for 9% of the time, Pallas kernels for 16%

profile of v2, /device:TPU:1, one launch (start us, length us, event | category | flops | bytes accessed | tf_op | source)
XLA Modules:
  0.0 543.1 jit_solution(6178793119694384226)
XLA Ops:
  24.0 5.5 %multiply_sine_fusion = (f32[1024,256]{1,0:T(8,128)}, f32[1024,256]{1,0:T(8,128)}) fusion(f32[256]{0:T(256)S(1)} %multiply_exponential_fusion.1, f32[1024]{0:T(1024)S(1)} %iota_convert_fusion), kind=kLoop, calls=%fused_computation.47 | loop fusion | flops 262144 | bytes 2102272 | tf_op jit(solution)/shard_map/sin | solution.py:27
  32.7 4.5 and.104
  39.8 126.5 %all-gather.3.cloned.1.call-done = bf16[256,45184]{1,0:T(8,128)(2,1)} async-done(((bf16[8,45184]{1,0:T(8,128)(2,1)}), bf16[256,45184]{1,0:T(8,128)(2,1)}) %all-gather.3.cloned.1.call-update) | async-done | bytes 23134224 | tf_op jit(solution)/shard_map/all_gather | solution.py:219
  174.6 3.2 fusion.60
  177.8 4.6 slice.166
  182.4 4.7 fusion.59
  187.1 8.0 %fusion.61 = (bf16[32,8,9216]{2,1,0:T(8,128)(2,1)}, bf16[32,8,9216]{2,1,0:T(8,128)(2,1)}) fusion(bf16[32,8,45184]{2,1,0:T(8,128)(2,1)} %bitcast.258), kind=kLoop, calls=%fused_computation.215 | loop fusion | bytes 18874368 | tf_op jit(solution)/shard_map/slice | solution.py:223
  203.4 3.4 shard_map.442
  208.0 3.6 multiply_convert_fusion.1
  221.3 27.8 %shard_map.443 = (bf16[512,1024]{1,0:T(8,128)(2,1)S(1)}, f32[16,1,1024]{2,1,0:T(1,128)S(1)}) custom-call(bf16[1536,1024]{1,0:T(8,128)(2,1)S(1)} %convolution_convert_fusion.1.q_ref.k_ref.v_ref, bf16[1536,1024]{1,0:T(8,128)(2,1)S(1)} %convolution_convert_fusion.1.q_ref.k_ref.v_ref, bf16[1536,1024]{1,0:T(8,128)(2,1)S(1)} %convolution_convert_fusion.1.q_ref.k_ref.v_ref), custom_call_target="tpu_custom_call" | custom-call | tf_op jit(solution)/shard_map/pallas_call | solution.py:50
  252.8 5.3 multiply_convert_fusion
  258.1 7.4 %fusion.6.refs_3_ = bf16[1024,2048]{1,0:T(8,128)(2,1)S(1)} fusion(f32[1024,2048]{1,0:T(8,128)S(1)} %get-tuple-element.370, bf16[2048,512]{1,0:T(8,128)(2,1)S(1)} %bitcast.280, bf16[1,1024,512]{2,1,0:T(8,128)(2,1)S(1)} %copy-done.36), kind=kOutput, calls=%fused_computation.8 | convolution fusion | flops 2189426688 | bytes 15728640 | tf_op jit(solution)/shard_map/dot_general | solution.py:20
  265.5 3.4 multiply_reduce_fusion
  272.8 8.7 %shard_map.444 = bf16[16,16,4608]{2,1,0:T(8,128)(2,1)} custom-call(s32[1]{0:T(128)} %bitcast.106.scalars, bf16[1024,2048]{1,0:T(8,128)(2,1)} %get-tuple-element.369.refs_0_, bf16[1024,512]{1,0:T(8,128)(2,1)} %bitcast.259, bf16[1024,512]{1,0:T(8,128)(2,1)} %copy-done.38, bf16[1024,2048]{1,0:T(8,128)(2,1)} %copy-done.35, bf16[512,1024]{1,0:T(8,128)(2,1)} %copy-done.8, ...), custom_call_target="tpu_custom_call" | custom-call | tf_op jit(solution)/shard_map/pallas_call | solution.py:355
  285.7 22.7 %shard_map.445.rest_0_ = bf16[3,512,1024]{2,1,0:T(8,128)(2,1)S(1)} custom-call(bf16[1536,1024]{1,0:T(8,128)(2,1)S(1)} %convolution_convert_fusion.1.q_ref.k_ref.v_ref, bf16[1536,1024]{1,0:T(8,128)(2,1)S(1)} %convolution_convert_fusion.1.q_ref.k_ref.v_ref, bf16[1536,1024]{1,0:T(8,128)(2,1)S(1)} %convolution_convert_fusion.1.q_ref.k_ref.v_ref, ...), custom_call_target="tpu_custom_call" | custom-call | tf_op jit(solution)/shard_map/pallas_call | solution.py:92
  310.1 9.1 %shard_map.446 = (bf16[8,16,4608]{2,1,0:T(8,128)(2,1)}, bf16[8,16,4608]{2,1,0:T(8,128)(2,1)}) custom-call(s32[17]{0:T(128)} %pad_add_fusion.1.scalars, bf16[1024,2048]{1,0:T(8,128)(2,1)} %get-tuple-element.369.refs_0_, bf16[1024,512]{1,0:T(8,128)(2,1)} %bitcast.260, bf16[1024,512]{1,0:T(8,128)(2,1)} %copy-done.38, bf16[1024,2048]{1,0:T(8,128)(2,1)} %copy-done.35, ...), custom_call_target="tpu_custom_call" | custom-call | tf_op jit(solution)/shard_map/pallas_call | solution.py:355
  325.6 22.7 %shard_map.447 = bf16[3,512,1024]{2,1,0:T(8,128)(2,1)S(1)} custom-call(bf16[1536,1024]{1,0:T(8,128)(2,1)S(1)} %convolution_convert_fusion.1.q_ref.k_ref.v_ref, bf16[1536,1024]{1,0:T(8,128)(2,1)S(1)} %convolution_convert_fusion.1.q_ref.k_ref.v_ref, bf16[1536,1024]{1,0:T(8,128)(2,1)S(1)} %convolution_convert_fusion.1.q_ref.k_ref.v_ref, ...), custom_call_target="tpu_custom_call", output_to_operand_aliasing={{}: (6, {})} | custom-call | tf_op jit(solution)/shard_map/pallas_call | solution.py:92
  359.7 4.1 fusion.16.refs_3_
  363.9 6.1 %shard_map.449 = bf16[16,16,9216]{2,1,0:T(8,128)(2,1)} custom-call(s32[1]{0:T(128)} %bitcast.106.scalars, bf16[256,3072]{1,0:T(8,128)(2,1)} %copy-done.45, bf16[256,768]{1,0:T(8,128)(2,1)} %copy-done.50, bf16[256,768]{1,0:T(8,128)(2,1)} %copy-done.49, bf16[256,3072]{1,0:T(8,128)(2,1)} %fusion.16.refs_3_), custom_call_target="tpu_custom_call" | custom-call | tf_op jit(solution)/shard_map/pallas_call | solution.py:355
  371.6 4.1 multiply_reduce_fusion.9
  377.5 3.6 shard_map.450
  382.2 6.8 %shard_map.453 = bf16[16,16,7168]{2,1,0:T(8,128)(2,1)} custom-call(s32[1]{0:T(128)} %bitcast.106.scalars, bf16[768,256]{1,0:T(8,128)(2,1)} %copy-done.18, bf16[256,768]{1,0:T(8,128)(2,1)} %copy-done.47, bf16[256,768]{1,0:T(8,128)(2,1)} %copy-done.48, bf16[2304,256]{1,0:T(8,128)(2,1)} %bitcast.247, bf16[1024,512]{1,0:T(8,128)(2,1)} %copy-done.39, ...), custom_call_target="tpu_custom_call" | custom-call | tf_op jit(solution)/shard_map/pallas_call | solution.py:355
  390.4 7.5 %shard_map.451 = (bf16[8,16,9216]{2,1,0:T(8,128)(2,1)}, bf16[8,16,9216]{2,1,0:T(8,128)(2,1)}) custom-call(s32[17]{0:T(128)} %pad_add_fusion.1.scalars, bf16[256,3072]{1,0:T(8,128)(2,1)} %copy-done.45, bf16[256,768]{1,0:T(8,128)(2,1)} %copy-done.50, bf16[256,768]{1,0:T(8,128)(2,1)} %copy-done.49, bf16[256,3072]{1,0:T(8,128)(2,1)} %fusion.16.refs_3_, ...), custom_call_target="tpu_custom_call" | custom-call | tf_op jit(solution)/shard_map/pallas_call | solution.py:355
  399.8 3.4 multiply_reduce_fusion.10
  413.3 7.8 %shard_map.455 = (bf16[8,16,7168]{2,1,0:T(8,128)(2,1)}, bf16[8,16,7168]{2,1,0:T(8,128)(2,1)}) custom-call(s32[17]{0:T(128)} %pad_add_fusion.1.scalars, bf16[768,256]{1,0:T(8,128)(2,1)} %copy-done.18, bf16[256,768]{1,0:T(8,128)(2,1)} %copy-done.47, bf16[256,768]{1,0:T(8,128)(2,1)} %copy-done.48, bf16[2304,256]{1,0:T(8,128)(2,1)} %bitcast.248, ...), custom_call_target="tpu_custom_call" | custom-call | tf_op jit(solution)/shard_map/pallas_call | solution.py:355
  421.6 8.5 %collective-permute-done.8.recv_send.recv_keep = bf16[2,16,4608]{2,1,0:T(8,128)(2,1)S(1)} collective-permute-done((bf16[2,16,4608]{2,1,0:T(8,128)(2,1)S(1)}, bf16[2,16,4608]{2,1,0:T(8,128)(2,1)S(1)}, u32[]{:S(2)}, u32[]{:S(2)}) %collective-permute-start.8) | collective-permute-done | bytes 294944 | tf_op jit(solution)/shard_map/ppermute | solution.py:438
  437.7 3.6 shard_map.458
  445.3 14.1 %collective-permute-done.16.recv_send.recv_keep = bf16[4,16,9216]{2,1,0:T(8,128)(2,1)S(1)} collective-permute-done((bf16[4,16,9216]{2,1,0:T(8,128)(2,1)S(1)}, bf16[4,16,9216]{2,1,0:T(8,128)(2,1)S(1)}, u32[]{:S(2)}, u32[]{:S(2)}) %collective-permute-start.16) | collective-permute-done | bytes 1179680 | tf_op jit(solution)/shard_map/ppermute | solution.py:438
  465.2 13.0 %collective-permute-done.14.recv_send.recv_keep = bf16[8,16,1920]{2,1,0:T(8,128)(2,1)S(1)} collective-permute-done((bf16[8,16,1920]{2,1,0:T(8,128)(2,1)S(1)}, bf16[8,16,1920]{2,1,0:T(8,128)(2,1)S(1)}, u32[]{:S(2)}, u32[]{:S(2)}) %collective-permute-start.14) | collective-permute-done | bytes 491552 | tf_op jit(solution)/shard_map/ppermute | solution.py:427
  484.5 3.3 fusion.17
  487.8 11.1 %collective-permute-done.21.recv_send.recv_keep = bf16[2,16,7168]{2,1,0:T(8,128)(2,1)S(1)} collective-permute-done((bf16[2,16,7168]{2,1,0:T(8,128)(2,1)S(1)}, bf16[2,16,7168]{2,1,0:T(8,128)(2,1)S(1)}, u32[]{:S(2)}, u32[]{:S(2)}) %collective-permute-start.21) | collective-permute-done | bytes 458784 | tf_op jit(solution)/shard_map/ppermute | solution.py:438
  506.6 8.1 %collective-permute-start.23 = (bf16[16,1920]{1,0:T(8,128)(2,1)S(1)}, bf16[16,1920]{1,0:T(8,128)(2,1)S(1)}, u32[]{:S(2)}, u32[]{:S(2)}) collective-permute-start(bf16[16,1920]{1,0:T(8,128)(2,1)S(1)} %fusion.33.mine), channel_id=1, source_target_pairs={{0,1},{1,0},{2,3},{3,2},{4,5},{5,4},{6,7},{7,6},{8,9},{9,8},{10,11... | collective-permute-start | bytes 184328 | tf_op jit(solution)/shard_map/ppermute | solution.py:184
  (466 shorter events, 149.5 us)
Async XLA Ops:
  7.2 159.1 %all-gather.3.cloned.1.call-start = ((), (), s32[]{:S(2)}) async-start(), calls=%async_computation | async-start | bytes 23857152 | tf_op jit(solution)/shard_map/all_gather | solution.py:219
  19.4 10.1 %collective-permute-start.2 = (s32[7]{0:T(128)S(1)}, s32[7]{0:T(128)S(1)}, u32[]{:S(2)}, u32[]{:S(2)}) collective-permute-start(s32[7]{0:T(128)S(1)} %get-tuple-element.357), channel_id=1, source_target_pairs={{0,1},{1,0},{2,3},{3,2},{4,5},{5,4},{6,7},{7,6},{8,9},{9,8},{10,11... | collective-permute-start | bytes 92 | tf_op jit(solution)/shard_map/ppermute | solution.py:184
  19.5 12.0 %collective-permute-start.1 = (s32[7]{0:T(128)S(1)}, s32[7]{0:T(128)S(1)}, u32[]{:S(2)}, u32[]{:S(2)}) collective-permute-start(s32[7]{0:T(128)S(1)} %get-tuple-element.360), channel_id=1, source_target_pairs={{0,1},{1,0},{2,3},{3,2},{4,5},{5,4},{6,7},{7,6},{8,9},{9,8},{10,11... | collective-permute-start | bytes 92 | tf_op jit(solution)/shard_map/ppermute | solution.py:184
  20.7 16.5 %collective-permute-start = (bf16[254,448]{0,1:T(8,128)(2,1)S(1)}, bf16[254,448]{0,1:T(8,128)(2,1)S(1)}, u32[]{:S(2)}, u32[]{:S(2)}) collective-permute-start(bf16[254,448]{0,1:T(8,128)(2,1)S(1)} %get-tuple-element.348), channel_id=1, source_target_pairs={{0,1},{1,0},{2,3},{3,2},{4,5},{5,4},{6,7},{7,6},{8,9},{9,8},{10,11... | collective-permute-start | bytes 682760 | tf_op jit(solution)/shard_map/ppermute | solution.py:184
  37.2 131.7 %copy-start.72 = (pred[896,1024]{1,0:T(32,128)(4,1)}, pred[896,1024]{1,0:T(32,128)(4,1)S(1)}, u32[]{:S(2)}) copy-start(pred[896,1024]{1,0:T(32,128)(4,1)S(1)} %and.104) | copy-start | bytes 2752516
  39.8 159.4 %copy-start.62 = (bf16[254,1024]{1,0:T(8,128)(2,1)}, bf16[254,1024]{1,0:T(8,128)(2,1)S(1)}, u32[]{:S(2)}) copy-start(bf16[254,1024]{1,0:T(8,128)(2,1)S(1)} %convolution_convert_fusion.3) | copy-start | bytes 1560580
  206.8 170.6 %copy-start.18 = (bf16[768,256]{1,0:T(8,128)(2,1)}, bf16[768,256]{1,0:T(8,128)(2,1)S(1)}, u32[]{:S(2)}) copy-start(bf16[768,256]{1,0:T(8,128)(2,1)S(1)} %get-tuple-element.100.out_ref.refs_0_) | copy-start | bytes 1179652
  281.5 28.6 %collective-permute-start.3 = (bf16[16,16,4608]{2,1,0:T(8,128)(2,1)}, bf16[16,16,4608]{2,1,0:T(8,128)(2,1)}, u32[]{:S(2)}, u32[]{:S(2)}) collective-permute-start(bf16[16,16,4608]{2,1,0:T(8,128)(2,1)} %shard_map.444), channel_id=1, source_target_pairs={{0,1},{1,0},{2,3},{3,2},{4,5},{5,4},{6,7},{7,6},{8,9},{9,8},{10,11... | collective-permute-start | bytes 7077896 | tf_op jit(solution)/shard_map/ppermute | solution.py:184
  319.2 30.8 %collective-permute-start.4 = (bf16[8,16,4608]{2,1,0:T(8,128)(2,1)}, bf16[8,16,4608]{2,1,0:T(8,128)(2,1)}, u32[]{:S(2)}, u32[]{:S(2)}) collective-permute-start(bf16[8,16,4608]{2,1,0:T(8,128)(2,1)} %get-tuple-element.106), channel_id=1, source_target_pairs={{0,4},{1,3},{2,6},{3,1},{4,0},{5,7},{6,2},{7,5},{8,12},{9,11},{10,... | collective-permute-start | bytes 3538952 | tf_op jit(solution)/shard_map/ppermute | solution.py:427
  369.9 20.4 %collective-permute-start.6 = (bf16[16,16,9216]{2,1,0:T(8,128)(2,1)}, bf16[16,16,9216]{2,1,0:T(8,128)(2,1)}, u32[]{:S(2)}, u32[]{:S(2)}) collective-permute-start(bf16[16,16,9216]{2,1,0:T(8,128)(2,1)} %shard_map.449), channel_id=1, source_target_pairs={{0,1},{1,0},{2,3},{3,2},{4,5},{5,4},{6,7},{7,6},{8,9},{9,8},{10,11... | collective-permute-start | bytes 14155784 | tf_op jit(solution)/shard_map/ppermute | solution.py:184
  389.1 24.2 %collective-permute-start.9 = (bf16[16,16,7168]{2,1,0:T(8,128)(2,1)}, bf16[16,16,7168]{2,1,0:T(8,128)(2,1)}, u32[]{:S(2)}, u32[]{:S(2)}) collective-permute-start(bf16[16,16,7168]{2,1,0:T(8,128)(2,1)} %shard_map.453), channel_id=1, source_target_pairs={{0,1},{1,0},{2,3},{3,2},{4,5},{5,4},{6,7},{7,6},{8,9},{9,8},{10,11... | collective-permute-start | bytes 11010056 | tf_op jit(solution)/shard_map/ppermute | solution.py:184
  389.1 10.1 %collective-permute-start.5 = (bf16[4,16,4608]{2,1,0:T(8,128)(2,1)S(1)}, bf16[4,16,4608]{2,1,0:T(8,128)(2,1)S(1)}, u32[]{:S(2)}, u32[]{:S(2)}) collective-permute-start(bf16[4,16,4608]{2,1,0:T(8,128)(2,1)S(1)} %copy-done.26), channel_id=1, source_target_pairs={{0,2},{1,5},{2,0},{3,7},{4,6},{5,1},{6,4},{7,3},{8,10},{9,13},{10,... | collective-permute-start | bytes 1769480 | tf_op jit(solution)/shard_map/ppermute | solution.py:438
  398.0 36.0 %collective-permute-start.12 = (bf16[8,16,9216]{2,1,0:T(8,128)(2,1)}, bf16[8,16,9216]{2,1,0:T(8,128)(2,1)}, u32[]{:S(2)}, u32[]{:S(2)}) collective-permute-start(bf16[8,16,9216]{2,1,0:T(8,128)(2,1)} %get-tuple-element.117), channel_id=1, source_target_pairs={{0,4},{1,3},{2,6},{3,1},{4,0},{5,7},{6,2},{7,5},{8,12},{9,11},{10,... | collective-permute-start | bytes 7077896 | tf_op jit(solution)/shard_map/ppermute | solution.py:427
  409.2 28.5 %collective-permute-start.11 = (bf16[16,16,1920]{2,1,0:T(8,128)(2,1)}, bf16[16,16,1920]{2,1,0:T(8,128)(2,1)}, u32[]{:S(2)}, u32[]{:S(2)}) collective-permute-start(bf16[16,16,1920]{2,1,0:T(8,128)(2,1)} %shard_map.454), channel_id=1, source_target_pairs={{0,1},{1,0},{2,3},{3,2},{4,5},{5,4},{6,7},{7,6},{8,9},{9,8},{10,11... | collective-permute-start | bytes 2949128 | tf_op jit(solution)/shard_map/ppermute | solution.py:184
  421.1 38.7 %collective-permute-start.15 = (bf16[8,16,7168]{2,1,0:T(8,128)(2,1)}, bf16[8,16,7168]{2,1,0:T(8,128)(2,1)}, u32[]{:S(2)}, u32[]{:S(2)}) collective-permute-start(bf16[8,16,7168]{2,1,0:T(8,128)(2,1)} %get-tuple-element.125), channel_id=1, source_target_pairs={{0,4},{1,3},{2,6},{3,1},{4,0},{5,7},{6,2},{7,5},{8,12},{9,11},{10,... | collective-permute-start | bytes 5505032 | tf_op jit(solution)/shard_map/ppermute | solution.py:427
  421.6 8.5 %collective-permute-start.8 = (bf16[2,16,4608]{2,1,0:T(8,128)(2,1)S(1)}, bf16[2,16,4608]{2,1,0:T(8,128)(2,1)S(1)}, u32[]{:S(2)}, u32[]{:S(2)}) collective-permute-start(bf16[2,16,4608]{2,1,0:T(8,128)(2,1)S(1)} %get-tuple-element.119), channel_id=1, source_target_pairs={{0,8},{1,9},{2,10},{3,11},{4,12},{5,13},{6,14},{7,15},{8,0},{9,1},... | collective-permute-start | bytes 884744 | tf_op jit(solution)/shard_map/ppermute | solution.py:438
  430.2 11.1 %collective-permute-start.10 = (bf16[1,16,4608]{2,1,0:T(8,128)(2,1)S(1)}, bf16[1,16,4608]{2,1,0:T(8,128)(2,1)S(1)}, u32[]{:S(2)}, u32[]{:S(2)}) collective-permute-start(bf16[1,16,4608]{2,1,0:T(8,128)(2,1)S(1)} %get-tuple-element.128), channel_id=1, source_target_pairs={{0,16},{1,17},{2,18},{3,19},{4,20},{5,21},{6,22},{7,23},{8,24},{9,... | collective-permute-start | bytes 442376 | tf_op jit(solution)/shard_map/ppermute | solution.py:438
  432.6 9.1 %collective-permute-start.7 = (bf16[254,448]{1,0:T(8,128)(2,1)S(1)}, bf16[254,448]{1,0:T(8,128)(2,1)S(1)}, u32[]{:S(2)}, u32[]{:S(2)}) collective-permute-start(bf16[254,448]{1,0:T(8,128)(2,1)S(1)} %get-tuple-element.346), channel_id=1, source_target_pairs={{0,1},{1,0},{2,3},{3,2},{4,5},{5,4},{6,7},{7,6},{8,9},{9,8},{10,11... | collective-permute-start | bytes 682760 | tf_op jit(solution)/shard_map/ppermute | solution.py:184
  436.6 22.8 %collective-permute-start.16 = (bf16[4,16,9216]{2,1,0:T(8,128)(2,1)S(1)}, bf16[4,16,9216]{2,1,0:T(8,128)(2,1)S(1)}, u32[]{:S(2)}, u32[]{:S(2)}) collective-permute-start(bf16[4,16,9216]{2,1,0:T(8,128)(2,1)S(1)} %get-tuple-element.131), channel_id=1, source_target_pairs={{0,2},{1,5},{2,0},{3,7},{4,6},{5,1},{6,4},{7,3},{8,10},{9,13},{10,... | collective-permute-start | bytes 3538952 | tf_op jit(solution)/shard_map/ppermute | solution.py:438
  441.4 1.4 collective-permute-start.13
  463.6 17.8 %collective-permute-start.18 = (bf16[4,16,7168]{2,1,0:T(8,128)(2,1)S(1)}, bf16[4,16,7168]{2,1,0:T(8,128)(2,1)S(1)}, u32[]{:S(2)}, u32[]{:S(2)}) collective-permute-start(bf16[4,16,7168]{2,1,0:T(8,128)(2,1)S(1)} %get-tuple-element.144), channel_id=1, source_target_pairs={{0,2},{1,5},{2,0},{3,7},{4,6},{5,1},{6,4},{7,3},{8,10},{9,13},{10,... | collective-permute-start | bytes 2752520 | tf_op jit(solution)/shard_map/ppermute | solution.py:438
  464.9 13.3 %collective-permute-start.14 = (bf16[8,16,1920]{2,1,0:T(8,128)(2,1)S(1)}, bf16[8,16,1920]{2,1,0:T(8,128)(2,1)S(1)}, u32[]{:S(2)}, u32[]{:S(2)}) collective-permute-start(bf16[8,16,1920]{2,1,0:T(8,128)(2,1)S(1)} %copy-done.122), channel_id=1, source_target_pairs={{0,4},{1,3},{2,6},{3,1},{4,0},{5,7},{6,2},{7,5},{8,12},{9,11},{10,... | collective-permute-start | bytes 1474568 | tf_op jit(solution)/shard_map/ppermute | solution.py:427
  465.2 14.9 %collective-permute-start.19 = (bf16[2,16,9216]{2,1,0:T(8,128)(2,1)S(1)}, bf16[2,16,9216]{2,1,0:T(8,128)(2,1)S(1)}, u32[]{:S(2)}, u32[]{:S(2)}) collective-permute-start(bf16[2,16,9216]{2,1,0:T(8,128)(2,1)S(1)} %get-tuple-element.142), channel_id=1, source_target_pairs={{0,8},{1,9},{2,10},{3,11},{4,12},{5,13},{6,14},{7,15},{8,0},{9,1},... | collective-permute-start | bytes 1769480 | tf_op jit(solution)/shard_map/ppermute | solution.py:438
  478.3 5.8 %collective-permute-start.17 = (bf16[4,16,1920]{2,1,0:T(8,128)(2,1)S(1)}, bf16[4,16,1920]{2,1,0:T(8,128)(2,1)S(1)}, u32[]{:S(2)}, u32[]{:S(2)}) collective-permute-start(bf16[4,16,1920]{2,1,0:T(8,128)(2,1)S(1)} %get-tuple-element.147), channel_id=1, source_target_pairs={{0,2},{1,5},{2,0},{3,7},{4,6},{5,1},{6,4},{7,3},{8,10},{9,13},{10,... | collective-permute-start | bytes 737288 | tf_op jit(solution)/shard_map/ppermute | solution.py:438
  480.2 21.7 %collective-permute-start.26 = (bf16[1,16,9216]{2,1,0:T(8,128)(2,1)S(1)}, bf16[1,16,9216]{2,1,0:T(8,128)(2,1)S(1)}, u32[]{:S(2)}, u32[]{:S(2)}) collective-permute-start(bf16[1,16,9216]{2,1,0:T(8,128)(2,1)S(1)} %get-tuple-element.151), channel_id=1, source_target_pairs={{0,16},{1,17},{2,18},{3,19},{4,20},{5,21},{6,22},{7,23},{8,24},{9,... | collective-permute-start | bytes 884744 | tf_op jit(solution)/shard_map/ppermute | solution.py:438
  481.7 17.2 %collective-permute-start.21 = (bf16[2,16,7168]{2,1,0:T(8,128)(2,1)S(1)}, bf16[2,16,7168]{2,1,0:T(8,128)(2,1)S(1)}, u32[]{:S(2)}, u32[]{:S(2)}) collective-permute-start(bf16[2,16,7168]{2,1,0:T(8,128)(2,1)S(1)} %get-tuple-element.153), channel_id=1, source_target_pairs={{0,8},{1,9},{2,10},{3,11},{4,12},{5,13},{6,14},{7,15},{8,0},{9,1},... | collective-permute-start | bytes 1376264 | tf_op jit(solution)/shard_map/ppermute | solution.py:438
  484.4 17.2 %collective-permute-start.20 = (bf16[2,16,1920]{2,1,0:T(8,128)(2,1)S(1)}, bf16[2,16,1920]{2,1,0:T(8,128)(2,1)S(1)}, u32[]{:S(2)}, u32[]{:S(2)}) collective-permute-start(bf16[2,16,1920]{2,1,0:T(8,128)(2,1)S(1)} %get-tuple-element.156), channel_id=1, source_target_pairs={{0,8},{1,9},{2,10},{3,11},{4,12},{5,13},{6,14},{7,15},{8,0},{9,1},... | collective-permute-start | bytes 368648 | tf_op jit(solution)/shard_map/ppermute | solution.py:438
  501.6 4.9 collective-permute-start.22
  502.0 19.7 %collective-permute-start.27 = (bf16[16,9216]{1,0:T(8,128)(2,1)S(1)}, bf16[16,9216]{1,0:T(8,128)(2,1)S(1)}, u32[]{:S(2)}, u32[]{:S(2)}) collective-permute-start(bf16[16,9216]{1,0:T(8,128)(2,1)S(1)} %fusion.29.mine), channel_id=1, source_target_pairs={{0,1},{1,0},{2,3},{3,2},{4,5},{5,4},{6,7},{7,6},{8,9},{9,8},{10,11... | collective-permute-start | bytes 884744 | tf_op jit(solution)/shard_map/ppermute | solution.py:184
  503.9 13.9 %collective-permute-start.24 = (bf16[1,16,7168]{2,1,0:T(8,128)(2,1)S(1)}, bf16[1,16,7168]{2,1,0:T(8,128)(2,1)S(1)}, u32[]{:S(2)}, u32[]{:S(2)}) collective-permute-start(bf16[1,16,7168]{2,1,0:T(8,128)(2,1)S(1)} %get-tuple-element.159), channel_id=1, source_target_pairs={{0,16},{1,17},{2,18},{3,19},{4,20},{5,21},{6,22},{7,23},{8,24},{9,... | collective-permute-start | bytes 688136 | tf_op jit(solution)/shard_map/ppermute | solution.py:438
  506.6 17.9 %collective-permute-start.23 = (bf16[16,1920]{1,0:T(8,128)(2,1)S(1)}, bf16[16,1920]{1,0:T(8,128)(2,1)S(1)}, u32[]{:S(2)}, u32[]{:S(2)}) collective-permute-start(bf16[16,1920]{1,0:T(8,128)(2,1)S(1)} %fusion.33.mine), channel_id=1, source_target_pairs={{0,1},{1,0},{2,3},{3,2},{4,5},{5,4},{6,7},{7,6},{8,9},{9,8},{10,11... | collective-permute-start | bytes 184328 | tf_op jit(solution)/shard_map/ppermute | solution.py:184
  517.8 13.8 %collective-permute-start.25 = (bf16[16,7168]{1,0:T(8,128)(2,1)S(1)}, bf16[16,7168]{1,0:T(8,128)(2,1)S(1)}, u32[]{:S(2)}, u32[]{:S(2)}) collective-permute-start(bf16[16,7168]{1,0:T(8,128)(2,1)S(1)} %fusion.30.mine), channel_id=1, source_target_pairs={{0,1},{1,0},{2,3},{3,2},{4,5},{5,4},{6,7},{7,6},{8,9},{9,8},{10,11... | collective-permute-start | bytes 688136 | tf_op jit(solution)/shard_map/ppermute | solution.py:184
  (128 other events, 750.6 us)
Sparse Core Ops, SparseCore 0:
  18.9 147.4 all-gather.2

commit v3 on v2

--- a/solution.py
+++ b/solution.py
@@ -129,21 +129,20 @@
     return jax.nn.gelu(upper, approximate=True)
 
 
-def block_forward(rows_in, weights, head_count, heads_a_step):
-    gain_one, shift_one, w_qkv, w_out, gain_two, shift_two, w_up, w_down = weights
+def attn_half(rows_in, gain_one, shift_one, w_qkv, w_out, head_count, heads_a_step):
     normed_one, unit_one, inverse_one = norm_forward(rows_in, gain_one, shift_one)
     mixed_rows = dot(w_qkv, normed_one, 0, 1).astype(BF16)
     attn_rows, lse = attend_forward(mixed_rows, head_count, heads_a_step)
     middle = rows_in + dot(attn_rows, w_out, 0, 0)
+    return middle, (unit_one, inverse_one, normed_one, mixed_rows, lse, attn_rows)
+
+
+def mlp_half(middle, saved, gain_two, shift_two, w_up, w_down):
     normed_two, unit_two, inverse_two = norm_forward(middle, gain_two, shift_two)
     upper = dot(normed_two, w_up, 1, 0)
     active = gelu_tanh(upper).astype(BF16)
     rows_out = middle + dot(active, w_down, 1, 0)
-    saved = (
-        unit_one, inverse_one, normed_one, mixed_rows, lse, attn_rows,
-        unit_two, inverse_two, normed_two, upper, active,
-    )
-    return rows_out, saved
+    return rows_out, saved + (unit_two, inverse_two, normed_two, upper, active)
 
 
 def mlp_backward(grad_out, weights, saved):
@@ -364,6 +363,99 @@
     )(*args)
 
 
+def assemble_kernel(scalars, *refs, spots):
+    pieces, outs, sem = refs[:8], refs[8:-1], refs[-1]
+    copies = []
+    for index, piece in enumerate(pieces):
+        line = scalars[1 + index]
+        side = scalars[0] if index < 4 else 1 - scalars[0]
+        for which, rows, first, half, at in spots:
+            lanes = pl.ds(pl.multiple_of(side * half, 128), half)
+            copies.append(
+                pltpu.make_async_copy(
+                    piece.at[:, :, at : at + half],
+                    outs[which].at[:, line, first : first + rows, lanes],
+                    sem,
+                )
+            )
+    for copy in copies:
+        copy.start()
+    for copy in copies:
+        copy.wait()
+
+
+class Gather:
+    def __init__(self, shards, rows):
+        dp, side = lax.axis_index("dp"), lax.axis_index("band")
+        self.x, self.y, self.z, self.side = dp % 2, dp // 2 % 2, dp // 4, side
+        self.shapes, self.spots, parts, at = [], [], [], 0
+        for which, shard in enumerate(shards):
+            length, width = shard.shape
+            half = width // 2
+            mine = lax.dynamic_slice_in_dim(shard, side * half, half, 1)
+            for first in range(0, length, rows):
+                parts.append(mine[first : first + rows])
+                self.spots.append((which, rows, first, half, at))
+                at += half
+            self.shapes.append((4, 4, length, width))
+        self.one = jnp.concatenate(parts, 1)
+
+    def far_line(self):
+        self.arrived = lax.ppermute(self.one, BOTH, hop((8, 8)))
+        return self.one
+
+    def near_line(self, clock):
+        self.arrived, clock = tie(self.arrived, clock)
+        low = self.z < 2
+        self.two = jnp.stack(
+            [jnp.where(low, self.one, self.arrived), jnp.where(low, self.arrived, self.one)]
+        )
+        self.arrived = lax.ppermute(self.two, BOTH, hop((4, 4)))
+        return self.two
+
+    def plane(self, clock):
+        self.arrived, clock = tie(self.arrived, clock)
+        even = self.z % 2 == 0
+        four = jnp.stack(
+            [jnp.where(even, self.two, self.arrived), jnp.where(even, self.arrived, self.two)], 1
+        )
+        own = four.reshape(4, *self.one.shape)
+        self.pieces = [own, lax.ppermute(own, BOTH, SECOND_HOP), lax.ppermute(own, BOTH, FIRST_HOP)]
+        self.partner = [swap(own)]
+        return own
+
+    def corner(self, clock):
+        self.pieces[1], clock = tie(self.pieces[1], clock)
+        self.pieces.append(lax.ppermute(self.pieces[1], BOTH, FIRST_HOP))
+        self.partner.append(swap(self.pieces[1]))
+        return self.pieces[1]
+
+    def pair(self, clock):
+        self.pieces[2:], clock = tie(self.pieces[2:], clock)
+        self.partner += [swap(piece) for piece in self.pieces[2:]]
+        return self.pieces[3]
+
+    def weights(self):
+        place = lambda x, y: y * 2 + x
+        here, across, corner = (
+            place(self.x, self.y), place(1 - self.x, self.y), place(1 - self.x, 1 - self.y)
+        )
+        along = place(self.x, 1 - self.y)
+        first = self.side == 0
+        one, two = jnp.where(first, across, along), jnp.where(first, along, across)
+        table = jnp.stack([self.side, here, one, two, corner, here, two, one, corner])
+        outs = vmem_call(
+            functools.partial(assemble_kernel, spots=self.spots),
+            [jax.ShapeDtypeStruct(shape, BF16) for shape in self.shapes],
+            table.astype(jnp.int32),
+            *self.pieces,
+            *self.partner,
+            away=8,
+            scratch_shapes=[pltpu.SemaphoreType.DMA(())],
+        )
+        return [out.reshape(-1, out.shape[3]) for out in outs]
+
+
 class Bucket:
     def __init__(self, products):
         dp, side = lax.axis_index("dp"), lax.axis_index("band")
@@ -472,25 +564,39 @@
     side = lax.axis_index("band")
     table_rows = band_table.shape[0]
     wave_count, pixel_size = band_table.shape[1:]
-    (
-        table, enc_vectors, w_enc_qkv, w_enc_out, w_enc_up, w_enc_down, w_proj,
-        dec_vectors, w_dec_qkv, w_dec_out, w_dec_up, w_dec_down,
-    ) = gather_all([
-        band_table.reshape(table_rows, -1),
-        columns([cls_token, enc_attn_gain, enc_attn_shift, enc_mlp_gain, enc_mlp_shift, loc_weight]),
-        enc_qkv, enc_out, enc_up, enc_down, projection,
-        columns([mask_token, dec_attn_gain, dec_attn_shift, dec_mlp_gain, dec_mlp_shift]),
-        dec_qkv, dec_out, dec_up, dec_down,
-    ])
+    fast = device_count == 32
+    enc_vectors = columns(
+        [cls_token, enc_attn_gain, enc_attn_shift, enc_mlp_gain, enc_mlp_shift, loc_weight], 2 * LANES
+    )
+    dec_vectors = columns(
+        [mask_token, dec_attn_gain, dec_attn_shift, dec_mlp_gain, dec_mlp_shift], 2 * LANES
+    )
+    shards = (
+        [band_table.reshape(table_rows, -1), enc_vectors, enc_qkv, enc_out],
+        [enc_up, enc_down, projection],
+        [dec_vectors, dec_qkv, dec_out, dec_up, dec_down],
+    )
+    if fast:
+        front, middle, back = (Gather(group, group[0].shape[0]) for group in shards)
+        clock = front.far_line()
+        clock = front.near_line(clock)
+        middle.one, clock = tie(middle.one, clock)
+        clock = middle.far_line()
+        clock = front.plane(clock)
+        clock = middle.near_line(clock)
+        back.one, clock = tie(back.one, clock)
+        clock = back.far_line()
+        clock = front.corner(clock)
+        clock = middle.plane(clock)
+        clock = back.near_line(clock)
+        clock = front.pair(clock)
+        groups = [front.weights()]
+    else:
+        weights = gather_all([shard for group in shards for shard in group])
+        groups = [weights[:4], weights[4:7], weights[7:]]
+    table, enc_vectors, w_enc_qkv, w_enc_out = groups[0]
     enc_vec = enc_vectors.T.astype(F32)
-    dec_vec = dec_vectors.T.astype(F32)
     loc_rows = enc_vec[5 : 5 + loc_weight.shape[1]]
-    enc_weights = (
-        enc_vec[1], enc_vec[2], w_enc_qkv, w_enc_out, enc_vec[3], enc_vec[4], w_enc_up, w_enc_down
-    )
-    dec_weights = (
-        dec_vec[1], dec_vec[2], w_dec_qkv, w_dec_out, dec_vec[3], dec_vec[4], w_dec_up, w_dec_down
-    )
 
     def own_chip(array):
         mine = lax.dynamic_index_in_dim(array, side, 0, keepdims=False)
@@ -515,10 +621,33 @@
     patch_rows = dot(wave_pixels, table, 1, 1) / band_count + sincos(picks.astype(F32), width)
     loc_token = jnp.dot(time_loc, loc_rows, precision=lax.Precision.HIGHEST)
     tokens = jnp.concatenate([enc_vec[0:1], loc_token, patch_rows[2:]], 0)
-    encoded, enc_saved = block_forward(tokens, enc_weights, HEADS_ENC, HEADS_ENC)
+    enc_half, enc_saved = attn_half(
+        tokens, enc_vec[1], enc_vec[2], w_enc_qkv, w_enc_out, HEADS_ENC, HEADS_ENC
+    )
+    if fast:
+        clock, enc_half = tie(clock, enc_half)
+        clock = middle.corner(clock)
+        clock = back.plane(clock)
+        clock = middle.pair(clock)
+        groups.append(middle.weights())
+    w_enc_up, w_enc_down, w_proj = groups[1]
+    enc_weights = (
+        enc_vec[1], enc_vec[2], w_enc_qkv, w_enc_out, enc_vec[3], enc_vec[4], w_enc_up, w_enc_down
+    )
+    encoded, enc_saved = mlp_half(enc_half, enc_saved, *enc_weights[4:])
     latent_in = encoded.astype(BF16)
     latent = dot(latent_in, w_proj, 1, 0).astype(BF16)
 
+    if fast:
+        clock, latent = tie(clock, latent)
+        clock = back.corner(clock)
+        clock = back.pair(clock)
+        groups.append(back.weights())
+    dec_vectors, w_dec_qkv, w_dec_out, w_dec_up, w_dec_down = groups[2]
+    dec_vec = dec_vectors.T.astype(F32)
+    dec_weights = (
+        dec_vec[1], dec_vec[2], w_dec_qkv, w_dec_out, dec_vec[3], dec_vec[4], w_dec_up, w_dec_down
+    )
     positions = jnp.arange(cotangent.shape[1], dtype=jnp.int32)
     matches = positions[:, None] == picks[None, :]
     hidden = 1.0 - jnp.sum(matches.astype(F32), 1, keepdims=True)
@@ -528,8 +657,8 @@
         + hidden * dec_vec[0]
         + sincos(positions.astype(F32), latent.shape[1])
     )
-    decoded, dec_saved = block_forward(inserted, dec_weights, HEADS_DEC, 1)
-    fast = device_count == 32
+    dec_half, dec_saved = attn_half(inserted, *dec_weights[:4], HEADS_DEC, 1)
+    decoded, dec_saved = mlp_half(dec_half, dec_saved, *dec_weights[4:])
     grad_out = cotangent[0].astype(F32)
     dec_branch, dec_upper, rest = mlp_backward(grad_out, dec_weights, dec_saved)
     grad_middle, dec_attn_branch, grad_attn, dec_norm_two = rest(dec_upper)

time: 549 us -> 507 us (0.923)
  waiting for transfers between devices: 183 us -> 127 us
  starting transfers between devices: 27.3 us -> 57.9 us
  local copies, waits for them, and re-layouts: 83.4 us -> 53.5 us
  Pallas kernels: 150 us -> 172 us
  between operations: 17.4 us -> 4.61 us
    all_gather x1 -> x0, waiting for transfers between devices: 127 us -> none  [gather_all(): whole = lax.all_gather(packed, BOTH, axis=0, tiled=False)]
    ppermute x0 -> x15, waiting for transfers between devices: none -> 68.6 us  [the longest x3 21.4 us: corner(): self.pieces.append(lax.ppermute(self.pieces[1], BOTH, FIRST_HOP))]
    slice x8 -> x0, local copies, waits for them, and re-layouts: 27.8 us -> none  [gather_all(): piece = unpack_rows(whole[:, :, at:at + span], half.shape[1])]
    pallas_call x12 -> x15, Pallas kernels: 59.7 us -> 81.2 us  [vmem_call(): pl.pallas_call(kernel, in_specs=[pl.BlockSpec(memory_space=pltpu.SMEM)] +...]
    ppermute x0 -> x15, starting transfers between devices: none -> 19 us  [the longest x3 8.96 us: far_line(): self.arrived = lax.ppermute(self.one, BOTH, hop((8, 8)))]
    ppermute x12, starting transfers between devices: 8.75 us -> 17 us  [later_hop(): self.arrived = lax.ppermute(self.send, BOTH, pairs)]
    dynamic_slice x12 -> x7, local copies, waits for them, and re-layouts: 6.76 us -> 0.97 us  [__init__(): mine = lax.dynamic_slice_in_dim(shard, side * half, half, 1)]
    ppermute x12 -> x24, starting transfers between devices: 15.2 us -> 18.8 us  [swap(): return lax.ppermute(array, 'band', [(0, 1), (1, 0)])]
  transfers between devices with their start and end apart: 29 -> 55, of which waited for: 10 -> 17; matrix products, arithmetic and copies ran while one was open for 9% -> 13% of each run, Pallas kernels for 16% -> 21%
where the time goes in v3:
time: 507 us; the launch traced here: 500 us
  Pallas kernels  172 us (34%)
  waiting for transfers between devices  127 us (25%)
  matrix products  60.2 us (12%)
  starting transfers between devices  57.9 us (11%)
  local copies, waits for them, and re-layouts  53.5 us (11%)
  other arithmetic  25.2 us (5%)
    pallas_call x15, Pallas kernels, vmem_call(): pl.pallas_call(kernel, in_specs=[pl.BlockSpec(memory_space=pltpu.SMEM)] +...  81.2 us
    dot_general x23, matrix products, dot(): lax.dot_general(a, b, (((ca,), (cb,)), ((), ())), preferred_element_type=...  58.7 us
    pallas_call x3, Pallas kernels, attend_backward(): pl.pallas_call(functools.partial(attend_backward_kernel, head_size=head_s...  49.2 us
    ppermute x12, waiting for transfers between devices, later_hop(): self.arrived = lax.ppermute(self.send, BOTH, pairs)  42.8 us
    pallas_call x2, Pallas kernels, attend_forward(): pl.pallas_call(functools.partial(attend_forward_kernel, head_size=head_si...  31.1 us
    unnamed x292, local copies, waits for them, and re-layouts  28.2 us
    ppermute x3, waiting for transfers between devices, corner(): self.pieces.append(lax.ppermute(self.pieces[1], BOTH, FIRST_HOP))  21.4 us
    ppermute x24, starting transfers between devices, swap(): return lax.ppermute(array, 'band', [(0, 1), (1, 0)])  18.8 us
  transfers between devices with their start and end apart: 55, of which 17 were waited for; matrix products, arithmetic and copies ran while one was open for 13% of the time, Pallas kernels for 21%

profile of v3, /device:TPU:1, one launch (start us, length us, event | category | flops | bytes accessed | tf_op | source)
XLA Modules:
  0.0 500.0 jit_solution(6880611087886412507)
XLA Ops:
  16.2 3.9 collective-permute-done
  22.2 5.5 %multiply_sine_fusion = (f32[1024,256]{1,0:T(8,128)}, f32[1024,256]{1,0:T(8,128)}) fusion(f32[256]{0:T(256)S(1)} %multiply_exponential_fusion.1, f32[1024]{0:T(1024)S(1)} %iota_convert_fusion), kind=kLoop, calls=%fused_computation.47 | loop fusion | flops 262144 | bytes 2102272 | tf_op jit(solution)/shard_map/sin | solution.py:27
  33.2 11.6 %collective-permute-done.1 = bf16[48,3328]{1,0:T(8,128)(2,1)S(1)} collective-permute-done((bf16[48,3328]{1,0:T(8,128)(2,1)S(1)}, bf16[48,3328]{1,0:T(8,128)(2,1)S(1)}, u32[]{:S(2)}, u32[]{:S(2)}) %collective-permute-start.1) | collective-permute-done | bytes 319520 | tf_op jit(solution)/shard_map/ppermute | solution.py:404
  51.7 12.3 %collective-permute-done.3 = bf16[2,48,3328]{2,1,0:T(8,128)(2,1)S(1)} collective-permute-done((bf16[2,48,3328]{2,1,0:T(8,128)(2,1)S(1)}, bf16[2,48,3328]{2,1,0:T(8,128)(2,1)S(1)}, u32[]{:S(2)}, u32[]{:S(2)}) %collective-permute-start.3) | collective-permute-done | bytes 639008 | tf_op jit(solution)/shard_map/ppermute | solution.py:413
  67.6 5.0 and.124
  78.0 9.3 %collective-permute-done.6.refs_1_ = bf16[4,48,3328]{2,1,0:T(8,128)(2,1)} collective-permute-done((bf16[4,48,3328]{2,1,0:T(8,128)(2,1)S(1)}, bf16[4,48,3328]{2,1,0:T(8,128)(2,1)}, u32[]{:S(2)}, u32[]{:S(2)}) %collective-permute-start.6) | collective-permute-done | bytes 1277984 | tf_op jit(solution)/shard_map/ppermute | solution.py:423
  93.2 6.5 %shard_map.442 = (bf16[4,4,48,1024]{3,2,1,0:T(8,128)(2,1)}, bf16[4,4,48,256]{3,2,1,0:T(8,128)(2,1)}, bf16[4,4,48,2304]{3,2,1,0:T(8,128)(2,1)}, bf16[4,4,48,768]{3,2,1,0:T(8,128)(2,1)}) custom-call(s32[9]{0:T(128)} %stack.133.scalars, bf16[4,48,2176]{2,1,0:T(8,128)(2,1)} %bitcast.10.refs_0_, bf16[4,48,2176]{2,1,0:T(8,128)(2,1)} %collective-permute-done.4.refs_1_, ...), custom_call_target="tpu_custom_call" | custom-call | tf_op jit(solution)/shard_map/pallas_call | solution.py:354
  103.5 8.0 %collective-permute-done.23.refs_1_ = bf16[4,32,3200]{2,1,0:T(8,128)(2,1)} collective-permute-done((bf16[4,32,3200]{2,1,0:T(8,128)(2,1)S(1)}, bf16[4,32,3200]{2,1,0:T(8,128)(2,1)}, u32[]{:S(2)}, u32[]{:S(2)}) %collective-permute-start.23) | collective-permute-done | bytes 819232 | tf_op jit(solution)/shard_map/ppermute | solution.py:423
  115.8 21.4 %collective-permute-done.25.refs_3_ = bf16[4,32,3200]{2,1,0:T(8,128)(2,1)S(1)} collective-permute-done((bf16[4,32,3200]{2,1,0:T(8,128)(2,1)}, bf16[4,32,3200]{2,1,0:T(8,128)(2,1)S(1)}, u32[]{:S(2)}, u32[]{:S(2)}) %collective-permute-start.25) | collective-permute-done | bytes 819232 | tf_op jit(solution)/shard_map/ppermute | solution.py:429
  148.1 3.8 collective-permute-done.29.refs_7_
  152.8 6.4 %shard_map.445 = (bf16[4,4,32,256]{3,2,1,0:T(8,128)(2,1)}, bf16[4,4,32,1536]{3,2,1,0:T(8,128)(2,1)}, bf16[4,4,32,512]{3,2,1,0:T(8,128)(2,1)}, bf16[4,4,32,2048]{3,2,1,0:T(8,128)(2,1)}, bf16[4,4,128,512]{3,2,1,0:T(8,128)(2,1)}) custom-call(s32[9]{0:T(128)} %stack.133.scalars, bf16[4,32,3200]{2,1,0:T(8,128)(2,1)} %bitcast.181, ...), custom_call_target="tpu_custom_call" | custom-call | tf_op jit(solution)/shard_map/pallas_call | solution.py:354
  161.1 8.7 %shard_map.444 = (bf16[4,4,48,3072]{3,2,1,0:T(8,128)(2,1)}, bf16[4,4,192,768]{3,2,1,0:T(8,128)(2,1)}, bf16[4,4,48,512]{3,2,1,0:T(8,128)(2,1)}) custom-call(s32[9]{0:T(128)} %stack.133.scalars, bf16[4,48,3328]{2,1,0:T(8,128)(2,1)} %bitcast.177, bf16[4,48,3328]{2,1,0:T(8,128)(2,1)} %collective-permute-done.6.refs_1_, ...), custom_call_target="tpu_custom_call" | custom-call | tf_op jit(solution)/shard_map/pallas_call | solution.py:354
  169.9 6.1 %multiply_convert_fusion.1 = (bf16[256,3072]{1,0:T(8,128)(2,1)S(1)}, f32[256,3072]{1,0:T(8,128)}) fusion(bf16[256,768]{1,0:T(8,128)(2,1)S(1)} %copy-done.50, bf16[768,3072]{1,0:T(8,128)(2,1)} %bitcast.216), kind=kOutput, calls=%fused_computation.27 | convolution fusion | flops 1215037440 | bytes 9830400 | tf_op jit(solution)/shard_map/dot_general | solution.py:20
  183.3 27.8 %shard_map.446 = (bf16[512,1024]{1,0:T(8,128)(2,1)S(1)}, f32[16,1,1024]{2,1,0:T(1,128)S(1)}) custom-call(bf16[1536,1024]{1,0:T(8,128)(2,1)S(1)} %convolution_convert_fusion.1.q_ref.k_ref.v_ref, bf16[1536,1024]{1,0:T(8,128)(2,1)S(1)} %convolution_convert_fusion.1.q_ref.k_ref.v_ref, bf16[1536,1024]{1,0:T(8,128)(2,1)S(1)} %convolution_convert_fusion.1.q_ref.k_ref.v_ref), custom_call_target="tpu_custom_call" | custom-call | tf_op jit(solution)/shard_map/pallas_call | solution.py:50
  214.8 5.3 %multiply_convert_fusion = (bf16[1024,2048]{1,0:T(8,128)(2,1)}, f32[1024,2048]{1,0:T(8,128)S(1)}) fusion(bf16[1024,512]{1,0:T(8,128)(2,1)S(1)} %add_convert_fusion.1.refs_2_, bf16[512,2048]{1,0:T(8,128)(2,1)S(1)} %bitcast.226), kind=kOutput, calls=%fused_computation.14 | convolution fusion | flops 2166358016 | bytes 15728640 | tf_op jit(solution)/shard_map/dot_general | solution.py:20
  220.1 7.8 %fusion.6.refs_3_ = bf16[1024,2048]{1,0:T(8,128)(2,1)S(1)} fusion(f32[1024,2048]{1,0:T(8,128)S(1)} %get-tuple-element.408, bf16[2048,512]{1,0:T(8,128)(2,1)S(1)} %bitcast.224, bf16[1,1024,512]{2,1,0:T(8,128)(2,1)S(1)} %copy-done.37), kind=kOutput, calls=%fused_computation.8 | convolution fusion | flops 2189426688 | bytes 15728640 | tf_op jit(solution)/shard_map/dot_general | solution.py:20
  235.0 8.7 %shard_map.447 = bf16[16,16,4608]{2,1,0:T(8,128)(2,1)} custom-call(s32[1]{0:T(128)} %bitcast.26.scalars, bf16[1024,2048]{1,0:T(8,128)(2,1)} %get-tuple-element.407.refs_0_, bf16[1024,512]{1,0:T(8,128)(2,1)} %bitcast.172, bf16[1024,512]{1,0:T(8,128)(2,1)} %copy-done.39, bf16[1024,2048]{1,0:T(8,128)(2,1)} %copy-done.36, bf16[512,1024]{1,0:T(8,128)(2,1)} %copy-done.8, ...), custom_call_target="tpu_custom_call" | custom-call | tf_op jit(solution)/shard_map/pallas_call | solution.py:354
  248.0 22.7 %shard_map.448.rest_0_ = bf16[3,512,1024]{2,1,0:T(8,128)(2,1)S(1)} custom-call(bf16[1536,1024]{1,0:T(8,128)(2,1)S(1)} %convolution_convert_fusion.1.q_ref.k_ref.v_ref, bf16[1536,1024]{1,0:T(8,128)(2,1)S(1)} %convolution_convert_fusion.1.q_ref.k_ref.v_ref, bf16[1536,1024]{1,0:T(8,128)(2,1)S(1)} %convolution_convert_fusion.1.q_ref.k_ref.v_ref, ...), custom_call_target="tpu_custom_call" | custom-call | tf_op jit(solution)/shard_map/pallas_call | solution.py:92
  272.4 9.1 %shard_map.449 = (bf16[8,16,4608]{2,1,0:T(8,128)(2,1)}, bf16[8,16,4608]{2,1,0:T(8,128)(2,1)}) custom-call(s32[17]{0:T(128)} %pad_add_fusion.1.scalars, bf16[1024,2048]{1,0:T(8,128)(2,1)} %get-tuple-element.407.refs_0_, bf16[1024,512]{1,0:T(8,128)(2,1)} %bitcast.173, bf16[1024,512]{1,0:T(8,128)(2,1)} %copy-done.39, bf16[1024,2048]{1,0:T(8,128)(2,1)} %copy-done.36, ...), custom_call_target="tpu_custom_call" | custom-call | tf_op jit(solution)/shard_map/pallas_call | solution.py:354
  288.0 22.9 %shard_map.450 = bf16[3,512,1024]{2,1,0:T(8,128)(2,1)S(1)} custom-call(bf16[1536,1024]{1,0:T(8,128)(2,1)S(1)} %convolution_convert_fusion.1.q_ref.k_ref.v_ref, bf16[1536,1024]{1,0:T(8,128)(2,1)S(1)} %convolution_convert_fusion.1.q_ref.k_ref.v_ref, bf16[1536,1024]{1,0:T(8,128)(2,1)S(1)} %convolution_convert_fusion.1.q_ref.k_ref.v_ref, ...), custom_call_target="tpu_custom_call", output_to_operand_aliasing={{}: (6, {})} | custom-call | tf_op jit(solution)/shard_map/pallas_call | solution.py:92
  322.2 4.1 fusion.16.refs_3_
  326.3 6.0 %shard_map.452 = bf16[16,16,9216]{2,1,0:T(8,128)(2,1)} custom-call(s32[1]{0:T(128)} %bitcast.26.scalars, bf16[256,3072]{1,0:T(8,128)(2,1)} %copy-done.42, bf16[256,768]{1,0:T(8,128)(2,1)} %copy-done.51, bf16[256,768]{1,0:T(8,128)(2,1)} %add_convert_fusion.3.refs_2_, bf16[256,3072]{1,0:T(8,128)(2,1)} %fusion.16.refs_3_), custom_call_target="tpu_custom_call" | custom-call | tf_op jit(solution)/shard_map/pallas_call | solution.py:354
  333.8 4.1 multiply_reduce_fusion.9
  344.3 6.8 %shard_map.456 = bf16[16,16,7168]{2,1,0:T(8,128)(2,1)} custom-call(s32[1]{0:T(128)} %bitcast.26.scalars, bf16[768,256]{1,0:T(8,128)(2,1)} %copy-done.15, bf16[256,768]{1,0:T(8,128)(2,1)} %copy-done.47, bf16[256,768]{1,0:T(8,128)(2,1)} %copy-done.48, bf16[2304,256]{1,0:T(8,128)(2,1)} %bitcast.169, bf16[1024,512]{1,0:T(8,128)(2,1)} %copy-done.40, ...), custom_call_target="tpu_custom_call" | custom-call | tf_op jit(solution)/shard_map/pallas_call | solution.py:354
  353.4 7.4 %shard_map.454 = (bf16[8,16,9216]{2,1,0:T(8,128)(2,1)}, bf16[8,16,9216]{2,1,0:T(8,128)(2,1)}) custom-call(s32[17]{0:T(128)} %pad_add_fusion.1.scalars, bf16[256,3072]{1,0:T(8,128)(2,1)} %copy-done.42, bf16[256,768]{1,0:T(8,128)(2,1)} %copy-done.51, bf16[256,768]{1,0:T(8,128)(2,1)} %add_convert_fusion.3.refs_2_, bf16[256,3072]{1,0:T(8,128)(2,1)} %fusion.16.refs_3_, ...), custom_call_target="tpu_custom_call" | custom-call | tf_op jit(solution)/shard_map/pallas_call | solution.py:354
  375.3 7.9 %shard_map.458 = (bf16[8,16,7168]{2,1,0:T(8,128)(2,1)}, bf16[8,16,7168]{2,1,0:T(8,128)(2,1)}) custom-call(s32[17]{0:T(128)} %pad_add_fusion.1.scalars, bf16[768,256]{1,0:T(8,128)(2,1)} %copy-done.15, bf16[256,768]{1,0:T(8,128)(2,1)} %copy-done.47, bf16[256,768]{1,0:T(8,128)(2,1)} %copy-done.48, bf16[2304,256]{1,0:T(8,128)(2,1)} %bitcast.170, ...), custom_call_target="tpu_custom_call" | custom-call | tf_op jit(solution)/shard_map/pallas_call | solution.py:354
  385.5 7.0 %collective-permute-done.35.recv_send.recv_keep = bf16[2,16,4608]{2,1,0:T(8,128)(2,1)S(1)} collective-permute-done((bf16[2,16,4608]{2,1,0:T(8,128)(2,1)S(1)}, bf16[2,16,4608]{2,1,0:T(8,128)(2,1)S(1)}, u32[]{:S(2)}, u32[]{:S(2)}) %collective-permute-start.35) | collective-permute-done | bytes 294944 | tf_op jit(solution)/shard_map/ppermute | solution.py:530
  401.0 3.6 shard_map.461
  408.8 13.4 %collective-permute-done.43.recv_send.recv_keep = bf16[4,16,9216]{2,1,0:T(8,128)(2,1)S(1)} collective-permute-done((bf16[4,16,9216]{2,1,0:T(8,128)(2,1)S(1)}, bf16[4,16,9216]{2,1,0:T(8,128)(2,1)S(1)}, u32[]{:S(2)}, u32[]{:S(2)}) %collective-permute-start.43) | collective-permute-done | bytes 1179680 | tf_op jit(solution)/shard_map/ppermute | solution.py:530
  429.5 10.5 %collective-permute-done.41.recv_send.recv_keep = bf16[8,16,1920]{2,1,0:T(8,128)(2,1)S(1)} collective-permute-done((bf16[8,16,1920]{2,1,0:T(8,128)(2,1)S(1)}, bf16[8,16,1920]{2,1,0:T(8,128)(2,1)S(1)}, u32[]{:S(2)}, u32[]{:S(2)}) %collective-permute-start.41) | collective-permute-done | bytes 491552 | tf_op jit(solution)/shard_map/ppermute | solution.py:519
  452.5 9.1 %collective-permute-done.48.recv_send.recv_keep = bf16[2,16,7168]{2,1,0:T(8,128)(2,1)S(1)} collective-permute-done((bf16[2,16,7168]{2,1,0:T(8,128)(2,1)S(1)}, bf16[2,16,7168]{2,1,0:T(8,128)(2,1)S(1)}, u32[]{:S(2)}, u32[]{:S(2)}) %collective-permute-start.48) | collective-permute-done | bytes 458784 | tf_op jit(solution)/shard_map/ppermute | solution.py:530
  472.7 8.9 %collective-permute-done.51 = bf16[1,16,7168]{2,1,0:T(8,128)(2,1)S(1)} collective-permute-done((bf16[1,16,7168]{2,1,0:T(8,128)(2,1)S(1)}, bf16[1,16,7168]{2,1,0:T(8,128)(2,1)S(1)}, u32[]{:S(2)}, u32[]{:S(2)}) %collective-permute-start.51) | collective-permute-done | bytes 229408 | tf_op jit(solution)/shard_map/ppermute | solution.py:530
  (542 shorter events, 194.0 us)
Async XLA Ops:
  2.4 43.2 %collective-permute-start.18 = (s32[7]{0:T(128)S(1)}, s32[7]{0:T(128)S(1)}, u32[]{:S(2)}, u32[]{:S(2)}) collective-permute-start(s32[7]{0:T(128)S(1)} %get-tuple-element.397), channel_id=1, source_target_pairs={{0,1},{1,0},{2,3},{3,2},{4,5},{5,4},{6,7},{7,6},{8,9},{9,8},{10,11... | collective-permute-start | bytes 92 | tf_op jit(solution)/shard_map/ppermute | solution.py:183
  3.2 44.4 %collective-permute-start.17 = (s32[7]{0:T(128)S(1)}, s32[7]{0:T(128)S(1)}, u32[]{:S(2)}, u32[]{:S(2)}) collective-permute-start(s32[7]{0:T(128)S(1)} %get-tuple-element.400), channel_id=1, source_target_pairs={{0,1},{1,0},{2,3},{3,2},{4,5},{5,4},{6,7},{7,6},{8,9},{9,8},{10,11... | collective-permute-start | bytes 92 | tf_op jit(solution)/shard_map/ppermute | solution.py:183
  12.5 60.1 %collective-permute-start.16 = (bf16[254,448]{0,1:T(8,128)(2,1)}, bf16[254,448]{0,1:T(8,128)(2,1)}, u32[]{:S(2)}, u32[]{:S(2)}) collective-permute-start(bf16[254,448]{0,1:T(8,128)(2,1)} %get-tuple-element.385), channel_id=1, source_target_pairs={{0,1},{1,0},{2,3},{3,2},{4,5},{5,4},{6,7},{7,6},{8,9},{9,8},{10,11... | collective-permute-start | bytes 682760 | tf_op jit(solution)/shard_map/ppermute | solution.py:183
  27.7 17.1 %collective-permute-start.1 = (bf16[48,3328]{1,0:T(8,128)(2,1)S(1)}, bf16[48,3328]{1,0:T(8,128)(2,1)S(1)}, u32[]{:S(2)}, u32[]{:S(2)}) collective-permute-start(bf16[48,3328]{1,0:T(8,128)(2,1)S(1)} %constant_dynamic-update-slice_fusion), channel_id=1, source_target_pairs={{0,16},{1,17},{2,18},{3,19},{4,20},{5,21},{6,22},{7,23},{8,24},{9,... | collective-permute-start | bytes 958472 | tf_op jit(solution)/shard_map/ppermute | solution.py:404
  32.0 19.5 %collective-permute-start.4 = (bf16[4,48,2176]{2,1,0:T(8,128)(2,1)}, bf16[4,48,2176]{2,1,0:T(8,128)(2,1)}, u32[]{:S(2)}, u32[]{:S(2)}) collective-permute-start(bf16[4,48,2176]{2,1,0:T(8,128)(2,1)} %bitcast.10.refs_0_), channel_id=1, source_target_pairs={{0,2},{1,5},{2,0},{3,7},{4,6},{5,1},{6,4},{7,3},{8,10},{9,13},{10,... | collective-permute-start | bytes 2506760 | tf_op jit(solution)/shard_map/ppermute | solution.py:423
  44.9 19.1 %collective-permute-start.3 = (bf16[2,48,3328]{2,1,0:T(8,128)(2,1)S(1)}, bf16[2,48,3328]{2,1,0:T(8,128)(2,1)S(1)}, u32[]{:S(2)}, u32[]{:S(2)}) collective-permute-start(bf16[2,48,3328]{2,1,0:T(8,128)(2,1)S(1)} %pad_maximum_fusion.5), channel_id=1, source_target_pairs={{0,8},{1,9},{2,10},{3,11},{4,12},{5,13},{6,14},{7,15},{8,0},{9,1},... | collective-permute-start | bytes 1916936 | tf_op jit(solution)/shard_map/ppermute | solution.py:413
  47.8 29.5 %collective-permute-start.10 = (bf16[4,48,2176]{2,1,0:T(8,128)(2,1)}, bf16[4,48,2176]{2,1,0:T(8,128)(2,1)}, u32[]{:S(2)}, u32[]{:S(2)}) collective-permute-start(bf16[4,48,2176]{2,1,0:T(8,128)(2,1)} %bitcast.10.refs_0_), channel_id=1, source_target_pairs={{0,4},{1,3},{2,6},{3,1},{4,0},{5,7},{6,2},{7,5},{8,12},{9,11},{10,... | collective-permute-start | bytes 2506760 | tf_op jit(solution)/shard_map/ppermute | solution.py:423
  49.0 16.7 %collective-permute-start.8 = (bf16[32,3200]{1,0:T(8,128)(2,1)S(1)}, bf16[32,3200]{1,0:T(8,128)(2,1)S(1)}, u32[]{:S(2)}, u32[]{:S(2)}) collective-permute-start(bf16[32,3200]{1,0:T(8,128)(2,1)S(1)} %constant_dynamic-update-slice_fusion.1), channel_id=1, source_target_pairs={{0,16},{1,17},{2,18},{3,19},{4,20},{5,21},{6,22},{7,23},{8,24},{9,... | collective-permute-start | bytes 614408 | tf_op jit(solution)/shard_map/ppermute | solution.py:404
  51.5 25.9 %collective-permute-start.11 = (bf16[4,48,2176]{2,1,0:T(8,128)(2,1)}, bf16[4,48,2176]{2,1,0:T(8,128)(2,1)}, u32[]{:S(2)}, u32[]{:S(2)}) collective-permute-start(bf16[4,48,2176]{2,1,0:T(8,128)(2,1)} %collective-permute-done.4.refs_1_), channel_id=1, source_target_pairs={{0,4},{1,3},{2,6},{3,1},{4,0},{5,7},{6,2},{7,5},{8,12},{9,11},{10,... | collective-permute-start | bytes 2506760 | tf_op jit(solution)/shard_map/ppermute | solution.py:429
  64.4 22.9 %collective-permute-start.6 = (bf16[4,48,3328]{2,1,0:T(8,128)(2,1)S(1)}, bf16[4,48,3328]{2,1,0:T(8,128)(2,1)}, u32[]{:S(2)}, u32[]{:S(2)}) collective-permute-start(bf16[4,48,3328]{2,1,0:T(8,128)(2,1)S(1)} %bitcast.174), channel_id=1, source_target_pairs={{0,2},{1,5},{2,0},{3,7},{4,6},{5,1},{6,4},{7,3},{8,10},{9,13},{10,... | collective-permute-start | bytes 3833864 | tf_op jit(solution)/shard_map/ppermute | solution.py:423
  66.6 20.8 %collective-permute-start.9 = (bf16[2,32,3200]{2,1,0:T(8,128)(2,1)}, bf16[2,32,3200]{2,1,0:T(8,128)(2,1)}, u32[]{:S(2)}, u32[]{:S(2)}) collective-permute-start(bf16[2,32,3200]{2,1,0:T(8,128)(2,1)} %pad_maximum_fusion.7), channel_id=1, source_target_pairs={{0,8},{1,9},{2,10},{3,11},{4,12},{5,13},{6,14},{7,15},{8,0},{9,1},... | collective-permute-start | bytes 1228808 | tf_op jit(solution)/shard_map/ppermute | solution.py:413
  77.4 67.4 %collective-permute-start.5 = (bf16[4,48,3328]{2,1,0:T(8,128)(2,1)S(1)}, bf16[4,48,3328]{2,1,0:T(8,128)(2,1)}, u32[]{:S(2)}, u32[]{:S(2)}) collective-permute-start(bf16[4,48,3328]{2,1,0:T(8,128)(2,1)S(1)} %bitcast.175), channel_id=1, source_target_pairs={{0,4},{1,3},{2,6},{3,1},{4,0},{5,7},{6,2},{7,5},{8,12},{9,11},{10,... | collective-permute-start | bytes 3833864 | tf_op jit(solution)/shard_map/ppermute | solution.py:423
  89.1 56.9 %collective-permute-start.26 = (bf16[4,32,3200]{2,1,0:T(8,128)(2,1)S(1)}, bf16[4,32,3200]{2,1,0:T(8,128)(2,1)}, u32[]{:S(2)}, u32[]{:S(2)}) collective-permute-start(bf16[4,32,3200]{2,1,0:T(8,128)(2,1)S(1)} %bitcast.178), channel_id=1, source_target_pairs={{0,1},{1,0},{2,3},{3,2},{4,5},{5,4},{6,7},{7,6},{8,9},{9,8},{10,11... | collective-permute-start | bytes 2457608 | tf_op jit(solution)/shard_map/ppermute | solution.py:183
  89.2 25.6 %collective-permute-start.24 = (bf16[4,32,3200]{2,1,0:T(8,128)(2,1)S(1)}, bf16[4,32,3200]{2,1,0:T(8,128)(2,1)}, u32[]{:S(2)}, u32[]{:S(2)}) collective-permute-start(bf16[4,32,3200]{2,1,0:T(8,128)(2,1)S(1)} %bitcast.179), channel_id=1, source_target_pairs={{0,4},{1,3},{2,6},{3,1},{4,0},{5,7},{6,2},{7,5},{8,12},{9,11},{10,... | collective-permute-start | bytes 2457608 | tf_op jit(solution)/shard_map/ppermute | solution.py:423
  91.1 20.4 %collective-permute-start.23 = (bf16[4,32,3200]{2,1,0:T(8,128)(2,1)S(1)}, bf16[4,32,3200]{2,1,0:T(8,128)(2,1)}, u32[]{:S(2)}, u32[]{:S(2)}) collective-permute-start(bf16[4,32,3200]{2,1,0:T(8,128)(2,1)S(1)} %bitcast.180), channel_id=1, source_target_pairs={{0,2},{1,5},{2,0},{3,7},{4,6},{5,1},{6,4},{7,3},{8,10},{9,13},{10,... | collective-permute-start | bytes 2457608 | tf_op jit(solution)/shard_map/ppermute | solution.py:423
  92.3 53.5 %collective-permute-start.7 = (bf16[4,48,3328]{2,1,0:T(8,128)(2,1)}, bf16[4,48,3328]{2,1,0:T(8,128)(2,1)}, u32[]{:S(2)}, u32[]{:S(2)}) collective-permute-start(bf16[4,48,3328]{2,1,0:T(8,128)(2,1)} %collective-permute-done.6.refs_1_), channel_id=1, source_target_pairs={{0,4},{1,3},{2,6},{3,1},{4,0},{5,7},{6,2},{7,5},{8,12},{9,11},{10,... | collective-permute-start | bytes 3833864 | tf_op jit(solution)/shard_map/ppermute | solution.py:429
  111.5 25.7 %collective-permute-start.25 = (bf16[4,32,3200]{2,1,0:T(8,128)(2,1)}, bf16[4,32,3200]{2,1,0:T(8,128)(2,1)S(1)}, u32[]{:S(2)}, u32[]{:S(2)}) collective-permute-start(bf16[4,32,3200]{2,1,0:T(8,128)(2,1)} %collective-permute-done.23.refs_1_), channel_id=1, source_target_pairs={{0,4},{1,3},{2,6},{3,1},{4,0},{5,7},{6,2},{7,5},{8,12},{9,11},{10,... | collective-permute-start | bytes 2457608 | tf_op jit(solution)/shard_map/ppermute | solution.py:429
  114.8 31.5 %collective-permute-start.27 = (bf16[4,32,3200]{2,1,0:T(8,128)(2,1)}, bf16[4,32,3200]{2,1,0:T(8,128)(2,1)}, u32[]{:S(2)}, u32[]{:S(2)}) collective-permute-start(bf16[4,32,3200]{2,1,0:T(8,128)(2,1)} %collective-permute-done.23.refs_1_), channel_id=1, source_target_pairs={{0,1},{1,0},{2,3},{3,2},{4,5},{5,4},{6,7},{7,6},{8,9},{9,8},{10,11... | collective-permute-start | bytes 2457608 | tf_op jit(solution)/shard_map/ppermute | solution.py:183
  144.8 16.3 %collective-permute-start.19 = (bf16[4,48,3328]{2,1,0:T(8,128)(2,1)S(1)}, bf16[4,48,3328]{2,1,0:T(8,128)(2,1)}, u32[]{:S(2)}, u32[]{:S(2)}) collective-permute-start(bf16[4,48,3328]{2,1,0:T(8,128)(2,1)S(1)} %bitcast.176), channel_id=1, source_target_pairs={{0,1},{1,0},{2,3},{3,2},{4,5},{5,4},{6,7},{7,6},{8,9},{9,8},{10,11... | collective-permute-start | bytes 3833864 | tf_op jit(solution)/shard_map/ppermute | solution.py:183
  243.7 28.7 %collective-permute-start.30 = (bf16[16,16,4608]{2,1,0:T(8,128)(2,1)}, bf16[16,16,4608]{2,1,0:T(8,128)(2,1)}, u32[]{:S(2)}, u32[]{:S(2)}) collective-permute-start(bf16[16,16,4608]{2,1,0:T(8,128)(2,1)} %shard_map.447), channel_id=1, source_target_pairs={{0,1},{1,0},{2,3},{3,2},{4,5},{5,4},{6,7},{7,6},{8,9},{9,8},{10,11... | collective-permute-start | bytes 7077896 | tf_op jit(solution)/shard_map/ppermute | solution.py:183
  281.5 31.0 %collective-permute-start.31 = (bf16[8,16,4608]{2,1,0:T(8,128)(2,1)}, bf16[8,16,4608]{2,1,0:T(8,128)(2,1)}, u32[]{:S(2)}, u32[]{:S(2)}) collective-permute-start(bf16[8,16,4608]{2,1,0:T(8,128)(2,1)} %get-tuple-element.164), channel_id=1, source_target_pairs={{0,4},{1,3},{2,6},{3,1},{4,0},{5,7},{6,2},{7,5},{8,12},{9,11},{10,... | collective-permute-start | bytes 3538952 | tf_op jit(solution)/shard_map/ppermute | solution.py:519
  332.3 21.1 %collective-permute-start.33 = (bf16[16,16,9216]{2,1,0:T(8,128)(2,1)}, bf16[16,16,9216]{2,1,0:T(8,128)(2,1)}, u32[]{:S(2)}, u32[]{:S(2)}) collective-permute-start(bf16[16,16,9216]{2,1,0:T(8,128)(2,1)} %shard_map.452), channel_id=1, source_target_pairs={{0,1},{1,0},{2,3},{3,2},{4,5},{5,4},{6,7},{7,6},{8,9},{9,8},{10,11... | collective-permute-start | bytes 14155784 | tf_op jit(solution)/shard_map/ppermute | solution.py:183
  351.1 24.2 %collective-permute-start.36 = (bf16[16,16,7168]{2,1,0:T(8,128)(2,1)}, bf16[16,16,7168]{2,1,0:T(8,128)(2,1)}, u32[]{:S(2)}, u32[]{:S(2)}) collective-permute-start(bf16[16,16,7168]{2,1,0:T(8,128)(2,1)} %shard_map.456), channel_id=1, source_target_pairs={{0,1},{1,0},{2,3},{3,2},{4,5},{5,4},{6,7},{7,6},{8,9},{9,8},{10,11... | collective-permute-start | bytes 11010056 | tf_op jit(solution)/shard_map/ppermute | solution.py:183
  360.9 36.8 %collective-permute-start.39 = (bf16[8,16,9216]{2,1,0:T(8,128)(2,1)}, bf16[8,16,9216]{2,1,0:T(8,128)(2,1)}, u32[]{:S(2)}, u32[]{:S(2)}) collective-permute-start(bf16[8,16,9216]{2,1,0:T(8,128)(2,1)} %get-tuple-element.175), channel_id=1, source_target_pairs={{0,4},{1,3},{2,6},{3,1},{4,0},{5,7},{6,2},{7,5},{8,12},{9,11},{10,... | collective-permute-start | bytes 7077896 | tf_op jit(solution)/shard_map/ppermute | solution.py:519
  371.6 29.4 %collective-permute-start.38 = (bf16[16,16,1920]{2,1,0:T(8,128)(2,1)}, bf16[16,16,1920]{2,1,0:T(8,128)(2,1)}, u32[]{:S(2)}, u32[]{:S(2)}) collective-permute-start(bf16[16,16,1920]{2,1,0:T(8,128)(2,1)} %shard_map.457), channel_id=1, source_target_pairs={{0,1},{1,0},{2,3},{3,2},{4,5},{5,4},{6,7},{7,6},{8,9},{9,8},{10,11... | collective-permute-start | bytes 2949128 | tf_op jit(solution)/shard_map/ppermute | solution.py:183
  383.2 39.4 %collective-permute-start.42 = (bf16[8,16,7168]{2,1,0:T(8,128)(2,1)}, bf16[8,16,7168]{2,1,0:T(8,128)(2,1)}, u32[]{:S(2)}, u32[]{:S(2)}) collective-permute-start(bf16[8,16,7168]{2,1,0:T(8,128)(2,1)} %get-tuple-element.183), channel_id=1, source_target_pairs={{0,4},{1,3},{2,6},{3,1},{4,0},{5,7},{6,2},{7,5},{8,12},{9,11},{10,... | collective-permute-start | bytes 5505032 | tf_op jit(solution)/shard_map/ppermute | solution.py:519
  400.3 22.0 %collective-permute-start.43 = (bf16[4,16,9216]{2,1,0:T(8,128)(2,1)S(1)}, bf16[4,16,9216]{2,1,0:T(8,128)(2,1)S(1)}, u32[]{:S(2)}, u32[]{:S(2)}) collective-permute-start(bf16[4,16,9216]{2,1,0:T(8,128)(2,1)S(1)} %get-tuple-element.189), channel_id=1, source_target_pairs={{0,2},{1,5},{2,0},{3,7},{4,6},{5,1},{6,4},{7,3},{8,10},{9,13},{10,... | collective-permute-start | bytes 3538952 | tf_op jit(solution)/shard_map/ppermute | solution.py:530
  426.5 18.8 %collective-permute-start.45 = (bf16[4,16,7168]{2,1,0:T(8,128)(2,1)S(1)}, bf16[4,16,7168]{2,1,0:T(8,128)(2,1)S(1)}, u32[]{:S(2)}, u32[]{:S(2)}) collective-permute-start(bf16[4,16,7168]{2,1,0:T(8,128)(2,1)S(1)} %get-tuple-element.202), channel_id=1, source_target_pairs={{0,2},{1,5},{2,0},{3,7},{4,6},{5,1},{6,4},{7,3},{8,10},{9,13},{10,... | collective-permute-start | bytes 2752520 | tf_op jit(solution)/shard_map/ppermute | solution.py:530
  443.0 22.1 %collective-permute-start.53 = (bf16[1,16,9216]{2,1,0:T(8,128)(2,1)S(1)}, bf16[1,16,9216]{2,1,0:T(8,128)(2,1)S(1)}, u32[]{:S(2)}, u32[]{:S(2)}) collective-permute-start(bf16[1,16,9216]{2,1,0:T(8,128)(2,1)S(1)} %get-tuple-element.209), channel_id=1, source_target_pairs={{0,16},{1,17},{2,18},{3,19},{4,20},{5,21},{6,22},{7,23},{8,24},{9,... | collective-permute-start | bytes 884744 | tf_op jit(solution)/shard_map/ppermute | solution.py:530
  447.4 16.8 %collective-permute-start.47 = (bf16[2,16,1920]{2,1,0:T(8,128)(2,1)S(1)}, bf16[2,16,1920]{2,1,0:T(8,128)(2,1)S(1)}, u32[]{:S(2)}, u32[]{:S(2)}) collective-permute-start(bf16[2,16,1920]{2,1,0:T(8,128)(2,1)S(1)} %get-tuple-element.214), channel_id=1, source_target_pairs={{0,8},{1,9},{2,10},{3,11},{4,12},{5,13},{6,14},{7,15},{8,0},{9,1},... | collective-permute-start | bytes 368648 | tf_op jit(solution)/shard_map/ppermute | solution.py:530
  465.2 19.8 %collective-permute-start.54 = (bf16[16,9216]{1,0:T(8,128)(2,1)S(1)}, bf16[16,9216]{1,0:T(8,128)(2,1)S(1)}, u32[]{:S(2)}, u32[]{:S(2)}) collective-permute-start(bf16[16,9216]{1,0:T(8,128)(2,1)S(1)} %fusion.29.mine), channel_id=1, source_target_pairs={{0,1},{1,0},{2,3},{3,2},{4,5},{5,4},{6,7},{7,6},{8,9},{9,8},{10,11... | collective-permute-start | bytes 884744 | tf_op jit(solution)/shard_map/ppermute | solution.py:183
  469.5 18.4 %collective-permute-start.50 = (bf16[16,1920]{1,0:T(8,128)(2,1)S(1)}, bf16[16,1920]{1,0:T(8,128)(2,1)S(1)}, u32[]{:S(2)}, u32[]{:S(2)}) collective-permute-start(bf16[16,1920]{1,0:T(8,128)(2,1)S(1)} %fusion.32.mine), channel_id=1, source_target_pairs={{0,1},{1,0},{2,3},{3,2},{4,5},{5,4},{6,7},{7,6},{8,9},{9,8},{10,11... | collective-permute-start | bytes 184328 | tf_op jit(solution)/shard_map/ppermute | solution.py:183
  (162 other events, 1671.0 us)

commit v4 on v3

--- a/solution.py
+++ b/solution.py
@@ -261,6 +261,11 @@
     return jnp.pad(stacked, ((0, 0), (0, lanes - stacked.shape[1])))
 
 
+def vector_rows(vectors):
+    stacked = jnp.stack(vectors)
+    return jnp.pad(stacked, ((0, TILE - stacked.shape[0]), (0, 0))).astype(BF16)
+
+
 def hop(flips):
     return [
         (dp * 2 + band, (dp ^ flips[band]) * 2 + band) for dp in range(16) for band in range(2)
@@ -287,12 +292,11 @@
 def products_of(jobs, spots, refs, which):
     ins = list(refs)
     for (left_axis, right_axis), spot in zip(jobs, spots):
-        left = None if left_axis is None else ins.pop(0)
-        right = ins.pop(0)
+        left, right = ins.pop(0), ins.pop(0)
         half = spot[1]
         span = pl.ds(pl.multiple_of(which * half, 128), half)
         values = right[span] if right_axis == 1 else right[:, span]
-        yield values if left is None else dot(left[...], values, left_axis, right_axis)
+        yield dot(left[...], values, left_axis, right_axis)
 
 
 def send_kernel(scalars, *refs, jobs, spots):
@@ -338,29 +342,34 @@
                 out[group * TILE : (group + 1) * TILE, lanes] = source[:, span].astype(F32)
 
 
-def grid_call(kernel, scalars, grid, in_specs, out_specs, out_shape, *args):
+def without(kernel, start, count):
+    return lambda *refs: kernel(*refs[:start], *refs[start + count :])
+
+
+def grid_call(kernel, scalars, grid, in_specs, out_specs, out_shape, *args, after=()):
+    away = [pl.BlockSpec(memory_space=pl.ANY)] * len(after)
     return pl.pallas_call(
-        kernel,
+        without(kernel, 1 + len(args), len(after)),
         grid_spec=pltpu.PrefetchScalarGridSpec(
-            num_scalar_prefetch=1, grid=grid, in_specs=in_specs, out_specs=out_specs
+            num_scalar_prefetch=1, grid=grid, in_specs=in_specs + away, out_specs=out_specs
         ),
         out_shape=out_shape,
         compiler_params=pltpu.CompilerParams(vmem_limit_bytes=40 << 20),
-    )(scalars, *args)
-
-
-def vmem_call(kernel, out_shape, *args, away=0, scratch_shapes=()):
+    )(scalars, *args, *after)
+
+
+def vmem_call(kernel, out_shape, *args, away=0, scratch_shapes=(), after=()):
     whole = pl.BlockSpec(memory_space=pltpu.VMEM)
     return pl.pallas_call(
-        kernel,
+        without(kernel, len(args), len(after)),
         in_specs=[pl.BlockSpec(memory_space=pltpu.SMEM)]
         + [whole] * (len(args) - 1 - away)
-        + [pl.BlockSpec(memory_space=pl.ANY)] * away,
+        + [pl.BlockSpec(memory_space=pl.ANY)] * (away + len(after)),
         out_specs=[whole] * len(out_shape),
         out_shape=out_shape,
         scratch_shapes=scratch_shapes,
         compiler_params=pltpu.CompilerParams(vmem_limit_bytes=56 << 20),
-    )(*args)
+    )(*args, *after)
 
 
 def assemble_kernel(scalars, *refs, spots):
@@ -435,7 +444,7 @@
         self.partner += [swap(piece) for piece in self.pieces[2:]]
         return self.pieces[3]
 
-    def weights(self):
+    def weights(self, after=()):
         place = lambda x, y: y * 2 + x
         here, across, corner = (
             place(self.x, self.y), place(1 - self.x, self.y), place(1 - self.x, 1 - self.y)
@@ -452,27 +461,28 @@
             *self.partner,
             away=8,
             scratch_shapes=[pltpu.SemaphoreType.DMA(())],
+            after=after,
         )
         return [out.reshape(-1, out.shape[3]) for out in outs]
 
 
 class Bucket:
-    def __init__(self, products):
+    def __init__(self, products, after=()):
         dp, side = lax.axis_index("dp"), lax.axis_index("band")
         self.x, self.y, self.z, self.side = dp % 2, dp // 2 % 2, dp // 4, side
         self.scalars = side[None].astype(jnp.int32)
         shapes, self.jobs, self.args = [], [], []
         for left, left_axis, right, right_axis in products:
-            length = right.shape[0] if left is None else left.shape[1 - left_axis]
-            shapes.append((length // 16, right.shape[1 - right_axis] // 2))
+            shapes.append((left.shape[1 - left_axis] // 16, right.shape[1 - right_axis] // 2))
             self.jobs.append((left_axis, right_axis))
-            self.args += [right] if left is None else [left, right]
+            self.args += [left, right]
         self.spots, self.total = places(shapes)
         (self.send,) = vmem_call(
             functools.partial(send_kernel, jobs=self.jobs, spots=self.spots),
             [self.shaped(16)],
             self.scalars,
             *self.args,
+            after=after,
         )
 
     def shaped(self, count):
@@ -481,7 +491,7 @@
     def block(self, index):
         return pl.BlockSpec((1, TILE, self.total), index)
 
-    def split(self, count, table, goes, stays):
+    def split(self, count, table, goes, stays, after=()):
         goes, stays, out = self.block(goes), self.block(stays), self.block(lambda i, t: (i, 0, 0))
         self.send, self.keep = grid_call(
             split_kernel,
@@ -494,12 +504,13 @@
             self.keep,
             self.arrived,
             self.arrived,
+            after=after,
         )
 
     def pair_hop(self):
         self.arrived = swap(self.send)
 
-    def first_hop(self, clock):
+    def first_hop(self, clock, after=()):
         self.arrived, clock = tie(self.arrived, clock)
         line = jnp.arange(8, dtype=jnp.int32)
         z, other = line // 2, line % 2
@@ -515,30 +526,32 @@
             away=1,
             scratch_shapes=[pltpu.VMEM((16, TILE, self.total), BF16), pltpu.SemaphoreType.DMA(())]
             + [pltpu.VMEM((16 * rows, half), F32) for rows, half, _ in self.spots],
+            after=after,
         )
         self.arrived = lax.ppermute(self.send, BOTH, FIRST_HOP)
         return self.send
 
-    def later_hop(self, clock, count, bit, pairs):
+    def later_hop(self, clock, count, bit, pairs, after):
         self.arrived, clock = tie(self.arrived, clock)
         self.split(
             count,
             bit[None],
             lambda i, t: (2 * i + 1 - t[0], 0, 0),
             lambda i, t: (2 * i + t[0], 0, 0),
+            after,
         )
         self.arrived = lax.ppermute(self.send, BOTH, pairs)
         return self.send
 
-    def second_hop(self, clock):
+    def second_hop(self, clock, after=()):
         far = jnp.where(self.side == 0, self.x, self.y)
-        return self.later_hop(clock, 4, far, SECOND_HOP)
-
-    def third_hop(self, clock):
-        return self.later_hop(clock, 2, self.z % 2, hop((4, 4)))
-
-    def fourth_hop(self, clock):
-        return self.later_hop(clock, 1, self.z // 2, hop((8, 8)))
+        return self.later_hop(clock, 4, far, SECOND_HOP, after)
+
+    def third_hop(self, clock, after=()):
+        return self.later_hop(clock, 2, self.z % 2, hop((4, 4)), after)
+
+    def fourth_hop(self, clock, after=()):
+        return self.later_hop(clock, 1, self.z // 2, hop((8, 8)), after)
 
     def finish(self):
         mine = (self.keep[0].astype(F32) + self.arrived[0].astype(F32)).astype(BF16)
@@ -604,8 +617,7 @@
         return jnp.concatenate([mine, swap(theirs)], -1)
 
     chip_pixels = own_chip(pixels)
-    chip_mask = own_chip(band_mask)
-    chip_waves = own_chip(wavelengths)
+    chip_mask, chip_waves = own_chip(jnp.stack([band_mask, wavelengths], 1))
     picks = visible[0]
     slot_wave = (chip_waves[:, None] == jnp.arange(wave_count, dtype=jnp.int32)) & (
         chip_mask[:, None] > 0
@@ -629,7 +641,7 @@
         clock = middle.corner(clock)
         clock = back.plane(clock)
         clock = middle.pair(clock)
-        groups.append(middle.weights())
+        groups.append(middle.weights([enc_saved[5]]))
     w_enc_up, w_enc_down, w_proj = groups[1]
     enc_weights = (
         enc_vec[1], enc_vec[2], w_enc_qkv, w_enc_out, enc_vec[3], enc_vec[4], w_enc_up, w_enc_down
@@ -642,7 +654,7 @@
         clock, latent = tie(clock, latent)
         clock = back.corner(clock)
         clock = back.pair(clock)
-        groups.append(back.weights())
+        groups.append(back.weights([latent]))
     dec_vectors, w_dec_qkv, w_dec_out, w_dec_up, w_dec_down = groups[2]
     dec_vec = dec_vectors.T.astype(F32)
     dec_weights = (
@@ -657,9 +669,10 @@
         + hidden * dec_vec[0]
         + sincos(positions.astype(F32), latent.shape[1])
     )
-    dec_half, dec_saved = attn_half(inserted, *dec_weights[:4], HEADS_DEC, 1)
+    dec_half, dec_saved = attn_half(inserted, *dec_weights[:4], HEADS_DEC, 8)
     decoded, dec_saved = mlp_half(dec_half, dec_saved, *dec_weights[4:])
     grad_out = cotangent[0].astype(F32)
+    to_columns = jnp.eye(TILE, 2 * LANES, dtype=BF16)
     dec_branch, dec_upper, rest = mlp_backward(grad_out, dec_weights, dec_saved)
     grad_middle, dec_attn_branch, grad_attn, dec_norm_two = rest(dec_upper)
     dec_products = (
@@ -671,16 +684,13 @@
         early = Bucket(dec_products)
         grad_attn, early.send = tie(grad_attn, early.send)
         early.pair_hop()
-        dec_mixed = attn_backward(grad_attn, dec_saved, HEADS_DEC, 1, (0, 2))
+    dec_mixed = attn_backward(grad_attn, dec_saved, HEADS_DEC, 4)
+    if fast:
         dec_mixed, early.send = tie(dec_mixed, early.first_hop(dec_mixed))
-        dec_mixed = attn_backward(grad_attn, dec_saved, HEADS_DEC, 1, (1, 2), dec_mixed)
-        dec_mixed, early.send = tie(dec_mixed, early.second_hop(dec_mixed))
-    else:
-        dec_mixed = attn_backward(grad_attn, dec_saved, HEADS_DEC, 1)
     dec_mixed = dec_mixed.reshape(dec_saved[3].shape)
     grad_inserted, dec_norm_one = input_backward(grad_middle, dec_mixed, dec_weights, dec_saved)
     grad_mask = jnp.sum(grad_inserted * hidden, 0)
-    dec_vec_grads = columns((grad_mask, *dec_norm_one, *dec_norm_two), 2 * LANES).astype(BF16)
+    dec_vec_grads = vector_rows((grad_mask, *dec_norm_one, *dec_norm_two))
     grad_latent = dot(matches, grad_inserted.astype(BF16), 0, 0).astype(BF16)
     grad_encoded = dot(grad_latent, w_proj, 1, 1)
 
@@ -690,7 +700,7 @@
         (enc_saved[8], 0, enc_upper, 0),
     )
     if fast:
-        first = Bucket(first_products)
+        first = Bucket(first_products, [early.second_hop(enc_upper)])
         enc_upper, first.send = tie(enc_upper, first.send)
         first.pair_hop()
     grad_middle, enc_attn_branch, grad_attn, enc_norm_two = rest(enc_upper)
@@ -701,7 +711,7 @@
         (enc_saved[2], 0, enc_mixed, 1),
         (dec_saved[2], 0, dec_mixed, 1),
         (latent_in, 0, grad_latent, 0),
-        (None, None, dec_vec_grads, 0),
+        (dec_vec_grads, 0, to_columns, 0),
     )
     if fast:
         clock = first.first_hop(enc_mixed)
@@ -711,15 +721,13 @@
         enc_mixed, _ = tie(enc_mixed, second.send)
     grad_tokens, enc_norm_one = input_backward(grad_middle, enc_mixed, enc_weights, enc_saved)
     grad_loc_row = grad_tokens[1:2]
-    grad_loc = jnp.dot(grad_loc_row.T, time_loc, precision=lax.Precision.HIGHEST)
     grad_time = jnp.dot(grad_loc_row, loc_rows.T, precision=lax.Precision.HIGHEST)
-    enc_vec_grads = columns(
-        (grad_tokens[0], *enc_norm_one, *enc_norm_two, grad_loc), 2 * LANES
-    ).astype(BF16)
+    grad_loc = time_loc[0][:, None] * grad_loc_row
+    enc_vec_grads = vector_rows((grad_tokens[0], *enc_norm_one, *enc_norm_two, *grad_loc))
     grad_raw = (grad_tokens / band_count).astype(BF16)
     third_products = (
         (grad_raw, 0, wave_pixels, 0),
-        (None, None, enc_vec_grads, 0),
+        (enc_vec_grads, 0, to_columns, 0),
     )
     if fast:
         third = Bucket(third_products)
@@ -734,26 +742,25 @@
     ).astype(F32)
     if fast:
         clock = second.first_hop(grad_chip)
-        clock = early.fourth_hop(clock)
-        clock = first.second_hop(clock)
-        clock = third.first_hop(clock)
+        clock = first.second_hop(clock, [clock])
+        clock = third.first_hop(clock, [clock])
+        clock = early.fourth_hop(clock, [clock])
+        clock = first.third_hop(clock)
+        clock = second.second_hop(clock)
+        clock = third.second_hop(clock)
         early.arrived, clock = tie(early.arrived, clock)
         s_dec_down, s_dec_up, s_dec_out = early.finish()
-        grad_pixels, s_dec_up = tie(grad_pixels, s_dec_up)
-        clock = first.third_hop(s_dec_up)
-        clock = second.second_hop(clock)
-        clock = third.second_hop(clock)
         clock = first.fourth_hop(clock)
         clock = second.third_hop(clock)
         clock = third.third_hop(clock)
         clock = second.fourth_hop(clock)
-        clock = third.fourth_hop(clock)
+        clock = third.fourth_hop(clock, [s_dec_up])
         s_enc_down, s_enc_up = first.finish()
         second_sums = second.finish()
         third_sums = third.finish()
     else:
         whole = lambda products: scatter_sums([
-            right if left is None else dot(left, right, i, j).astype(BF16)
+            dot(left, right, i, j).astype(BF16)
             for left, i, right, j in products
         ], device_count)
         s_dec_down, s_dec_up, s_dec_out = whole(dec_products)

time: 507 us -> 481 us (0.949)
  waiting for transfers between devices: 127 us -> 99 us
  starting transfers between devices: 57.9 us -> 66.3 us
  Pallas kernels: 172 us -> 166 us
  matrix products: 60.2 us -> 66 us
    ppermute x3, waiting for transfers between devices: 17.3 us -> 4.11 us  [plane(): lax.ppermute(own, BOTH, SECOND_HOP)]
    ppermute x24 -> x23, starting transfers between devices: 18.8 us -> 27.9 us  [swap(): return lax.ppermute(array, 'band', [(0, 1), (1, 0)])]
    ppermute x12, waiting for transfers between devices: 42.8 us -> 35 us  [later_hop(): self.arrived = lax.ppermute(self.send, BOTH, pairs)]
    dot_general x23, matrix products: 58.7 us -> 64.5 us  [dot(): lax.dot_general(a, b, (((ca,), (cb,)), ((), ())), preferred_element_type=...]
    ppermute x4, waiting for transfers between devices: 10.6 us -> 5.4 us  [first_hop(): self.arrived = lax.ppermute(self.send, BOTH, FIRST_HOP)]
    unnamed x292 -> x274, local copies, waits for them, and re-layouts: 28.2 us -> 24.4 us
    pallas_call x3 -> x2, Pallas kernels: 49.2 us -> 47.6 us  [attend_backward(): pl.pallas_call(functools.partial(attend_backward_kernel, head_size=head_s...]
  transfers between devices with their start and end apart: 55 -> 54, of which waited for: 17 -> 15; matrix products, arithmetic and copies ran while one was open for 13% -> 18% of each run, Pallas kernels for 21% -> 23%
where the time goes in v4:
time: 481 us; the launch traced here: 474 us
  Pallas kernels  166 us (35%)
  waiting for transfers between devices  99 us (21%)
  starting transfers between devices  66.3 us (14%)
  matrix products  66 us (14%)
  local copies, waits for them, and re-layouts  49.2 us (10%)
  other arithmetic  24.2 us (5%)
    pallas_call x15, Pallas kernels, vmem_call(): pl.pallas_call(without(kernel, len(args), len(after)), in_specs=[pl.Block...  82 us
    dot_general x23, matrix products, dot(): lax.dot_general(a, b, (((ca,), (cb,)), ((), ())), preferred_element_type=...  64.5 us
    pallas_call x2, Pallas kernels, attend_backward(): pl.pallas_call(functools.partial(attend_backward_kernel, head_size=head_s...  47.6 us
    ppermute x12, waiting for transfers between devices, later_hop(): self.arrived = lax.ppermute(self.send, BOTH, pairs)  35 us
    pallas_call x2, Pallas kernels, attend_forward(): pl.pallas_call(functools.partial(attend_forward_kernel, head_size=head_si...  28.7 us
    ppermute x23, starting transfers between devices, swap(): return lax.ppermute(array, 'band', [(0, 1), (1, 0)])  27.9 us
    unnamed x274, local copies, waits for them, and re-layouts  24.4 us
    ppermute x3, waiting for transfers between devices, corner(): self.pieces.append(lax.ppermute(self.pieces[1], BOTH, FIRST_HOP))  24.1 us
  transfers between devices with their start and end apart: 54, of which 15 were waited for; matrix products, arithmetic and copies ran while one was open for 18% of the time, Pallas kernels for 23%

profile of v4, /device:TPU:1, one launch (start us, length us, event | category | flops | bytes accessed | tf_op | source)
XLA Modules:
  0.0 474.4 jit_solution(3585313060613957147)
XLA Ops:
  19.1 5.6 %multiply_sine_fusion = (f32[1024,256]{1,0:T(8,128)}, f32[1024,256]{1,0:T(8,128)}) fusion(f32[256]{0:T(256)S(1)} %multiply_exponential_fusion.1, f32[1024]{0:T(1024)S(1)} %iota_convert_fusion), kind=kLoop, calls=%fused_computation.47 | loop fusion | flops 262144 | bytes 2102272 | tf_op jit(solution)/shard_map/sin | solution.py:27
  30.2 11.5 %collective-permute-done.1 = bf16[48,3328]{1,0:T(8,128)(2,1)S(1)} collective-permute-done((bf16[48,3328]{1,0:T(8,128)(2,1)S(1)}, bf16[48,3328]{1,0:T(8,128)(2,1)S(1)}, u32[]{:S(2)}, u32[]{:S(2)}) %collective-permute-start.1) | collective-permute-done | bytes 319520 | tf_op jit(solution)/shard_map/ppermute | solution.py:413
  46.7 14.3 %collective-permute-done.3 = bf16[2,48,3328]{2,1,0:T(8,128)(2,1)S(1)} collective-permute-done((bf16[2,48,3328]{2,1,0:T(8,128)(2,1)S(1)}, bf16[2,48,3328]{2,1,0:T(8,128)(2,1)S(1)}, u32[]{:S(2)}, u32[]{:S(2)}) %collective-permute-start.3) | collective-permute-done | bytes 639008 | tf_op jit(solution)/shard_map/ppermute | solution.py:422
  64.5 5.0 %and.124 = pred[896,1024]{1,0:T(32,128)(4,1)} reshape(pred[14,64,16,64]{3,2,1,0:T(8,128)(4,1)S(1)} %broadcast_and_fusion) | data formatting | bytes 1835008 | tf_op jit(solution)/shard_map/and | solution.py:626
  75.5 4.1 collective-permute-done.6.refs_2_
  79.6 4.0 collective-permute-start.14
  90.4 6.5 %shard_map.442 = (bf16[4,4,48,1024]{3,2,1,0:T(8,128)(2,1)}, bf16[4,4,48,256]{3,2,1,0:T(8,128)(2,1)}, bf16[4,4,48,2304]{3,2,1,0:T(8,128)(2,1)}, bf16[4,4,48,768]{3,2,1,0:T(8,128)(2,1)}) custom-call(s32[9]{0:T(128)} %stack.187.refs_0_, bf16[4,48,2176]{2,1,0:T(8,128)(2,1)} %bitcast.10.refs_1_, bf16[4,48,2176]{2,1,0:T(8,128)(2,1)} %collective-permute-done.4.refs_2_, ...), custom_call_target="tpu_custom_call" | custom-call | tf_op jit(solution)/shard_map/pallas_call | solution.py:363
  102.4 14.3 %collective-permute-done.7.refs_4_ = bf16[4,48,3328]{2,1,0:T(8,128)(2,1)} collective-permute-done((bf16[4,48,3328]{2,1,0:T(8,128)(2,1)}, bf16[4,48,3328]{2,1,0:T(8,128)(2,1)}, u32[]{:S(2)}, u32[]{:S(2)}) %collective-permute-start.7) | collective-permute-done | bytes 1277984 | tf_op jit(solution)/shard_map/ppermute | solution.py:438
  126.9 9.8 %collective-permute-done.24.refs_4_ = bf16[4,32,3200]{2,1,0:T(8,128)(2,1)S(1)} collective-permute-done((bf16[4,32,3200]{2,1,0:T(8,128)(2,1)}, bf16[4,32,3200]{2,1,0:T(8,128)(2,1)S(1)}, u32[]{:S(2)}, u32[]{:S(2)}) %collective-permute-start.24) | collective-permute-done | bytes 819232 | tf_op jit(solution)/shard_map/ppermute | solution.py:438
  137.7 8.5 %shard_map.444 = (bf16[4,4,48,3072]{3,2,1,0:T(8,128)(2,1)}, bf16[4,4,192,768]{3,2,1,0:T(8,128)(2,1)}, bf16[4,4,48,512]{3,2,1,0:T(8,128)(2,1)}) custom-call(s32[9]{0:T(128)} %stack.187.refs_0_, bf16[4,48,3328]{2,1,0:T(8,128)(2,1)} %bitcast.175, bf16[4,48,3328]{2,1,0:T(8,128)(2,1)} %collective-permute-done.6.refs_2_, ...), custom_call_target="tpu_custom_call" | custom-call | tf_op jit(solution)/shard_map/pallas_call | solution.py:363
  146.3 6.1 %multiply_convert_fusion.1 = (bf16[256,3072]{1,0:T(8,128)(2,1)S(1)}, f32[256,3072]{1,0:T(8,128)}) fusion(bf16[256,768]{1,0:T(8,128)(2,1)S(1)} %add_convert_fusion.3.refs_3_, bf16[768,3072]{1,0:T(8,128)(2,1)} %bitcast.214), kind=kOutput, calls=%fused_computation.27 | convolution fusion | flops 1215037440 | bytes 9830400 | tf_op jit(solution)/shard_map/dot_general | solution.py:20
  157.5 6.3 %shard_map.445 = (bf16[4,4,32,256]{3,2,1,0:T(8,128)(2,1)}, bf16[4,4,32,1536]{3,2,1,0:T(8,128)(2,1)}, bf16[4,4,32,512]{3,2,1,0:T(8,128)(2,1)}, bf16[4,4,32,2048]{3,2,1,0:T(8,128)(2,1)}, bf16[4,4,128,512]{3,2,1,0:T(8,128)(2,1)}) custom-call(s32[9]{0:T(128)} %stack.187.refs_0_, bf16[4,32,3200]{2,1,0:T(8,128)(2,1)} %bitcast.25.refs_1_, ...), custom_call_target="tpu_custom_call" | custom-call | tf_op jit(solution)/shard_map/pallas_call | solution.py:363
  170.6 25.4 %shard_map.446 = (bf16[512,1024]{1,0:T(8,128)(2,1)S(1)}, f32[16,1,1024]{2,1,0:T(1,128)S(1)}) custom-call(bf16[1536,1024]{1,0:T(8,128)(2,1)S(1)} %convolution_convert_fusion.1.q_ref.k_ref.v_ref, bf16[1536,1024]{1,0:T(8,128)(2,1)S(1)} %convolution_convert_fusion.1.q_ref.k_ref.v_ref, bf16[1536,1024]{1,0:T(8,128)(2,1)S(1)} %convolution_convert_fusion.1.q_ref.k_ref.v_ref), custom_call_target="tpu_custom_call" | custom-call | tf_op jit(solution)/shard_map/pallas_call | solution.py:50
  199.6 5.3 %multiply_convert_fusion = (bf16[1024,2048]{1,0:T(8,128)(2,1)}, f32[1024,2048]{1,0:T(8,128)S(1)}) fusion(bf16[1024,512]{1,0:T(8,128)(2,1)S(1)} %add_convert_fusion.1.refs_3_, bf16[512,2048]{1,0:T(8,128)(2,1)S(1)} %bitcast.222), kind=kOutput, calls=%fused_computation.14 | convolution fusion | flops 2166358016 | bytes 15728640 | tf_op jit(solution)/shard_map/dot_general | solution.py:20
  204.9 7.4 %fusion.6.refs_4_ = bf16[1024,2048]{1,0:T(8,128)(2,1)S(1)} fusion(f32[1024,2048]{1,0:T(8,128)S(1)} %get-tuple-element.399, bf16[2048,512]{1,0:T(8,128)(2,1)S(1)} %bitcast.220, bf16[1,1024,512]{2,1,0:T(8,128)(2,1)S(1)} %copy-done.35), kind=kOutput, calls=%fused_computation.8 | convolution fusion | flops 2189426688 | bytes 15728640 | tf_op jit(solution)/shard_map/dot_general | solution.py:20
  219.5 8.7 %shard_map.447 = bf16[16,16,4608]{2,1,0:T(8,128)(2,1)} custom-call(s32[1]{0:T(128)} %bitcast.26.refs_0_, bf16[1024,2048]{1,0:T(8,128)(2,1)} %get-tuple-element.398.refs_1_, bf16[1024,512]{1,0:T(8,128)(2,1)} %bitcast.170, bf16[1024,512]{1,0:T(8,128)(2,1)} %copy-done.38, bf16[1024,2048]{1,0:T(8,128)(2,1)} %copy-done.34, bf16[512,1024]{1,0:T(8,128)(2,1)} %copy-done.5, ...), custom_call_target="tpu_custom_call" | custom-call | tf_op jit(solution)/shard_map/pallas_call | solution.py:363
  231.6 44.0 %shard_map.448 = bf16[3,512,1024]{2,1,0:T(8,128)(2,1)S(1)} custom-call(bf16[1536,1024]{1,0:T(8,128)(2,1)S(1)} %convolution_convert_fusion.1.q_ref.k_ref.v_ref, bf16[1536,1024]{1,0:T(8,128)(2,1)S(1)} %convolution_convert_fusion.1.q_ref.k_ref.v_ref, bf16[1536,1024]{1,0:T(8,128)(2,1)S(1)} %convolution_convert_fusion.1.q_ref.k_ref.v_ref, ...), custom_call_target="tpu_custom_call" | custom-call | tf_op jit(solution)/shard_map/pallas_call | solution.py:92
  275.6 10.3 %shard_map.449 = (bf16[8,16,4608]{2,1,0:T(8,128)(2,1)}, bf16[8,16,4608]{2,1,0:T(8,128)(2,1)}) custom-call(s32[17]{0:T(128)} %pad_add_fusion.1.refs_0_, bf16[1024,2048]{1,0:T(8,128)(2,1)} %get-tuple-element.398.refs_1_, bf16[1024,512]{1,0:T(8,128)(2,1)} %bitcast.171, bf16[1024,512]{1,0:T(8,128)(2,1)} %copy-done.38, bf16[1024,2048]{1,0:T(8,128)(2,1)} %copy-done.34, ...), custom_call_target="tpu_custom_call" | custom-call | tf_op jit(solution)/shard_map/pallas_call | solution.py:363
  287.2 4.8 %multiply_reduce_fusion.1 = (bf16[512]{0:T(512)(128)(2,1)}, f32[1024]{0:T(1024)S(1)}, f32[1024]{0:T(1024)S(1)}, bf16[512]{0:T(512)(128)(2,1)}, f32[1024,512]{1,0:T(8,128)S(1)}) fusion(f32[1024,512]{1,0:T(8,128)S(1)} %copy-done.26, f32[1024]{0:T(1024)S(1)} %add_rsqrt_fusion.1, f32[1024]{0:T(1024)S(1)} %broadcast_multiply_fusion.5, f32[512]{0:T(512)S(1)} %bitcast.193, ...), kind=kOutput, calls=%fused_computation.30 | convolution fusion | flops 1615328256 | bytes 8933376 | tf_op jit(solution)/shard_map/dot_general | solution.py:20
  295.5 7.3 %fusion.16.refs_4_ = bf16[256,3072]{1,0:T(8,128)(2,1)} fusion(f32[256,3072]{1,0:T(8,128)S(1)} %copy-done.129, bf16[256,768]{1,0:T(8,128)(2,1)S(1)} %get-tuple-element.402.refs_2_, bf16[3072,768]{1,0:T(8,128)(2,1)} %bitcast.216), kind=kOutput, calls=%fused_computation.26 | convolution fusion | flops 1223688192 | bytes 9830400 | tf_op jit(solution)/shard_map/dot_general | solution.py:20
  305.1 6.0 %shard_map.451 = bf16[16,16,9216]{2,1,0:T(8,128)(2,1)} custom-call(s32[1]{0:T(128)} %bitcast.26.refs_0_, bf16[256,3072]{1,0:T(8,128)(2,1)} %copy-done.40, bf16[256,768]{1,0:T(8,128)(2,1)} %copy-done.49, bf16[256,768]{1,0:T(8,128)(2,1)} %copy-done.48, bf16[256,3072]{1,0:T(8,128)(2,1)} %fusion.16.refs_4_, bf16[4,16,4608]{2,1,0:T(8,128)(2,1)} %copy-done.21), custom_call_target="tpu_custom_call" | custom-call | tf_op jit(solution)/shard_map/pallas_call | solution.py:363
  312.8 4.1 multiply_reduce_fusion.9
  318.7 3.6 shard_map.452
  323.3 6.8 %shard_map.455 = bf16[16,16,7168]{2,1,0:T(8,128)(2,1)} custom-call(s32[1]{0:T(128)} %bitcast.26.refs_0_, bf16[768,256]{1,0:T(8,128)(2,1)} %copy-done.9, bf16[256,768]{1,0:T(8,128)(2,1)} %copy-done.45, bf16[256,768]{1,0:T(8,128)(2,1)} %copy-done.46, bf16[2304,256]{1,0:T(8,128)(2,1)} %bitcast.167, bf16[1024,512]{1,0:T(8,128)(2,1)} %copy-done.37, ...), custom_call_target="tpu_custom_call" | custom-call | tf_op jit(solution)/shard_map/pallas_call | solution.py:363
  333.6 7.5 %shard_map.453 = (bf16[8,16,9216]{2,1,0:T(8,128)(2,1)}, bf16[8,16,9216]{2,1,0:T(8,128)(2,1)}) custom-call(s32[17]{0:T(128)} %pad_add_fusion.1.refs_0_, bf16[256,3072]{1,0:T(8,128)(2,1)} %copy-done.40, bf16[256,768]{1,0:T(8,128)(2,1)} %copy-done.49, bf16[256,768]{1,0:T(8,128)(2,1)} %copy-done.48, bf16[256,3072]{1,0:T(8,128)(2,1)} %fusion.16.refs_4_, ...), custom_call_target="tpu_custom_call" | custom-call | tf_op jit(solution)/shard_map/pallas_call | solution.py:363
  355.2 7.8 %shard_map.457 = (bf16[8,16,7168]{2,1,0:T(8,128)(2,1)}, bf16[8,16,7168]{2,1,0:T(8,128)(2,1)}) custom-call(s32[17]{0:T(128)} %pad_add_fusion.1.refs_0_, bf16[768,256]{1,0:T(8,128)(2,1)} %copy-done.9, bf16[256,768]{1,0:T(8,128)(2,1)} %copy-done.45, bf16[256,768]{1,0:T(8,128)(2,1)} %copy-done.46, bf16[2304,256]{1,0:T(8,128)(2,1)} %bitcast.168, ...), custom_call_target="tpu_custom_call" | custom-call | tf_op jit(solution)/shard_map/pallas_call | solution.py:363
  364.1 5.4 %collective-permute-done.35.refs_3_.refs_4_ = bf16[8,16,9216]{2,1,0:T(8,128)(2,1)S(1)} collective-permute-done((bf16[8,16,9216]{2,1,0:T(8,128)(2,1)}, bf16[8,16,9216]{2,1,0:T(8,128)(2,1)S(1)}, u32[]{:S(2)}, u32[]{:S(2)}) %collective-permute-start.35) | collective-permute-done | bytes 2359328 | tf_op jit(solution)/shard_map/ppermute | solution.py:531
  385.1 16.0 %collective-permute-done.39.refs_3_.refs_4_ = bf16[4,16,9216]{2,1,0:T(8,128)(2,1)S(1)} collective-permute-done((bf16[4,16,9216]{2,1,0:T(8,128)(2,1)}, bf16[4,16,9216]{2,1,0:T(8,128)(2,1)S(1)}, u32[]{:S(2)}, u32[]{:S(2)}) %collective-permute-start.39) | collective-permute-done | bytes 1179680 | tf_op jit(solution)/shard_map/ppermute | solution.py:543
  420.8 3.6 collective-permute-start.47
  429.7 5.5 %collective-permute-done.45.refs_3_.refs_4_ = bf16[2,16,7168]{2,1,0:T(8,128)(2,1)S(1)} collective-permute-done((bf16[2,16,7168]{2,1,0:T(8,128)(2,1)S(1)}, bf16[2,16,7168]{2,1,0:T(8,128)(2,1)S(1)}, u32[]{:S(2)}, u32[]{:S(2)}) %collective-permute-start.45) | collective-permute-done | bytes 458784 | tf_op jit(solution)/shard_map/ppermute | solution.py:543
  439.6 4.7 collective-permute-start.53
  448.4 8.9 %collective-permute-done.50 = bf16[1,16,7168]{2,1,0:T(8,128)(2,1)S(1)} collective-permute-done((bf16[1,16,7168]{2,1,0:T(8,128)(2,1)S(1)}, bf16[1,16,7168]{2,1,0:T(8,128)(2,1)S(1)}, u32[]{:S(2)}, u32[]{:S(2)}) %collective-permute-start.50) | collective-permute-done | bytes 229408 | tf_op jit(solution)/shard_map/ppermute | solution.py:543
  (518 shorter events, 182.1 us)
Async XLA Ops:
  8.5 33.5 %collective-permute-start.17 = (s32[2,7]{1,0:T(2,128)S(1)}, s32[2,7]{1,0:T(2,128)S(1)}, u32[]{:S(2)}, u32[]{:S(2)}) collective-permute-start(s32[2,7]{1,0:T(2,128)S(1)} %bitcast.202), channel_id=1, source_target_pairs={{0,1},{1,0},{2,3},{3,2},{4,5},{5,4},{6,7},{7,6},{8,9},{9,8},{10,11... | collective-permute-start | bytes 176 | tf_op jit(solution)/shard_map/ppermute | solution.py:183
  11.4 58.8 %collective-permute-start.16 = (bf16[254,448]{0,1:T(8,128)(2,1)}, bf16[254,448]{0,1:T(8,128)(2,1)}, u32[]{:S(2)}, u32[]{:S(2)}) collective-permute-start(bf16[254,448]{0,1:T(8,128)(2,1)} %get-tuple-element.377), channel_id=1, source_target_pairs={{0,1},{1,0},{2,3},{3,2},{4,5},{5,4},{6,7},{7,6},{8,9},{9,8},{10,11... | collective-permute-start | bytes 682760 | tf_op jit(solution)/shard_map/ppermute | solution.py:183
  24.7 17.1 %collective-permute-start.1 = (bf16[48,3328]{1,0:T(8,128)(2,1)S(1)}, bf16[48,3328]{1,0:T(8,128)(2,1)S(1)}, u32[]{:S(2)}, u32[]{:S(2)}) collective-permute-start(bf16[48,3328]{1,0:T(8,128)(2,1)S(1)} %constant_dynamic-update-slice_fusion), channel_id=1, source_target_pairs={{0,16},{1,17},{2,18},{3,19},{4,20},{5,21},{6,22},{7,23},{8,24},{9,... | collective-permute-start | bytes 958472 | tf_op jit(solution)/shard_map/ppermute | solution.py:413
  29.0 17.5 %collective-permute-start.4 = (bf16[4,48,2176]{2,1,0:T(8,128)(2,1)}, bf16[4,48,2176]{2,1,0:T(8,128)(2,1)}, u32[]{:S(2)}, u32[]{:S(2)}) collective-permute-start(bf16[4,48,2176]{2,1,0:T(8,128)(2,1)} %bitcast.10.refs_1_), channel_id=1, source_target_pairs={{0,2},{1,5},{2,0},{3,7},{4,6},{5,1},{6,4},{7,3},{8,10},{9,13},{10,... | collective-permute-start | bytes 2506760 | tf_op jit(solution)/shard_map/ppermute | solution.py:432
  41.9 19.1 %collective-permute-start.3 = (bf16[2,48,3328]{2,1,0:T(8,128)(2,1)S(1)}, bf16[2,48,3328]{2,1,0:T(8,128)(2,1)S(1)}, u32[]{:S(2)}, u32[]{:S(2)}) collective-permute-start(bf16[2,48,3328]{2,1,0:T(8,128)(2,1)S(1)} %pad_maximum_fusion.5), channel_id=1, source_target_pairs={{0,8},{1,9},{2,10},{3,11},{4,12},{5,13},{6,14},{7,15},{8,0},{9,1},... | collective-permute-start | bytes 1916936 | tf_op jit(solution)/shard_map/ppermute | solution.py:422
  42.8 32.1 %collective-permute-start.10 = (bf16[4,48,2176]{2,1,0:T(8,128)(2,1)}, bf16[4,48,2176]{2,1,0:T(8,128)(2,1)}, u32[]{:S(2)}, u32[]{:S(2)}) collective-permute-start(bf16[4,48,2176]{2,1,0:T(8,128)(2,1)} %bitcast.10.refs_1_), channel_id=1, source_target_pairs={{0,4},{1,3},{2,6},{3,1},{4,0},{5,7},{6,2},{7,5},{8,12},{9,11},{10,... | collective-permute-start | bytes 2506760 | tf_op jit(solution)/shard_map/ppermute | solution.py:432
  44.0 18.7 %collective-permute-start.8 = (bf16[32,3200]{1,0:T(8,128)(2,1)S(1)}, bf16[32,3200]{1,0:T(8,128)(2,1)S(1)}, u32[]{:S(2)}, u32[]{:S(2)}) collective-permute-start(bf16[32,3200]{1,0:T(8,128)(2,1)S(1)} %constant_dynamic-update-slice_fusion.1), channel_id=1, source_target_pairs={{0,16},{1,17},{2,18},{3,19},{4,20},{5,21},{6,22},{7,23},{8,24},{9,... | collective-permute-start | bytes 614408 | tf_op jit(solution)/shard_map/ppermute | solution.py:413
  46.5 28.5 %collective-permute-start.11 = (bf16[4,48,2176]{2,1,0:T(8,128)(2,1)}, bf16[4,48,2176]{2,1,0:T(8,128)(2,1)}, u32[]{:S(2)}, u32[]{:S(2)}) collective-permute-start(bf16[4,48,2176]{2,1,0:T(8,128)(2,1)} %collective-permute-done.4.refs_2_), channel_id=1, source_target_pairs={{0,4},{1,3},{2,6},{3,1},{4,0},{5,7},{6,2},{7,5},{8,12},{9,11},{10,... | collective-permute-start | bytes 2506760 | tf_op jit(solution)/shard_map/ppermute | solution.py:438
  61.3 18.3 %collective-permute-start.6 = (bf16[4,48,3328]{2,1,0:T(8,128)(2,1)S(1)}, bf16[4,48,3328]{2,1,0:T(8,128)(2,1)}, u32[]{:S(2)}, u32[]{:S(2)}) collective-permute-start(bf16[4,48,3328]{2,1,0:T(8,128)(2,1)S(1)} %bitcast.172), channel_id=1, source_target_pairs={{0,2},{1,5},{2,0},{3,7},{4,6},{5,1},{6,4},{7,3},{8,10},{9,13},{10,... | collective-permute-start | bytes 3833864 | tf_op jit(solution)/shard_map/ppermute | solution.py:432
  63.5 20.1 %collective-permute-start.9 = (bf16[2,32,3200]{2,1,0:T(8,128)(2,1)}, bf16[2,32,3200]{2,1,0:T(8,128)(2,1)}, u32[]{:S(2)}, u32[]{:S(2)}) collective-permute-start(bf16[2,32,3200]{2,1,0:T(8,128)(2,1)} %pad_maximum_fusion.7), channel_id=1, source_target_pairs={{0,8},{1,9},{2,10},{3,11},{4,12},{5,13},{6,14},{7,15},{8,0},{9,1},... | collective-permute-start | bytes 1228808 | tf_op jit(solution)/shard_map/ppermute | solution.py:422
  74.9 26.7 %collective-permute-start.5 = (bf16[4,48,3328]{2,1,0:T(8,128)(2,1)S(1)}, bf16[4,48,3328]{2,1,0:T(8,128)(2,1)}, u32[]{:S(2)}, u32[]{:S(2)}) collective-permute-start(bf16[4,48,3328]{2,1,0:T(8,128)(2,1)S(1)} %bitcast.173), channel_id=1, source_target_pairs={{0,4},{1,3},{2,6},{3,1},{4,0},{5,7},{6,2},{7,5},{8,12},{9,11},{10,... | collective-permute-start | bytes 3833864 | tf_op jit(solution)/shard_map/ppermute | solution.py:432
  85.8 51.3 %collective-permute-start.18 = (bf16[4,48,3328]{2,1,0:T(8,128)(2,1)S(1)}, bf16[4,48,3328]{2,1,0:T(8,128)(2,1)}, u32[]{:S(2)}, u32[]{:S(2)}) collective-permute-start(bf16[4,48,3328]{2,1,0:T(8,128)(2,1)S(1)} %bitcast.174), channel_id=1, source_target_pairs={{0,1},{1,0},{2,3},{3,2},{4,5},{5,4},{6,7},{7,6},{8,9},{9,8},{10,11... | collective-permute-start | bytes 3833864 | tf_op jit(solution)/shard_map/ppermute | solution.py:183
  86.4 30.3 %collective-permute-start.7 = (bf16[4,48,3328]{2,1,0:T(8,128)(2,1)}, bf16[4,48,3328]{2,1,0:T(8,128)(2,1)}, u32[]{:S(2)}, u32[]{:S(2)}) collective-permute-start(bf16[4,48,3328]{2,1,0:T(8,128)(2,1)} %collective-permute-done.6.refs_2_), channel_id=1, source_target_pairs={{0,4},{1,3},{2,6},{3,1},{4,0},{5,7},{6,2},{7,5},{8,12},{9,11},{10,... | collective-permute-start | bytes 3833864 | tf_op jit(solution)/shard_map/ppermute | solution.py:438
  88.2 28.5 %collective-permute-start.22 = (bf16[4,32,3200]{2,1,0:T(8,128)(2,1)}, bf16[4,32,3200]{2,1,0:T(8,128)(2,1)}, u32[]{:S(2)}, u32[]{:S(2)}) collective-permute-start(bf16[4,32,3200]{2,1,0:T(8,128)(2,1)} %bitcast.25.refs_1_), channel_id=1, source_target_pairs={{0,2},{1,5},{2,0},{3,7},{4,6},{5,1},{6,4},{7,3},{8,10},{9,13},{10,... | collective-permute-start | bytes 2457608 | tf_op jit(solution)/shard_map/ppermute | solution.py:432
  89.4 35.7 %collective-permute-start.23 = (bf16[4,32,3200]{2,1,0:T(8,128)(2,1)}, bf16[4,32,3200]{2,1,0:T(8,128)(2,1)}, u32[]{:S(2)}, u32[]{:S(2)}) collective-permute-start(bf16[4,32,3200]{2,1,0:T(8,128)(2,1)} %bitcast.25.refs_1_), channel_id=1, source_target_pairs={{0,4},{1,3},{2,6},{3,1},{4,0},{5,7},{6,2},{7,5},{8,12},{9,11},{10,... | collective-permute-start | bytes 2457608 | tf_op jit(solution)/shard_map/ppermute | solution.py:432
  101.7 35.5 %collective-permute-start.19 = (bf16[4,48,3328]{2,1,0:T(8,128)(2,1)}, bf16[4,48,3328]{2,1,0:T(8,128)(2,1)}, u32[]{:S(2)}, u32[]{:S(2)}) collective-permute-start(bf16[4,48,3328]{2,1,0:T(8,128)(2,1)} %collective-permute-done.6.refs_2_), channel_id=1, source_target_pairs={{0,1},{1,0},{2,3},{3,2},{4,5},{5,4},{6,7},{7,6},{8,9},{9,8},{10,11... | collective-permute-start | bytes 3833864 | tf_op jit(solution)/shard_map/ppermute | solution.py:183
  116.7 20.9 %collective-permute-start.20 = (bf16[4,48,3328]{2,1,0:T(8,128)(2,1)}, bf16[4,48,3328]{2,1,0:T(8,128)(2,1)}, u32[]{:S(2)}, u32[]{:S(2)}) collective-permute-start(bf16[4,48,3328]{2,1,0:T(8,128)(2,1)} %collective-permute-done.5.refs_3_), channel_id=1, source_target_pairs={{0,1},{1,0},{2,3},{3,2},{4,5},{5,4},{6,7},{7,6},{8,9},{9,8},{10,11... | collective-permute-start | bytes 3833864 | tf_op jit(solution)/shard_map/ppermute | solution.py:183
  116.7 21.0 %collective-permute-start.21 = (bf16[4,48,3328]{2,1,0:T(8,128)(2,1)}, bf16[4,48,3328]{2,1,0:T(8,128)(2,1)}, u32[]{:S(2)}, u32[]{:S(2)}) collective-permute-start(bf16[4,48,3328]{2,1,0:T(8,128)(2,1)} %collective-permute-done.7.refs_4_), channel_id=1, source_target_pairs={{0,1},{1,0},{2,3},{3,2},{4,5},{5,4},{6,7},{7,6},{8,9},{9,8},{10,11... | collective-permute-start | bytes 3833864 | tf_op jit(solution)/shard_map/ppermute | solution.py:183
  136.7 18.5 %collective-permute-start.25 = (bf16[4,32,3200]{2,1,0:T(8,128)(2,1)}, bf16[4,32,3200]{2,1,0:T(8,128)(2,1)S(1)}, u32[]{:S(2)}, u32[]{:S(2)}) collective-permute-start(bf16[4,32,3200]{2,1,0:T(8,128)(2,1)} %bitcast.25.refs_1_), channel_id=1, source_target_pairs={{0,1},{1,0},{2,3},{3,2},{4,5},{5,4},{6,7},{7,6},{8,9},{9,8},{10,11... | collective-permute-start | bytes 2457608 | tf_op jit(solution)/shard_map/ppermute | solution.py:183
  137.1 18.1 %collective-permute-start.26 = (bf16[4,32,3200]{2,1,0:T(8,128)(2,1)}, bf16[4,32,3200]{2,1,0:T(8,128)(2,1)S(1)}, u32[]{:S(2)}, u32[]{:S(2)}) collective-permute-start(bf16[4,32,3200]{2,1,0:T(8,128)(2,1)} %collective-permute-done.22.refs_2_), channel_id=1, source_target_pairs={{0,1},{1,0},{2,3},{3,2},{4,5},{5,4},{6,7},{7,6},{8,9},{9,8},{10,11... | collective-permute-start | bytes 2457608 | tf_op jit(solution)/shard_map/ppermute | solution.py:183
  137.2 18.0 %collective-permute-start.27 = (bf16[4,32,3200]{2,1,0:T(8,128)(2,1)}, bf16[4,32,3200]{2,1,0:T(8,128)(2,1)S(1)}, u32[]{:S(2)}, u32[]{:S(2)}) collective-permute-start(bf16[4,32,3200]{2,1,0:T(8,128)(2,1)} %collective-permute-done.23.refs_3_), channel_id=1, source_target_pairs={{0,1},{1,0},{2,3},{3,2},{4,5},{5,4},{6,7},{7,6},{8,9},{9,8},{10,11... | collective-permute-start | bytes 2457608 | tf_op jit(solution)/shard_map/ppermute | solution.py:183
  137.6 17.6 %collective-permute-start.28 = (bf16[4,32,3200]{2,1,0:T(8,128)(2,1)S(1)}, bf16[4,32,3200]{2,1,0:T(8,128)(2,1)S(1)}, u32[]{:S(2)}, u32[]{:S(2)}) collective-permute-start(bf16[4,32,3200]{2,1,0:T(8,128)(2,1)S(1)} %collective-permute-done.24.refs_4_), channel_id=1, source_target_pairs={{0,1},{1,0},{2,3},{3,2},{4,5},{5,4},{6,7},{7,6},{8,9},{9,8},{10,11... | collective-permute-start | bytes 2457608 | tf_op jit(solution)/shard_map/ppermute | solution.py:183
  228.2 47.5 %collective-permute-start.29 = (bf16[16,16,4608]{2,1,0:T(8,128)(2,1)}, bf16[16,16,4608]{2,1,0:T(8,128)(2,1)}, u32[]{:S(2)}, u32[]{:S(2)}) collective-permute-start(bf16[16,16,4608]{2,1,0:T(8,128)(2,1)} %shard_map.447), channel_id=1, source_target_pairs={{0,1},{1,0},{2,3},{3,2},{4,5},{5,4},{6,7},{7,6},{8,9},{9,8},{10,11... | collective-permute-start | bytes 7077896 | tf_op jit(solution)/shard_map/ppermute | solution.py:183
  311.1 22.5 %collective-permute-start.32 = (bf16[16,16,9216]{2,1,0:T(8,128)(2,1)}, bf16[16,16,9216]{2,1,0:T(8,128)(2,1)}, u32[]{:S(2)}, u32[]{:S(2)}) collective-permute-start(bf16[16,16,9216]{2,1,0:T(8,128)(2,1)} %shard_map.451), channel_id=1, source_target_pairs={{0,1},{1,0},{2,3},{3,2},{4,5},{5,4},{6,7},{7,6},{8,9},{9,8},{10,11... | collective-permute-start | bytes 14155784 | tf_op jit(solution)/shard_map/ppermute | solution.py:183
  330.1 25.1 %collective-permute-start.36 = (bf16[16,16,7168]{2,1,0:T(8,128)(2,1)}, bf16[16,16,7168]{2,1,0:T(8,128)(2,1)}, u32[]{:S(2)}, u32[]{:S(2)}) collective-permute-start(bf16[16,16,7168]{2,1,0:T(8,128)(2,1)} %shard_map.455), channel_id=1, source_target_pairs={{0,1},{1,0},{2,3},{3,2},{4,5},{5,4},{6,7},{7,6},{8,9},{9,8},{10,11... | collective-permute-start | bytes 11010056 | tf_op jit(solution)/shard_map/ppermute | solution.py:183
  341.2 28.3 %collective-permute-start.35 = (bf16[8,16,9216]{2,1,0:T(8,128)(2,1)}, bf16[8,16,9216]{2,1,0:T(8,128)(2,1)S(1)}, u32[]{:S(2)}, u32[]{:S(2)}) collective-permute-start(bf16[8,16,9216]{2,1,0:T(8,128)(2,1)} %get-tuple-element.170), channel_id=1, source_target_pairs={{0,4},{1,3},{2,6},{3,1},{4,0},{5,7},{6,2},{7,5},{8,12},{9,11},{10,... | collective-permute-start | bytes 7077896 | tf_op jit(solution)/shard_map/ppermute | solution.py:531
  362.9 40.2 %collective-permute-start.38 = (bf16[8,16,7168]{2,1,0:T(8,128)(2,1)}, bf16[8,16,7168]{2,1,0:T(8,128)(2,1)}, u32[]{:S(2)}, u32[]{:S(2)}) collective-permute-start(bf16[8,16,7168]{2,1,0:T(8,128)(2,1)} %get-tuple-element.178.refs_5_), channel_id=1, source_target_pairs={{0,4},{1,3},{2,6},{3,1},{4,0},{5,7},{6,2},{7,5},{8,12},{9,11},{10,... | collective-permute-start | bytes 5505032 | tf_op jit(solution)/shard_map/ppermute | solution.py:531
  372.7 28.4 %collective-permute-start.39 = (bf16[4,16,9216]{2,1,0:T(8,128)(2,1)}, bf16[4,16,9216]{2,1,0:T(8,128)(2,1)S(1)}, u32[]{:S(2)}, u32[]{:S(2)}) collective-permute-start(bf16[4,16,9216]{2,1,0:T(8,128)(2,1)} %get-tuple-element.180.refs_6_), channel_id=1, source_target_pairs={{0,2},{1,5},{2,0},{3,7},{4,6},{5,1},{6,4},{7,3},{8,10},{9,13},{10,... | collective-permute-start | bytes 3538952 | tf_op jit(solution)/shard_map/ppermute | solution.py:543
  380.8 34.6 %collective-permute-start.37 = (bf16[8,16,1920]{2,1,0:T(8,128)(2,1)}, bf16[8,16,1920]{2,1,0:T(8,128)(2,1)S(1)}, u32[]{:S(2)}, u32[]{:S(2)}) collective-permute-start(bf16[8,16,1920]{2,1,0:T(8,128)(2,1)} %get-tuple-element.183.refs_5_), channel_id=1, source_target_pairs={{0,4},{1,3},{2,6},{3,1},{4,0},{5,7},{6,2},{7,5},{8,12},{9,11},{10,... | collective-permute-start | bytes 1474568 | tf_op jit(solution)/shard_map/ppermute | solution.py:531
  412.6 45.7 %collective-permute-start.33 = (bf16[254,448]{1,0:T(8,128)(2,1)S(1)}, bf16[254,448]{1,0:T(8,128)(2,1)S(1)}, u32[]{:S(2)}, u32[]{:S(2)}) collective-permute-start(bf16[254,448]{1,0:T(8,128)(2,1)S(1)} %get-tuple-element.375), channel_id=1, source_target_pairs={{0,1},{1,0},{2,3},{3,2},{4,5},{5,4},{6,7},{7,6},{8,9},{9,8},{10,11... | collective-permute-start | bytes 682760 | tf_op jit(solution)/shard_map/ppermute | solution.py:183
  416.9 22.6 %collective-permute-start.52 = (bf16[1,16,9216]{2,1,0:T(8,128)(2,1)S(1)}, bf16[1,16,9216]{2,1,0:T(8,128)(2,1)S(1)}, u32[]{:S(2)}, u32[]{:S(2)}) collective-permute-start(bf16[1,16,9216]{2,1,0:T(8,128)(2,1)S(1)} %get-tuple-element.198), channel_id=1, source_target_pairs={{0,16},{1,17},{2,18},{3,19},{4,20},{5,21},{6,22},{7,23},{8,24},{9,... | collective-permute-start | bytes 884744 | tf_op jit(solution)/shard_map/ppermute | solution.py:543
  439.6 20.1 %collective-permute-start.53 = (bf16[16,9216]{1,0:T(8,128)(2,1)S(1)}, bf16[16,9216]{1,0:T(8,128)(2,1)S(1)}, u32[]{:S(2)}, u32[]{:S(2)}) collective-permute-start(bf16[16,9216]{1,0:T(8,128)(2,1)S(1)} %fusion.29.refs_1_), channel_id=1, source_target_pairs={{0,1},{1,0},{2,3},{3,2},{4,5},{5,4},{6,7},{7,6},{8,9},{9,8},{10,11... | collective-permute-start | bytes 884744 | tf_op jit(solution)/shard_map/ppermute | solution.py:183
  (152 other events, 1248.6 us)

commit v5 on v4

--- a/solution.py
+++ b/solution.py
@@ -142,7 +142,7 @@
     upper = dot(normed_two, w_up, 1, 0)
     active = gelu_tanh(upper).astype(BF16)
     rows_out = middle + dot(active, w_down, 1, 0)
-    return rows_out, saved + (unit_two, inverse_two, normed_two, upper, active)
+    return rows_out, saved + (unit_two, inverse_two, normed_two, upper.astype(BF16), active)
 
 
 def mlp_backward(grad_out, weights, saved):
@@ -150,7 +150,7 @@
     unit_two, inverse_two, upper = saved[6], saved[7], saved[9]
     grad_branch = grad_out.astype(BF16)
     grad_active = dot(grad_branch, w_down, 1, 1)
-    grad_upper = jax.vjp(gelu_tanh, upper)[1](grad_active)[0].astype(BF16)
+    grad_upper = jax.vjp(gelu_tanh, upper.astype(F32))[1](grad_active)[0].astype(BF16)
 
     def rest(grad_upper):
         grad_normed = dot(grad_upper, w_up, 1, 1)

time: 481 us -> 496 us (1.031)
  waiting for transfers between devices: 99 us -> 119 us
  starting transfers between devices: 66.3 us -> 61.2 us
    ppermute x3, waiting for transfers between devices: 1.71 us -> 10.1 us  [plane(): lax.ppermute(own, BOTH, FIRST_HOP)]
    ppermute x3, waiting for transfers between devices: 24.1 us -> 31.1 us  [corner(): self.pieces.append(lax.ppermute(self.pieces[1], BOTH, FIRST_HOP))]
    ppermute x12, starting transfers between devices: 15.2 us -> 10.1 us  [later_hop(): self.arrived = lax.ppermute(self.send, BOTH, pairs)]
  transfers between devices with their start and end apart: 54 -> 54, of which waited for: 15 -> 17; matrix products, arithmetic and copies ran while one was open for 18% -> 18% of each run, Pallas kernels for 23% -> 22%
where the time goes in v5:
time: 496 us; the launch traced here: 489 us
  Pallas kernels  166 us (33%)
  waiting for transfers between devices  119 us (24%)
  matrix products  65.9 us (13%)
  starting transfers between devices  61.2 us (12%)
  local copies, waits for them, and re-layouts  49.2 us (10%)
  other arithmetic  24.4 us (5%)
    pallas_call x15, Pallas kernels, vmem_call(): pl.pallas_call(without(kernel, len(args), len(after)), in_specs=[pl.Block...  82.1 us
    dot_general x23, matrix products, dot(): lax.dot_general(a, b, (((ca,), (cb,)), ((), ())), preferred_element_type=...  64.3 us
    pallas_call x2, Pallas kernels, attend_backward(): pl.pallas_call(functools.partial(attend_backward_kernel, head_size=head_s...  47.6 us
    ppermute x12, waiting for transfers between devices, later_hop(): self.arrived = lax.ppermute(self.send, BOTH, pairs)  35.3 us
    ppermute x3, waiting for transfers between devices, corner(): self.pieces.append(lax.ppermute(self.pieces[1], BOTH, FIRST_HOP))  31.1 us
    pallas_call x2, Pallas kernels, attend_forward(): pl.pallas_call(functools.partial(attend_forward_kernel, head_size=head_si...  28.7 us
    ppermute x23, starting transfers between devices, swap(): return lax.ppermute(array, 'band', [(0, 1), (1, 0)])  28.1 us
    unnamed x274, local copies, waits for them, and re-layouts  24.4 us
  transfers between devices with their start and end apart: 54, of which 17 were waited for; matrix products, arithmetic and copies ran while one was open for 18% of the time, Pallas kernels for 22%

profile of v5, /device:TPU:1, one launch (start us, length us, event | category | flops | bytes accessed | tf_op | source)
XLA Modules:
  0.0 489.4 jit_solution(14127625322672305123)
XLA Ops:
  15.2 4.1 collective-permute-done
  20.7 5.6 %multiply_sine_fusion = (f32[1024,256]{1,0:T(8,128)}, f32[1024,256]{1,0:T(8,128)}) fusion(f32[256]{0:T(256)S(1)} %multiply_exponential_fusion.1, f32[1024]{0:T(1024)S(1)} %iota_convert_fusion), kind=kLoop, calls=%fused_computation.68 | loop fusion | flops 262144 | bytes 2102272 | tf_op jit(solution)/shard_map/sin | solution.py:27
  32.2 11.3 %collective-permute-done.1 = bf16[48,3328]{1,0:T(8,128)(2,1)S(1)} collective-permute-done((bf16[48,3328]{1,0:T(8,128)(2,1)S(1)}, bf16[48,3328]{1,0:T(8,128)(2,1)S(1)}, u32[]{:S(2)}, u32[]{:S(2)}) %collective-permute-start.1) | collective-permute-done | bytes 319520 | tf_op jit(solution)/shard_map/ppermute | solution.py:413
  49.0 13.7 %collective-permute-done.3 = bf16[2,48,3328]{2,1,0:T(8,128)(2,1)S(1)} collective-permute-done((bf16[2,48,3328]{2,1,0:T(8,128)(2,1)S(1)}, bf16[2,48,3328]{2,1,0:T(8,128)(2,1)S(1)}, u32[]{:S(2)}, u32[]{:S(2)}) %collective-permute-start.3) | collective-permute-done | bytes 639008 | tf_op jit(solution)/shard_map/ppermute | solution.py:422
  66.3 5.0 %and.124 = pred[896,1024]{1,0:T(32,128)(4,1)} reshape(pred[14,64,16,64]{3,2,1,0:T(8,128)(4,1)S(1)} %broadcast_and_fusion) | data formatting | bytes 1835008 | tf_op jit(solution)/shard_map/and | solution.py:626
  76.4 5.1 %collective-permute-done.6.refs_2_ = bf16[4,48,3328]{2,1,0:T(8,128)(2,1)} collective-permute-done((bf16[4,48,3328]{2,1,0:T(8,128)(2,1)S(1)}, bf16[4,48,3328]{2,1,0:T(8,128)(2,1)}, u32[]{:S(2)}, u32[]{:S(2)}) %collective-permute-start.6) | collective-permute-done | bytes 1277984 | tf_op jit(solution)/shard_map/ppermute | solution.py:432
  88.8 6.5 %shard_map.442 = (bf16[4,4,48,1024]{3,2,1,0:T(8,128)(2,1)}, bf16[4,4,48,256]{3,2,1,0:T(8,128)(2,1)}, bf16[4,4,48,2304]{3,2,1,0:T(8,128)(2,1)}, bf16[4,4,48,768]{3,2,1,0:T(8,128)(2,1)}) custom-call(s32[9]{0:T(128)} %stack.187.refs_0_, bf16[4,48,2176]{2,1,0:T(8,128)(2,1)} %bitcast.10.refs_1_, bf16[4,48,2176]{2,1,0:T(8,128)(2,1)} %collective-permute-done.4.refs_2_, ...), custom_call_target="tpu_custom_call" | custom-call | tf_op jit(solution)/shard_map/pallas_call | solution.py:363
  100.1 10.1 %collective-permute-done.5.refs_3_ = bf16[4,48,3328]{2,1,0:T(8,128)(2,1)} collective-permute-done((bf16[4,48,3328]{2,1,0:T(8,128)(2,1)S(1)}, bf16[4,48,3328]{2,1,0:T(8,128)(2,1)}, u32[]{:S(2)}, u32[]{:S(2)}) %collective-permute-start.5) | collective-permute-done | bytes 1277984 | tf_op jit(solution)/shard_map/ppermute | solution.py:432
  111.5 21.1 %collective-permute-done.7.refs_4_ = bf16[4,48,3328]{2,1,0:T(8,128)(2,1)} collective-permute-done((bf16[4,48,3328]{2,1,0:T(8,128)(2,1)}, bf16[4,48,3328]{2,1,0:T(8,128)(2,1)}, u32[]{:S(2)}, u32[]{:S(2)}) %collective-permute-start.7) | collective-permute-done | bytes 1277984 | tf_op jit(solution)/shard_map/ppermute | solution.py:438
  142.0 10.0 %collective-permute-done.24.refs_4_ = bf16[4,32,3200]{2,1,0:T(8,128)(2,1)S(1)} collective-permute-done((bf16[4,32,3200]{2,1,0:T(8,128)(2,1)}, bf16[4,32,3200]{2,1,0:T(8,128)(2,1)S(1)}, u32[]{:S(2)}, u32[]{:S(2)}) %collective-permute-start.24) | collective-permute-done | bytes 819232 | tf_op jit(solution)/shard_map/ppermute | solution.py:438
  154.0 8.5 %shard_map.444 = (bf16[4,4,48,3072]{3,2,1,0:T(8,128)(2,1)}, bf16[4,4,192,768]{3,2,1,0:T(8,128)(2,1)}, bf16[4,4,48,512]{3,2,1,0:T(8,128)(2,1)}) custom-call(s32[9]{0:T(128)} %stack.187.refs_0_, bf16[4,48,3328]{2,1,0:T(8,128)(2,1)} %bitcast.171, bf16[4,48,3328]{2,1,0:T(8,128)(2,1)} %collective-permute-done.6.refs_2_, ...), custom_call_target="tpu_custom_call" | custom-call | tf_op jit(solution)/shard_map/pallas_call | solution.py:363
  162.6 5.7 %fusion.29 = (bf16[256,3072]{1,0:T(8,128)(2,1)S(1)}, bf16[256,3072]{1,0:T(8,128)(2,1)}) fusion(bf16[256,768]{1,0:T(8,128)(2,1)S(1)} %add_convert_fusion.3.refs_3_, bf16[768,3072]{1,0:T(8,128)(2,1)} %bitcast.210), kind=kOutput, calls=%fused_computation.43 | convolution fusion | flops 1215823872 | bytes 8257536 | tf_op jit(solution)/shard_map/dot_general | solution.py:20
  173.4 6.3 %shard_map.445 = (bf16[4,4,32,256]{3,2,1,0:T(8,128)(2,1)}, bf16[4,4,32,1536]{3,2,1,0:T(8,128)(2,1)}, bf16[4,4,32,512]{3,2,1,0:T(8,128)(2,1)}, bf16[4,4,32,2048]{3,2,1,0:T(8,128)(2,1)}, bf16[4,4,128,512]{3,2,1,0:T(8,128)(2,1)}) custom-call(s32[9]{0:T(128)} %stack.187.refs_0_, bf16[4,32,3200]{2,1,0:T(8,128)(2,1)} %bitcast.25.refs_1_, ...), custom_call_target="tpu_custom_call" | custom-call | tf_op jit(solution)/shard_map/pallas_call | solution.py:363
  186.5 25.4 %shard_map.446 = (bf16[512,1024]{1,0:T(8,128)(2,1)S(1)}, f32[16,1,1024]{2,1,0:T(1,128)S(1)}) custom-call(bf16[1536,1024]{1,0:T(8,128)(2,1)S(1)} %convolution_convert_fusion.1.q_ref.k_ref.v_ref, bf16[1536,1024]{1,0:T(8,128)(2,1)S(1)} %convolution_convert_fusion.1.q_ref.k_ref.v_ref, bf16[1536,1024]{1,0:T(8,128)(2,1)S(1)} %convolution_convert_fusion.1.q_ref.k_ref.v_ref), custom_call_target="tpu_custom_call" | custom-call | tf_op jit(solution)/shard_map/pallas_call | solution.py:50
  215.5 5.3 %fusion.11 = (bf16[1024,2048]{1,0:T(8,128)(2,1)}, bf16[1024,2048]{1,0:T(8,128)(2,1)S(1)}) fusion(bf16[1024,512]{1,0:T(8,128)(2,1)S(1)} %add_convert_fusion.1.refs_3_, bf16[512,2048]{1,0:T(8,128)(2,1)S(1)} %bitcast.218), kind=kOutput, calls=%fused_computation.16 | convolution fusion | flops 2168455168 | bytes 11534336 | tf_op jit(solution)/shard_map/dot_general | solution.py:20
  220.9 7.6 %fusion.3.refs_4_ = bf16[1024,2048]{1,0:T(8,128)(2,1)S(1)} fusion(bf16[1024,2048]{1,0:T(8,128)(2,1)S(1)} %get-tuple-element.399, bf16[2048,512]{1,0:T(8,128)(2,1)S(1)} %bitcast.216, bf16[1,1024,512]{2,1,0:T(8,128)(2,1)S(1)} %copy-done.35), kind=kOutput, calls=%fused_computation.8 | convolution fusion | flops 2191523840 | bytes 11534336 | tf_op jit(solution)/shard_map/dot_general | solution.py:20
  235.6 8.8 %shard_map.447 = bf16[16,16,4608]{2,1,0:T(8,128)(2,1)} custom-call(s32[1]{0:T(128)} %bitcast.26.refs_0_, bf16[1024,2048]{1,0:T(8,128)(2,1)} %get-tuple-element.398.refs_1_, bf16[1024,512]{1,0:T(8,128)(2,1)} %bitcast.166, bf16[1024,512]{1,0:T(8,128)(2,1)} %copy-done.38, bf16[1024,2048]{1,0:T(8,128)(2,1)} %copy-done.34, bf16[512,1024]{1,0:T(8,128)(2,1)} %copy-done.5, ...), custom_call_target="tpu_custom_call" | custom-call | tf_op jit(solution)/shard_map/pallas_call | solution.py:363
  247.9 44.0 %shard_map.448 = bf16[3,512,1024]{2,1,0:T(8,128)(2,1)S(1)} custom-call(bf16[1536,1024]{1,0:T(8,128)(2,1)S(1)} %convolution_convert_fusion.1.q_ref.k_ref.v_ref, bf16[1536,1024]{1,0:T(8,128)(2,1)S(1)} %convolution_convert_fusion.1.q_ref.k_ref.v_ref, bf16[1536,1024]{1,0:T(8,128)(2,1)S(1)} %convolution_convert_fusion.1.q_ref.k_ref.v_ref, ...), custom_call_target="tpu_custom_call" | custom-call | tf_op jit(solution)/shard_map/pallas_call | solution.py:92
  291.9 10.3 %shard_map.449 = (bf16[8,16,4608]{2,1,0:T(8,128)(2,1)}, bf16[8,16,4608]{2,1,0:T(8,128)(2,1)}) custom-call(s32[17]{0:T(128)} %pad_add_fusion.1.refs_0_, bf16[1024,2048]{1,0:T(8,128)(2,1)} %get-tuple-element.398.refs_1_, bf16[1024,512]{1,0:T(8,128)(2,1)} %bitcast.167, bf16[1024,512]{1,0:T(8,128)(2,1)} %copy-done.38, bf16[1024,2048]{1,0:T(8,128)(2,1)} %copy-done.34, ...), custom_call_target="tpu_custom_call" | custom-call | tf_op jit(solution)/shard_map/pallas_call | solution.py:363
  303.6 4.8 multiply_reduce_fusion.1
  311.9 7.3 %fusion.21.refs_4_ = bf16[256,3072]{1,0:T(8,128)(2,1)} fusion(bf16[256,3072]{1,0:T(8,128)(2,1)S(1)} %copy-done.129, bf16[256,768]{1,0:T(8,128)(2,1)S(1)} %get-tuple-element.402.refs_2_, bf16[3072,768]{1,0:T(8,128)(2,1)} %bitcast.212), kind=kOutput, calls=%fused_computation.35 | convolution fusion | flops 1224474624 | bytes 8257536 | tf_op jit(solution)/shard_map/dot_general | solution.py:20
  321.5 6.0 %shard_map.451 = bf16[16,16,9216]{2,1,0:T(8,128)(2,1)} custom-call(s32[1]{0:T(128)} %bitcast.26.refs_0_, bf16[256,3072]{1,0:T(8,128)(2,1)} %copy-done.40, bf16[256,768]{1,0:T(8,128)(2,1)} %copy-done.49, bf16[256,768]{1,0:T(8,128)(2,1)} %copy-done.48, bf16[256,3072]{1,0:T(8,128)(2,1)} %fusion.21.refs_4_, bf16[4,16,4608]{2,1,0:T(8,128)(2,1)} %copy-done.21), custom_call_target="tpu_custom_call" | custom-call | tf_op jit(solution)/shard_map/pallas_call | solution.py:363
  329.1 4.1 multiply_reduce_fusion.9
  339.7 6.8 %shard_map.455 = bf16[16,16,7168]{2,1,0:T(8,128)(2,1)} custom-call(s32[1]{0:T(128)} %bitcast.26.refs_0_, bf16[768,256]{1,0:T(8,128)(2,1)} %copy-done.9, bf16[256,768]{1,0:T(8,128)(2,1)} %copy-done.45, bf16[256,768]{1,0:T(8,128)(2,1)} %copy-done.46, bf16[2304,256]{1,0:T(8,128)(2,1)} %bitcast.163, bf16[1024,512]{1,0:T(8,128)(2,1)} %copy-done.37, ...), custom_call_target="tpu_custom_call" | custom-call | tf_op jit(solution)/shard_map/pallas_call | solution.py:363
  350.0 7.5 %shard_map.453 = (bf16[8,16,9216]{2,1,0:T(8,128)(2,1)}, bf16[8,16,9216]{2,1,0:T(8,128)(2,1)}) custom-call(s32[17]{0:T(128)} %pad_add_fusion.1.refs_0_, bf16[256,3072]{1,0:T(8,128)(2,1)} %copy-done.40, bf16[256,768]{1,0:T(8,128)(2,1)} %copy-done.49, bf16[256,768]{1,0:T(8,128)(2,1)} %copy-done.48, bf16[256,3072]{1,0:T(8,128)(2,1)} %fusion.21.refs_4_, ...), custom_call_target="tpu_custom_call" | custom-call | tf_op jit(solution)/shard_map/pallas_call | solution.py:363
  371.6 7.8 %shard_map.457 = (bf16[8,16,7168]{2,1,0:T(8,128)(2,1)}, bf16[8,16,7168]{2,1,0:T(8,128)(2,1)}) custom-call(s32[17]{0:T(128)} %pad_add_fusion.1.refs_0_, bf16[768,256]{1,0:T(8,128)(2,1)} %copy-done.9, bf16[256,768]{1,0:T(8,128)(2,1)} %copy-done.45, bf16[256,768]{1,0:T(8,128)(2,1)} %copy-done.46, bf16[2304,256]{1,0:T(8,128)(2,1)} %bitcast.164, ...), custom_call_target="tpu_custom_call" | custom-call | tf_op jit(solution)/shard_map/pallas_call | solution.py:363
  380.5 5.4 %collective-permute-done.35.refs_3_.refs_4_ = bf16[8,16,9216]{2,1,0:T(8,128)(2,1)S(1)} collective-permute-done((bf16[8,16,9216]{2,1,0:T(8,128)(2,1)}, bf16[8,16,9216]{2,1,0:T(8,128)(2,1)S(1)}, u32[]{:S(2)}, u32[]{:S(2)}) %collective-permute-start.35) | collective-permute-done | bytes 2359328 | tf_op jit(solution)/shard_map/ppermute | solution.py:531
  401.1 16.4 %collective-permute-done.39.refs_3_.refs_4_ = bf16[4,16,9216]{2,1,0:T(8,128)(2,1)S(1)} collective-permute-done((bf16[4,16,9216]{2,1,0:T(8,128)(2,1)}, bf16[4,16,9216]{2,1,0:T(8,128)(2,1)S(1)}, u32[]{:S(2)}, u32[]{:S(2)}) %collective-permute-start.39) | collective-permute-done | bytes 1179680 | tf_op jit(solution)/shard_map/ppermute | solution.py:543
  435.8 4.6 collective-permute-start.47
  444.7 5.5 %collective-permute-done.45.refs_3_.refs_4_ = bf16[2,16,7168]{2,1,0:T(8,128)(2,1)S(1)} collective-permute-done((bf16[2,16,7168]{2,1,0:T(8,128)(2,1)S(1)}, bf16[2,16,7168]{2,1,0:T(8,128)(2,1)S(1)}, u32[]{:S(2)}, u32[]{:S(2)}) %collective-permute-start.45) | collective-permute-done | bytes 458784 | tf_op jit(solution)/shard_map/ppermute | solution.py:543
  454.5 4.7 collective-permute-start.53
  463.4 8.9 %collective-permute-done.50 = bf16[1,16,7168]{2,1,0:T(8,128)(2,1)S(1)} collective-permute-done((bf16[1,16,7168]{2,1,0:T(8,128)(2,1)S(1)}, bf16[1,16,7168]{2,1,0:T(8,128)(2,1)S(1)}, u32[]{:S(2)}, u32[]{:S(2)}) %collective-permute-start.50) | collective-permute-done | bytes 229408 | tf_op jit(solution)/shard_map/ppermute | solution.py:543
  (518 shorter events, 181.9 us)
Async XLA Ops:
  1.7 41.9 %collective-permute-start.17 = (s32[2,7]{1,0:T(2,128)S(1)}, s32[2,7]{1,0:T(2,128)S(1)}, u32[]{:S(2)}, u32[]{:S(2)}) collective-permute-start(s32[2,7]{1,0:T(2,128)S(1)} %bitcast.198), channel_id=1, source_target_pairs={{0,1},{1,0},{2,3},{3,2},{4,5},{5,4},{6,7},{7,6},{8,9},{9,8},{10,11... | collective-permute-start | bytes 176 | tf_op jit(solution)/shard_map/ppermute | solution.py:183
  11.1 60.2 %collective-permute-start.16 = (bf16[254,448]{0,1:T(8,128)(2,1)}, bf16[254,448]{0,1:T(8,128)(2,1)}, u32[]{:S(2)}, u32[]{:S(2)}) collective-permute-start(bf16[254,448]{0,1:T(8,128)(2,1)} %get-tuple-element.377), channel_id=1, source_target_pairs={{0,1},{1,0},{2,3},{3,2},{4,5},{5,4},{6,7},{7,6},{8,9},{9,8},{10,11... | collective-permute-start | bytes 682760 | tf_op jit(solution)/shard_map/ppermute | solution.py:183
  26.3 17.2 %collective-permute-start.1 = (bf16[48,3328]{1,0:T(8,128)(2,1)S(1)}, bf16[48,3328]{1,0:T(8,128)(2,1)S(1)}, u32[]{:S(2)}, u32[]{:S(2)}) collective-permute-start(bf16[48,3328]{1,0:T(8,128)(2,1)S(1)} %constant_dynamic-update-slice_fusion), channel_id=1, source_target_pairs={{0,16},{1,17},{2,18},{3,19},{4,20},{5,21},{6,22},{7,23},{8,24},{9,... | collective-permute-start | bytes 958472 | tf_op jit(solution)/shard_map/ppermute | solution.py:413
  31.3 17.5 %collective-permute-start.4 = (bf16[4,48,2176]{2,1,0:T(8,128)(2,1)}, bf16[4,48,2176]{2,1,0:T(8,128)(2,1)}, u32[]{:S(2)}, u32[]{:S(2)}) collective-permute-start(bf16[4,48,2176]{2,1,0:T(8,128)(2,1)} %bitcast.10.refs_1_), channel_id=1, source_target_pairs={{0,2},{1,5},{2,0},{3,7},{4,6},{5,1},{6,4},{7,3},{8,10},{9,13},{10,... | collective-permute-start | bytes 2506760 | tf_op jit(solution)/shard_map/ppermute | solution.py:432
  43.6 19.2 %collective-permute-start.3 = (bf16[2,48,3328]{2,1,0:T(8,128)(2,1)S(1)}, bf16[2,48,3328]{2,1,0:T(8,128)(2,1)S(1)}, u32[]{:S(2)}, u32[]{:S(2)}) collective-permute-start(bf16[2,48,3328]{2,1,0:T(8,128)(2,1)S(1)} %pad_maximum_fusion.5), channel_id=1, source_target_pairs={{0,8},{1,9},{2,10},{3,11},{4,12},{5,13},{6,14},{7,15},{8,0},{9,1},... | collective-permute-start | bytes 1916936 | tf_op jit(solution)/shard_map/ppermute | solution.py:422
  45.1 30.8 %collective-permute-start.10 = (bf16[4,48,2176]{2,1,0:T(8,128)(2,1)}, bf16[4,48,2176]{2,1,0:T(8,128)(2,1)}, u32[]{:S(2)}, u32[]{:S(2)}) collective-permute-start(bf16[4,48,2176]{2,1,0:T(8,128)(2,1)} %bitcast.10.refs_1_), channel_id=1, source_target_pairs={{0,4},{1,3},{2,6},{3,1},{4,0},{5,7},{6,2},{7,5},{8,12},{9,11},{10,... | collective-permute-start | bytes 2506760 | tf_op jit(solution)/shard_map/ppermute | solution.py:432
  46.3 18.1 %collective-permute-start.8 = (bf16[32,3200]{1,0:T(8,128)(2,1)S(1)}, bf16[32,3200]{1,0:T(8,128)(2,1)S(1)}, u32[]{:S(2)}, u32[]{:S(2)}) collective-permute-start(bf16[32,3200]{1,0:T(8,128)(2,1)S(1)} %constant_dynamic-update-slice_fusion.1), channel_id=1, source_target_pairs={{0,16},{1,17},{2,18},{3,19},{4,20},{5,21},{6,22},{7,23},{8,24},{9,... | collective-permute-start | bytes 614408 | tf_op jit(solution)/shard_map/ppermute | solution.py:413
  48.8 27.2 %collective-permute-start.11 = (bf16[4,48,2176]{2,1,0:T(8,128)(2,1)}, bf16[4,48,2176]{2,1,0:T(8,128)(2,1)}, u32[]{:S(2)}, u32[]{:S(2)}) collective-permute-start(bf16[4,48,2176]{2,1,0:T(8,128)(2,1)} %collective-permute-done.4.refs_2_), channel_id=1, source_target_pairs={{0,4},{1,3},{2,6},{3,1},{4,0},{5,7},{6,2},{7,5},{8,12},{9,11},{10,... | collective-permute-start | bytes 2506760 | tf_op jit(solution)/shard_map/ppermute | solution.py:438
  63.1 18.4 %collective-permute-start.6 = (bf16[4,48,3328]{2,1,0:T(8,128)(2,1)S(1)}, bf16[4,48,3328]{2,1,0:T(8,128)(2,1)}, u32[]{:S(2)}, u32[]{:S(2)}) collective-permute-start(bf16[4,48,3328]{2,1,0:T(8,128)(2,1)S(1)} %bitcast.168), channel_id=1, source_target_pairs={{0,2},{1,5},{2,0},{3,7},{4,6},{5,1},{6,4},{7,3},{8,10},{9,13},{10,... | collective-permute-start | bytes 3833864 | tf_op jit(solution)/shard_map/ppermute | solution.py:432
  65.3 17.4 %collective-permute-start.9 = (bf16[2,32,3200]{2,1,0:T(8,128)(2,1)}, bf16[2,32,3200]{2,1,0:T(8,128)(2,1)}, u32[]{:S(2)}, u32[]{:S(2)}) collective-permute-start(bf16[2,32,3200]{2,1,0:T(8,128)(2,1)} %pad_maximum_fusion.7), channel_id=1, source_target_pairs={{0,8},{1,9},{2,10},{3,11},{4,12},{5,13},{6,14},{7,15},{8,0},{9,1},... | collective-permute-start | bytes 1228808 | tf_op jit(solution)/shard_map/ppermute | solution.py:422
  76.0 77.4 %collective-permute-start.18 = (bf16[4,48,3328]{2,1,0:T(8,128)(2,1)S(1)}, bf16[4,48,3328]{2,1,0:T(8,128)(2,1)}, u32[]{:S(2)}, u32[]{:S(2)}) collective-permute-start(bf16[4,48,3328]{2,1,0:T(8,128)(2,1)S(1)} %bitcast.169), channel_id=1, source_target_pairs={{0,1},{1,0},{2,3},{3,2},{4,5},{5,4},{6,7},{7,6},{8,9},{9,8},{10,11... | collective-permute-start | bytes 3833864 | tf_op jit(solution)/shard_map/ppermute | solution.py:183
  84.8 25.3 %collective-permute-start.5 = (bf16[4,48,3328]{2,1,0:T(8,128)(2,1)S(1)}, bf16[4,48,3328]{2,1,0:T(8,128)(2,1)}, u32[]{:S(2)}, u32[]{:S(2)}) collective-permute-start(bf16[4,48,3328]{2,1,0:T(8,128)(2,1)S(1)} %bitcast.170), channel_id=1, source_target_pairs={{0,4},{1,3},{2,6},{3,1},{4,0},{5,7},{6,2},{7,5},{8,12},{9,11},{10,... | collective-permute-start | bytes 3833864 | tf_op jit(solution)/shard_map/ppermute | solution.py:432
  86.1 54.2 %collective-permute-start.23 = (bf16[4,32,3200]{2,1,0:T(8,128)(2,1)}, bf16[4,32,3200]{2,1,0:T(8,128)(2,1)}, u32[]{:S(2)}, u32[]{:S(2)}) collective-permute-start(bf16[4,32,3200]{2,1,0:T(8,128)(2,1)} %bitcast.25.refs_1_), channel_id=1, source_target_pairs={{0,4},{1,3},{2,6},{3,1},{4,0},{5,7},{6,2},{7,5},{8,12},{9,11},{10,... | collective-permute-start | bytes 2457608 | tf_op jit(solution)/shard_map/ppermute | solution.py:432
  86.3 47.6 %collective-permute-start.22 = (bf16[4,32,3200]{2,1,0:T(8,128)(2,1)}, bf16[4,32,3200]{2,1,0:T(8,128)(2,1)}, u32[]{:S(2)}, u32[]{:S(2)}) collective-permute-start(bf16[4,32,3200]{2,1,0:T(8,128)(2,1)} %bitcast.25.refs_1_), channel_id=1, source_target_pairs={{0,2},{1,5},{2,0},{3,7},{4,6},{5,1},{6,4},{7,3},{8,10},{9,13},{10,... | collective-permute-start | bytes 2457608 | tf_op jit(solution)/shard_map/ppermute | solution.py:432
  87.6 45.0 %collective-permute-start.7 = (bf16[4,48,3328]{2,1,0:T(8,128)(2,1)}, bf16[4,48,3328]{2,1,0:T(8,128)(2,1)}, u32[]{:S(2)}, u32[]{:S(2)}) collective-permute-start(bf16[4,48,3328]{2,1,0:T(8,128)(2,1)} %collective-permute-done.6.refs_2_), channel_id=1, source_target_pairs={{0,4},{1,3},{2,6},{3,1},{4,0},{5,7},{6,2},{7,5},{8,12},{9,11},{10,... | collective-permute-start | bytes 3833864 | tf_op jit(solution)/shard_map/ppermute | solution.py:438
  110.1 43.3 %collective-permute-start.19 = (bf16[4,48,3328]{2,1,0:T(8,128)(2,1)}, bf16[4,48,3328]{2,1,0:T(8,128)(2,1)}, u32[]{:S(2)}, u32[]{:S(2)}) collective-permute-start(bf16[4,48,3328]{2,1,0:T(8,128)(2,1)} %collective-permute-done.6.refs_2_), channel_id=1, source_target_pairs={{0,1},{1,0},{2,3},{3,2},{4,5},{5,4},{6,7},{7,6},{8,9},{9,8},{10,11... | collective-permute-start | bytes 3833864 | tf_op jit(solution)/shard_map/ppermute | solution.py:183
  132.6 21.3 %collective-permute-start.20 = (bf16[4,48,3328]{2,1,0:T(8,128)(2,1)}, bf16[4,48,3328]{2,1,0:T(8,128)(2,1)}, u32[]{:S(2)}, u32[]{:S(2)}) collective-permute-start(bf16[4,48,3328]{2,1,0:T(8,128)(2,1)} %collective-permute-done.5.refs_3_), channel_id=1, source_target_pairs={{0,1},{1,0},{2,3},{3,2},{4,5},{5,4},{6,7},{7,6},{8,9},{9,8},{10,11... | collective-permute-start | bytes 3833864 | tf_op jit(solution)/shard_map/ppermute | solution.py:183
  134.0 20.0 %collective-permute-start.21 = (bf16[4,48,3328]{2,1,0:T(8,128)(2,1)}, bf16[4,48,3328]{2,1,0:T(8,128)(2,1)}, u32[]{:S(2)}, u32[]{:S(2)}) collective-permute-start(bf16[4,48,3328]{2,1,0:T(8,128)(2,1)} %collective-permute-done.7.refs_4_), channel_id=1, source_target_pairs={{0,1},{1,0},{2,3},{3,2},{4,5},{5,4},{6,7},{7,6},{8,9},{9,8},{10,11... | collective-permute-start | bytes 3833864 | tf_op jit(solution)/shard_map/ppermute | solution.py:183
  152.0 19.0 %collective-permute-start.25 = (bf16[4,32,3200]{2,1,0:T(8,128)(2,1)}, bf16[4,32,3200]{2,1,0:T(8,128)(2,1)S(1)}, u32[]{:S(2)}, u32[]{:S(2)}) collective-permute-start(bf16[4,32,3200]{2,1,0:T(8,128)(2,1)} %bitcast.25.refs_1_), channel_id=1, source_target_pairs={{0,1},{1,0},{2,3},{3,2},{4,5},{5,4},{6,7},{7,6},{8,9},{9,8},{10,11... | collective-permute-start | bytes 2457608 | tf_op jit(solution)/shard_map/ppermute | solution.py:183
  153.4 17.7 %collective-permute-start.26 = (bf16[4,32,3200]{2,1,0:T(8,128)(2,1)}, bf16[4,32,3200]{2,1,0:T(8,128)(2,1)S(1)}, u32[]{:S(2)}, u32[]{:S(2)}) collective-permute-start(bf16[4,32,3200]{2,1,0:T(8,128)(2,1)} %collective-permute-done.22.refs_2_), channel_id=1, source_target_pairs={{0,1},{1,0},{2,3},{3,2},{4,5},{5,4},{6,7},{7,6},{8,9},{9,8},{10,11... | collective-permute-start | bytes 2457608 | tf_op jit(solution)/shard_map/ppermute | solution.py:183
  153.5 17.6 %collective-permute-start.27 = (bf16[4,32,3200]{2,1,0:T(8,128)(2,1)}, bf16[4,32,3200]{2,1,0:T(8,128)(2,1)S(1)}, u32[]{:S(2)}, u32[]{:S(2)}) collective-permute-start(bf16[4,32,3200]{2,1,0:T(8,128)(2,1)} %collective-permute-done.23.refs_3_), channel_id=1, source_target_pairs={{0,1},{1,0},{2,3},{3,2},{4,5},{5,4},{6,7},{7,6},{8,9},{9,8},{10,11... | collective-permute-start | bytes 2457608 | tf_op jit(solution)/shard_map/ppermute | solution.py:183
  153.9 17.2 %collective-permute-start.28 = (bf16[4,32,3200]{2,1,0:T(8,128)(2,1)S(1)}, bf16[4,32,3200]{2,1,0:T(8,128)(2,1)S(1)}, u32[]{:S(2)}, u32[]{:S(2)}) collective-permute-start(bf16[4,32,3200]{2,1,0:T(8,128)(2,1)S(1)} %collective-permute-done.24.refs_4_), channel_id=1, source_target_pairs={{0,1},{1,0},{2,3},{3,2},{4,5},{5,4},{6,7},{7,6},{8,9},{9,8},{10,11... | collective-permute-start | bytes 2457608 | tf_op jit(solution)/shard_map/ppermute | solution.py:183
  244.4 47.6 %collective-permute-start.29 = (bf16[16,16,4608]{2,1,0:T(8,128)(2,1)}, bf16[16,16,4608]{2,1,0:T(8,128)(2,1)}, u32[]{:S(2)}, u32[]{:S(2)}) collective-permute-start(bf16[16,16,4608]{2,1,0:T(8,128)(2,1)} %shard_map.447), channel_id=1, source_target_pairs={{0,1},{1,0},{2,3},{3,2},{4,5},{5,4},{6,7},{7,6},{8,9},{9,8},{10,11... | collective-permute-start | bytes 7077896 | tf_op jit(solution)/shard_map/ppermute | solution.py:183
  327.5 22.5 %collective-permute-start.32 = (bf16[16,16,9216]{2,1,0:T(8,128)(2,1)}, bf16[16,16,9216]{2,1,0:T(8,128)(2,1)}, u32[]{:S(2)}, u32[]{:S(2)}) collective-permute-start(bf16[16,16,9216]{2,1,0:T(8,128)(2,1)} %shard_map.451), channel_id=1, source_target_pairs={{0,1},{1,0},{2,3},{3,2},{4,5},{5,4},{6,7},{7,6},{8,9},{9,8},{10,11... | collective-permute-start | bytes 14155784 | tf_op jit(solution)/shard_map/ppermute | solution.py:183
  346.4 25.1 %collective-permute-start.36 = (bf16[16,16,7168]{2,1,0:T(8,128)(2,1)}, bf16[16,16,7168]{2,1,0:T(8,128)(2,1)}, u32[]{:S(2)}, u32[]{:S(2)}) collective-permute-start(bf16[16,16,7168]{2,1,0:T(8,128)(2,1)} %shard_map.455), channel_id=1, source_target_pairs={{0,1},{1,0},{2,3},{3,2},{4,5},{5,4},{6,7},{7,6},{8,9},{9,8},{10,11... | collective-permute-start | bytes 11010056 | tf_op jit(solution)/shard_map/ppermute | solution.py:183
  357.6 28.3 %collective-permute-start.35 = (bf16[8,16,9216]{2,1,0:T(8,128)(2,1)}, bf16[8,16,9216]{2,1,0:T(8,128)(2,1)S(1)}, u32[]{:S(2)}, u32[]{:S(2)}) collective-permute-start(bf16[8,16,9216]{2,1,0:T(8,128)(2,1)} %get-tuple-element.170), channel_id=1, source_target_pairs={{0,4},{1,3},{2,6},{3,1},{4,0},{5,7},{6,2},{7,5},{8,12},{9,11},{10,... | collective-permute-start | bytes 7077896 | tf_op jit(solution)/shard_map/ppermute | solution.py:531
  379.3 38.8 %collective-permute-start.38 = (bf16[8,16,7168]{2,1,0:T(8,128)(2,1)}, bf16[8,16,7168]{2,1,0:T(8,128)(2,1)}, u32[]{:S(2)}, u32[]{:S(2)}) collective-permute-start(bf16[8,16,7168]{2,1,0:T(8,128)(2,1)} %get-tuple-element.178.refs_5_), channel_id=1, source_target_pairs={{0,4},{1,3},{2,6},{3,1},{4,0},{5,7},{6,2},{7,5},{8,12},{9,11},{10,... | collective-permute-start | bytes 5505032 | tf_op jit(solution)/shard_map/ppermute | solution.py:531
  389.1 28.4 %collective-permute-start.39 = (bf16[4,16,9216]{2,1,0:T(8,128)(2,1)}, bf16[4,16,9216]{2,1,0:T(8,128)(2,1)S(1)}, u32[]{:S(2)}, u32[]{:S(2)}) collective-permute-start(bf16[4,16,9216]{2,1,0:T(8,128)(2,1)} %get-tuple-element.180.refs_6_), channel_id=1, source_target_pairs={{0,2},{1,5},{2,0},{3,7},{4,6},{5,1},{6,4},{7,3},{8,10},{9,13},{10,... | collective-permute-start | bytes 3538952 | tf_op jit(solution)/shard_map/ppermute | solution.py:543
  397.1 33.6 %collective-permute-start.37 = (bf16[8,16,1920]{2,1,0:T(8,128)(2,1)}, bf16[8,16,1920]{2,1,0:T(8,128)(2,1)S(1)}, u32[]{:S(2)}, u32[]{:S(2)}) collective-permute-start(bf16[8,16,1920]{2,1,0:T(8,128)(2,1)} %get-tuple-element.183.refs_5_), channel_id=1, source_target_pairs={{0,4},{1,3},{2,6},{3,1},{4,0},{5,7},{6,2},{7,5},{8,12},{9,11},{10,... | collective-permute-start | bytes 1474568 | tf_op jit(solution)/shard_map/ppermute | solution.py:531
  427.6 45.7 %collective-permute-start.33 = (bf16[254,448]{1,0:T(8,128)(2,1)S(1)}, bf16[254,448]{1,0:T(8,128)(2,1)S(1)}, u32[]{:S(2)}, u32[]{:S(2)}) collective-permute-start(bf16[254,448]{1,0:T(8,128)(2,1)S(1)} %get-tuple-element.375), channel_id=1, source_target_pairs={{0,1},{1,0},{2,3},{3,2},{4,5},{5,4},{6,7},{7,6},{8,9},{9,8},{10,11... | collective-permute-start | bytes 682760 | tf_op jit(solution)/shard_map/ppermute | solution.py:183
  432.2 22.3 %collective-permute-start.52 = (bf16[1,16,9216]{2,1,0:T(8,128)(2,1)S(1)}, bf16[1,16,9216]{2,1,0:T(8,128)(2,1)S(1)}, u32[]{:S(2)}, u32[]{:S(2)}) collective-permute-start(bf16[1,16,9216]{2,1,0:T(8,128)(2,1)S(1)} %get-tuple-element.198), channel_id=1, source_target_pairs={{0,16},{1,17},{2,18},{3,19},{4,20},{5,21},{6,22},{7,23},{8,24},{9,... | collective-permute-start | bytes 884744 | tf_op jit(solution)/shard_map/ppermute | solution.py:543
  454.5 20.1 %collective-permute-start.53 = (bf16[16,9216]{1,0:T(8,128)(2,1)S(1)}, bf16[16,9216]{1,0:T(8,128)(2,1)S(1)}, u32[]{:S(2)}, u32[]{:S(2)}) collective-permute-start(bf16[16,9216]{1,0:T(8,128)(2,1)S(1)} %fusion.47.refs_1_), channel_id=1, source_target_pairs={{0,1},{1,0},{2,3},{3,2},{4,5},{5,4},{6,7},{7,6},{8,9},{9,8},{10,11... | collective-permute-start | bytes 884744 | tf_op jit(solution)/shard_map/ppermute | solution.py:183
  (152 other events, 1370.9 us)
